TPU v7x, 32 devices: a whole 2x2x4 slice. The times are simulated.
32 devices in a mesh: prow: 4 (over y, x), pcol: 8 (over z, core).
Axes of the slice: x: 2, y: 2, z: 4, core: 2. Of those that a mesh axis runs over, the one named last changes fastest.
Arguments:
- inverse_top: bfloat16 [64, 64, 128, 128], P('prow', 'pcol'), may hold values from -6 to 6
- rows_one: int32 [8, 32], replicated, may hold values from 0 to 63, as said below
- panel_one: bfloat16 [8, 32, 128, 128], P('pcol', 'prow'), may hold values from -0.09375 to 0.09375
- base_one: float32 [8, 128, 128], P('pcol'), may hold values from -6 to 6
- parent_two: int32 [8], replicated, may hold values from 0 to 7
- order_two: int32 [8, 32], replicated, may hold values from 0 to 31, as said below
- panel_two: bfloat16 [8, 32, 128, 128], P('pcol', 'prow'), may hold values from -0.09375 to 0.09375
- link_two: bfloat16 [8, 128, 128], P('pcol'), may hold values from -0.5 to 0.5
- base_two: float32 [8, 128, 128], P('pcol'), may hold values from -6 to 6
Outputs:
- column_one: bfloat16 [8, 32, 128, 128], P('pcol', 'prow')
- diagonal_one: bfloat16 [8, 128, 128], P('pcol')
- column_two: bfloat16 [8, 32, 128, 128], P('pcol', 'prow')
- upper_two: bfloat16 [8, 128, 128], P('pcol')
- diagonal_two: bfloat16 [8, 128, 128], P('pcol')
Inputs may be any that keep to these rules, and one draw needn't show every extreme that they name: For every supernode k and process row p, rows_one[k, p * 8] to rows_one[k, p * 8 + 7] are 8 distinct ancestors between p * 16 and p * 16 + 15. In every draw some process column c holds 8 ancestors (ancestor // 8 == c) of every level-one supernode. Each block order_two[k, p * 8] to order_two[k, p * 8 + 7] is a permutation of p * 8 to p * 8 + 7.
All inputs are finite; a program needn't handle non-finite values.
Results may differ from a plain program's by a relative error of at most 0.024.
Values may be sent and summed in bfloat16 or wider, within the bound.
No kernel may reach another device: no remote copies, remote signals or barrier semaphores. Data moves between devices by JAX's collectives and lax.ppermute only.
A program may use at most 192 MiB of HBM per device.

v0:
```python
import jax
import jax.numpy as jnp
from jax import lax
from jax.sharding import PartitionSpec as P


def slot_positions(rows_all, dests, width, capacity):
    owner = rows_all // width
    length = rows_all.shape[1]
    positions = jnp.arange(length, dtype=jnp.int32)
    same_owner = owner[:, :, None] == owner[:, None, :]
    earlier = positions[None, None, :] < positions[None, :, None]
    ranking = jnp.sum(jnp.logical_and(same_owner, earlier), axis=2)
    slot_ids = jnp.arange(capacity, dtype=jnp.int32)
    matches = jnp.logical_and(
        owner[None, :, None, :] == dests[:, None, None, None],
        ranking[None, :, None, :] == slot_ids[None, None, :, None],
    )
    where_at = jnp.sum(jnp.where(matches, positions, 0), axis=3)
    present = jnp.any(matches, axis=3)
    return (where_at, present)


def pack_panels(full_panel, my_rows, width, capacity, columns):
    where_at, present = slot_positions(
        my_rows, jnp.arange(columns, dtype=jnp.int32), width, capacity
    )
    children = jnp.arange(my_rows.shape[0], dtype=jnp.int32)[None, :, None]
    selected = full_panel[children, where_at]
    return jnp.where(present[:, :, :, None, None], selected, jnp.zeros((), selected.dtype))


def local_indices(rows_all, prow_at, pcol_at, per_row, height, width):
    where_at, present = slot_positions(rows_all, jnp.reshape(pcol_at, (1,)), width, per_row)
    targets = jnp.take_along_axis(rows_all, where_at[0], axis=1)
    col_local = jnp.where(present[0], targets - pcol_at * width, 0)
    row_local = lax.dynamic_slice_in_dim(rows_all, prow_at * per_row, per_row, 1) - prow_at * height
    return (row_local, col_local)


def tile_products(inverse_local, received, row_local, col_local):
    blocks = inverse_local[row_local[:, :, None], col_local[:, None, :]]
    return jnp.einsum("kabij,kbjl->kail", blocks, received, preferred_element_type=jnp.float32)


def flatten_received(received):
    return received.reshape((received.shape[0] * received.shape[1],) + received.shape[2:])


def local(
    inverse_top, rows_one, panel_one, base_one, parent_two, order_two, panel_two, link_two, base_two
):
    per_col = panel_one.shape[0]
    per_row = panel_one.shape[1]
    height = inverse_top.shape[0]
    width = inverse_top.shape[1]
    columns = lax.axis_size("pcol")
    prow_at = lax.axis_index("prow")
    pcol_at = lax.axis_index("pcol")
    rows_two = jnp.take_along_axis(rows_one[parent_two], order_two, axis=1)
    mine_one = lax.dynamic_slice_in_dim(rows_one, pcol_at * per_col, per_col, 0)
    mine_two = lax.dynamic_slice_in_dim(rows_two, pcol_at * per_col, per_col, 0)
    row_one, col_one = local_indices(rows_one, prow_at, pcol_at, per_row, height, width)
    row_two, col_two = local_indices(rows_two, prow_at, pcol_at, per_row, height, width)
    full_one = lax.all_gather(panel_one, "prow", axis=1, tiled=True)
    outgoing_one = pack_panels(full_one, mine_one, width, per_row, columns)
    received_one = lax.all_to_all(outgoing_one, "pcol", split_axis=0, concat_axis=0, tiled=True)
    flat_one = flatten_received(received_one)
    summed_one = lax.psum_scatter(
        tile_products(inverse_top, flat_one, row_one, col_one).astype(jnp.bfloat16),
        "pcol",
        scatter_dimension=0,
        tiled=True,
    ).astype(jnp.float32)
    full_two = lax.all_gather(panel_two, "prow", axis=1, tiled=True)
    outgoing_two = pack_panels(full_two, mine_two, width, per_row, columns)
    received_two = lax.all_to_all(outgoing_two, "pcol", split_axis=0, concat_axis=0, tiled=True)
    flat_two = flatten_received(received_two)
    summed_two = lax.psum_scatter(
        tile_products(inverse_top, flat_two, row_two, col_two).astype(jnp.bfloat16),
        "pcol",
        scatter_dimension=0,
        tiled=True,
    ).astype(jnp.float32)
    column_one = (-summed_one).astype(jnp.bfloat16)
    diag_part = jnp.einsum(
        "cmij,cmil->cjl", panel_one, column_one, preferred_element_type=jnp.float32
    )
    diagonal_one = (
        base_one - lax.psum(diag_part.astype(jnp.bfloat16), "prow").astype(jnp.float32)
    ).astype(jnp.bfloat16)
    all_cols, all_diag = (
        lax.all_gather(column_one, "pcol", axis=0, tiled=True),
        lax.all_gather(diagonal_one, "pcol", axis=0, tiled=True),
    )
    my_parent = lax.dynamic_slice_in_dim(parent_two, pcol_at * per_col, per_col, 0)
    my_order = (
        lax.dynamic_slice(order_two, (pcol_at * per_col, prow_at * per_row), (per_col, per_row))
        - prow_at * per_row
    )
    near_cols = all_cols[my_parent[:, None], my_order]
    near_diag = all_diag[my_parent]
    carried = jnp.einsum("cmij,cjl->cmil", near_cols, link_two, preferred_element_type=jnp.float32)
    column_two = (-(summed_two + carried)).astype(jnp.bfloat16)
    upper_part = jnp.einsum(
        "cmij,cmil->cjl", near_cols, panel_two, preferred_element_type=jnp.float32
    )
    parent_term = jnp.einsum(
        "cij,cjl->cil", near_diag, link_two, preferred_element_type=jnp.float32
    )
    upper_total = lax.psum(upper_part.astype(jnp.bfloat16), "prow").astype(jnp.float32)
    upper_two = (-(parent_term + upper_total)).astype(jnp.bfloat16)
    lower_part = jnp.einsum(
        "cmij,cmil->cjl", panel_two, column_two, preferred_element_type=jnp.float32
    )
    lower_total = lax.psum(lower_part.astype(jnp.bfloat16), "prow").astype(jnp.float32)
    link_term = jnp.einsum("cij,cil->cjl", link_two, upper_two, preferred_element_type=jnp.float32)
    diagonal_two = (base_two - link_term - lower_total).astype(jnp.bfloat16)
    return (column_one, diagonal_one, column_two, upper_two, diagonal_two)


def solution(mesh):
    return jax.shard_map(
        local,
        mesh=mesh,
        in_specs=(
            P("prow", "pcol", None, None),
            P(),
            P("pcol", "prow", None, None),
            P("pcol", None, None),
            P(),
            P(),
            P("pcol", "prow", None, None),
            P("pcol", None, None),
            P("pcol", None, None),
        ),
        out_specs=(
            P("pcol", "prow", None, None),
            P("pcol", None, None),
            P("pcol", "prow", None, None),
            P("pcol", None, None),
            P("pcol", None, None),
        ),
        check_vma=False,
    )
```

profile of v0, /device:TPU:0, one launch (start us, length us, event | category | flops | bytes accessed | tf_op | source)
XLA Modules:
  0.0 309.9 jit_solution(20878697101123459)
XLA Ops:
  7.9 0.7 fusion.58
  9.4 29.8 %all-gather.4.cloned.1.call-done = bf16[1,32,128,128]{3,2,0,1:T(8,128)(2,1)} async-done(((bf16[1,8,128,128]{3,2,0,1:T(8,128)(2,1)}), bf16[1,32,128,128]{3,2,0,1:T(8,128)(2,1)}) %all-gather.4.cloned.1.call-update) | async-done | bytes 1048592 | tf_op jit(solution)/shard_map/all_gather | solution.py:65
  39.2 2.2 gather_fusion.1
  41.4 1.6 broadcast_select_fusion.1
  43.0 4.7 %all-to-all-start = ((bf16[8,1,8,128,128]{4,3,2,1,0:T(8,128)(2,1)}), bf16[8,1,8,128,128]{4,3,2,1,0:T(8,128)(2,1)S(1)}, u32[]{:S(2)}, u32[]{:S(2)}) async-start(bf16[8,1,8,128,128]{4,3,2,1,0:T(8,128)(2,1)} %broadcast_select_fusion.1), calls=%async_computation | async-start | bytes 4194304 | tf_op jit(solution)/shard_map/all_to_all | solution.py:67
  49.2 1.4 gather_fusion.6
  51.5 0.7 gather_fusion.7
  52.8 13.0 %gather_fusion = bf16[512,128,128]{2,1,0:T(8,128)(2,1)} fusion(bf16[16,8,128,128]{3,2,1,0:T(8,128)(2,1)} %param.11, s32[512]{0:T(512)S(1)} %reshape.631), kind=kCustom, calls=%fused_computation.2 | custom fusion | bytes 33558528 | tf_op jit(solution)/shard_map/gather | solution.py:42
  65.8 30.9 %all-to-all-done = bf16[8,1,8,128,128]{4,3,2,1,0:T(8,128)(2,1)S(1)} async-done(((bf16[8,1,8,128,128]{4,3,2,1,0:T(8,128)(2,1)}), bf16[8,1,8,128,128]{4,3,2,1,0:T(8,128)(2,1)S(1)}, u32[]{:S(2)}, u32[]{:S(2)}) %all-to-all-start) | async-done | bytes 2097184 | tf_op jit(solution)/shard_map/all_to_all | solution.py:67
  96.8 9.7 %bitcast_convert_fusion.1 = bf16[8,8,128,128]{3,2,1,0:T(8,128)(2,1)} fusion(bf16[8,8,8,128,128]{4,3,2,1,0:T(8,128)(2,1)} %bitcast.157, bf16[8,1,8,128,128]{4,3,2,1,0:T(8,128)(2,1)S(1)} %all-to-all-done), kind=kOutput, calls=%fused_computation.10 | convolution fusion | flops 2148532224 | bytes 20971520 | tf_op jit(solution)/shard_map/kabij,kbjl->kail/dot_general | solution.py:43
  107.3 2.2 gather_fusion.4
  109.5 1.5 broadcast_select_fusion
  111.0 3.6 %all-to-all-start.1 = ((bf16[8,1,8,128,128]{4,3,2,1,0:T(8,128)(2,1)}), bf16[8,1,8,128,128]{4,3,2,1,0:T(8,128)(2,1)S(1)}, u32[]{:S(2)}, u32[]{:S(2)}) async-start(bf16[8,1,8,128,128]{4,3,2,1,0:T(8,128)(2,1)} %broadcast_select_fusion), calls=%async_computation.2 | async-start | bytes 4194304 | tf_op jit(solution)/shard_map/all_to_all | solution.py:77
  114.6 45.4 %reduce-scatter.3.cloned.1.call-done = bf16[1,8,128,128]{3,2,1,0:T(8,128)(2,1)} async-done(((bf16[8,8,128,128]{3,2,1,0:T(8,128)(2,1)}), bf16[1,8,128,128]{3,2,1,0:T(8,128)(2,1)}) %reduce-scatter.3.cloned.1.call-update) | async-done | bytes 262160 | tf_op jit(solution)/shard_map/reduce_scatter | solution.py:69
  160.0 1.7 negate_convert_fusion
  162.1 0.7 gather_fusion.8
  163.4 13.0 %gather_fusion.3 = bf16[512,128,128]{2,1,0:T(8,128)(2,1)} fusion(bf16[16,8,128,128]{3,2,1,0:T(8,128)(2,1)} %param.11, s32[512]{0:T(512)S(1)} %reshape.653), kind=kCustom, calls=%fused_computation.5 | custom fusion | bytes 33558528 | tf_op jit(solution)/shard_map/gather | solution.py:42
  176.4 2.1 all-to-all-done.1
  178.6 10.0 %bitcast_convert_fusion = bf16[8,8,128,128]{3,2,1,0:T(8,128)(2,1)} fusion(bf16[8,8,8,128,128]{4,3,2,1,0:T(8,128)(2,1)} %bitcast.158, bf16[8,1,8,128,128]{4,3,2,1,0:T(8,128)(2,1)S(1)} %all-to-all-done.1), kind=kOutput, calls=%fused_computation.9 | convolution fusion | flops 2148532224 | bytes 20971520 | tf_op jit(solution)/shard_map/kabij,kbjl->kail/dot_general | solution.py:43
  191.3 0.9 fusion.16
  192.2 10.8 %all-gather.8.cloned.1.call-done = bf16[8,8,128,128]{3,2,1,0:T(8,128)(2,1)} async-done(((bf16[1,8,128,128]{3,2,1,0:T(8,128)(2,1)}), bf16[8,8,128,128]{3,2,1,0:T(8,128)(2,1)}) %all-gather.8.cloned.1.call-update) | async-done | bytes 2097168 | tf_op jit(solution)/shard_map/all_gather | solution.py:93
  203.0 2.2 gather_fusion.5
  205.2 0.9 fusion.15
  206.1 34.4 %reduce-scatter.5.cloned.1.call-done = bf16[1,8,128,128]{3,2,1,0:T(8,128)(2,1)} async-done(((bf16[8,8,128,128]{3,2,1,0:T(8,128)(2,1)}), bf16[1,8,128,128]{3,2,1,0:T(8,128)(2,1)}) %reduce-scatter.5.cloned.1.call-update) | async-done | bytes 262160 | tf_op jit(solution)/shard_map/reduce_scatter | solution.py:79
  240.5 1.2 fusion.4
  241.7 0.9 fusion.14
  244.7 40.6 %all-reduce.6.cloned.1.call-done = (bf16[1,128,128]{1,2,0:T(8,128)(2,1)}, bf16[1,128,128]{2,1,0:T(8,128)(2,1)}, bf16[1,128,128]{1,2,0:T(8,128)(2,1)}) async-done(((bf16[1,128,128]{1,2,0:T(8,128)(2,1)}, bf16[1,128,128]{2,1,0:T(8,128)(2,1)}, bf16[1,128,128]{1,2,0:T(8,128)(2,1)}), (bf16[1,128,128]{1,2,0:T(8,128)(2,1)}, bf16[1,128,128]{2,1,0:T(8,128)(2,1)}, ...) | async-done | bytes 98320 | tf_op jit(solution)/shard_map/psum | solution.py:90
  285.2 0.8 subtract_convert_fusion
  286.1 14.3 %all_gather.15 = bf16[8,128,128]{2,1,0:T(8,128)(2,1)S(1)} all-gather(bf16[1,128,128]{2,1,0:T(8,128)(2,1)S(1)} %copy.48), channel_id=1, replica_groups=mesh['prow'=4,'pcol'=8] {'pcol'}, dimensions={0}, use_global_device_ids=true | all-gather | bytes 294912 | tf_op jit(solution)/shard_map/all_gather | solution.py:94
  300.4 0.9 fusion.10
  301.3 1.0 fusion.9
  302.3 0.7 copy.49
  (89 shorter events, 7.2 us)
Async XLA Ops:
  7.2 233.3 %copy-start = (bf16[1,128,128]{2,1,0:T(8,128)(2,1)S(1)}, bf16[1,128,128]{2,1,0:T(8,128)(2,1)}, u32[]{:S(2)}) copy-start(bf16[1,128,128]{2,1,0:T(8,128)(2,1)} %param.18) | copy-start | bytes 98308
  7.2 32.0 %all-gather.4.cloned.1.call-start = ((), (), s32[]{:S(2)}) async-start(), calls=%async_computation.4 | async-start | bytes 1310720 | tf_op jit(solution)/shard_map/all_gather | solution.py:65
  43.0 5.5 %copy-start.11 = (s32[8]{0:T(128)S(1)}, s32[8]{0:T(128)}, u32[]{:S(2)}) copy-start(s32[8]{0:T(128)} %param.15) | copy-start | bytes 100
  43.0 5.6 %copy-start.1 = (s32[8,32]{1,0:T(8,128)S(1)}, s32[8,32]{1,0:T(8,128)}, u32[]{:S(2)}) copy-start(s32[8,32]{1,0:T(8,128)} %param.12) | copy-start | bytes 3076
  43.0 6.1 %copy-start.10 = (s32[8,32]{1,0:T(8,128)S(1)}, s32[8,32]{1,0:T(8,128)}, u32[]{:S(2)}) copy-start(s32[8,32]{1,0:T(8,128)} %param.16) | copy-start | bytes 3076
  43.0 53.8 %all-to-all-start = ((bf16[8,1,8,128,128]{4,3,2,1,0:T(8,128)(2,1)}), bf16[8,1,8,128,128]{4,3,2,1,0:T(8,128)(2,1)S(1)}, u32[]{:S(2)}, u32[]{:S(2)}) async-start(bf16[8,1,8,128,128]{4,3,2,1,0:T(8,128)(2,1)} %broadcast_select_fusion.1), calls=%async_computation | async-start | bytes 4194304 | tf_op jit(solution)/shard_map/all_to_all | solution.py:67
  47.7 59.6 %all-gather.6.cloned.1.call-start = ((), (), s32[]{:S(2)}) async-start(), calls=%async_computation.6 | async-start | bytes 1310720 | tf_op jit(solution)/shard_map/all_gather | solution.py:75
  48.5 111.6 %reduce-scatter.3.cloned.1.call-start = ((), (), s32[]{:S(2)}) async-start(), calls=%async_computation.5 | async-start | bytes 2359296 | tf_op jit(solution)/shard_map/reduce_scatter | solution.py:69
  111.0 67.6 %all-to-all-start.1 = ((bf16[8,1,8,128,128]{4,3,2,1,0:T(8,128)(2,1)}), bf16[8,1,8,128,128]{4,3,2,1,0:T(8,128)(2,1)S(1)}, u32[]{:S(2)}, u32[]{:S(2)}) async-start(bf16[8,1,8,128,128]{4,3,2,1,0:T(8,128)(2,1)} %broadcast_select_fusion), calls=%async_computation.2 | async-start | bytes 4194304 | tf_op jit(solution)/shard_map/all_to_all | solution.py:77
  114.6 88.4 %all-gather.8.cloned.1.call-start = ((), (), s32[]{:S(2)}) async-start(), calls=%async_computation.8 | async-start | bytes 2359296 | tf_op jit(solution)/shard_map/all_gather | solution.py:93
  161.7 78.7 %reduce-scatter.5.cloned.1.call-start = ((), (), s32[]{:S(2)}) async-start(), calls=%async_computation.7 | async-start | bytes 2359296 | tf_op jit(solution)/shard_map/reduce_scatter | solution.py:79
  188.6 2.7 copy-start.3
  188.6 2.7 copy-start.5
  188.6 16.7 %copy-start.2 = (bf16[1,8,128,128]{3,2,1,0:T(8,128)(2,1)S(1)}, bf16[1,8,128,128]{3,2,1,0:T(8,128)(2,1)}, u32[]{:S(2)}) copy-start(bf16[1,8,128,128]{3,2,1,0:T(8,128)(2,1)} %param.17) | copy-start | bytes 786436
  188.6 54.0 %copy-start.8 = (f32[1,128,128]{2,1,0:T(8,128)S(1)}, f32[1,128,128]{2,1,0:T(8,128)}, u32[]{:S(2)}) copy-start(f32[1,128,128]{2,1,0:T(8,128)} %param.14) | copy-start | bytes 196612
  188.6 55.3 %copy-start.9 = (f32[1,128,128]{2,1,0:T(8,128)S(1)}, f32[1,128,128]{2,1,0:T(8,128)}, u32[]{:S(2)}) copy-start(f32[1,128,128]{2,1,0:T(8,128)} %param.19) | copy-start | bytes 196612
  188.6 96.6 %all-reduce.6.cloned.1.call-start = ((), (), s32[]{:S(2)}) async-start(), calls=%async_computation.9 | async-start | bytes 196608 | tf_op jit(solution)/shard_map/psum | solution.py:90
  241.7 61.4 %copy-start.4 = (bf16[1,8,128,128]{3,2,1,0:T(8,128)(2,1)}, bf16[1,8,128,128]{3,2,1,0:T(8,128)(2,1)S(1)}, u32[]{:S(2)}) copy-start(bf16[1,8,128,128]{3,2,1,0:T(8,128)(2,1)S(1)} %fusion.4) | copy-start | bytes 786436
  286.1 16.9 %copy-start.6 = (bf16[1,128,128]{2,1,0:T(8,128)(2,1)}, bf16[1,128,128]{2,1,0:T(8,128)(2,1)S(1)}, u32[]{:S(2)}) copy-start(bf16[1,128,128]{2,1,0:T(8,128)(2,1)S(1)} %copy.48) | copy-start | bytes 98308
  301.3 1.7 copy-start.7
Sparse Core Ops, SparseCore 0:
  9.9 29.3 all-gather.3
  50.4 27.0 all-gather.5
  106.6 53.3 reduce-scatter.2
  162.0 40.9 all-gather.7
  205.2 35.2 reduce-scatter.4
  244.1 41.1 all-reduce.5
where the time goes:
time: 311 us; the launch traced here: 310 us
  waiting for transfers between devices  195 us (63%)
  local copies, waits for them, and re-layouts  38.6 us (12%)
  matrix products  25.3 us (8%)
  between operations  18.2 us (6%)
  blocking collectives  14.3 us (5%)
  other arithmetic  9.38 us (3%)
  starting transfers between devices  8.58 us (3%)
    reduce_scatter x1, waiting for transfers between devices, local(): lax.psum_scatter(tile_products(inverse_top, flat_one, row_one, col_one).a...  45.4 us
    psum x1, waiting for transfers between devices, local(): lax.psum(diag_part.astype(jnp.bfloat16), 'prow').astype(jnp.float32)  40.6 us
    reduce_scatter x1, waiting for transfers between devices, local(): lax.psum_scatter(tile_products(inverse_top, flat_two, row_two, col_two).a...  34.4 us
    all_to_all x1, waiting for transfers between devices, local(): lax.all_to_all(outgoing_one, 'pcol', split_axis=0, concat_axis=0, tiled=T...  30.9 us
    all_gather x1, waiting for transfers between devices, local(): full_one = lax.all_gather(panel_one, 'prow', axis=1, tiled=True)  29.8 us
    gather x2, local copies, waits for them, and re-layouts, tile_products(): blocks = inverse_local[row_local[:, :, None], col_local[:, None, :]]  26 us
    dot_general x2, matrix products, tile_products(): jnp.einsum('kabij,kbjl->kail', blocks, received, preferred_element_type=j...  19.7 us
    all_gather x1, blocking collectives, local(): lax.all_gather(diagonal_one, 'pcol', axis=0, tiled=True)  14.3 us
  transfers between devices with their start and end apart: 8, of which 7 were waited for; matrix products, arithmetic and copies ran while one was open for 21% of the time, Pallas kernels for 0%

commit v1 on v0

v1 whole, which is shorter than its diff:
```python
import functools

import jax
import jax.numpy as jnp
from jax import lax
from jax.experimental import pallas as pl
from jax.experimental.pallas import tpu as pltpu
from jax.sharding import Mesh, PartitionSpec as P

ROW, CHIP, CORE = "prow", "pchip", "pcore"
F32 = jnp.float32
BF16 = jnp.bfloat16


def exchange(x, axis, step):
    size = lax.axis_size(axis)
    return lax.ppermute(x, axis, [(i, i ^ step) for i in range(size)])


def spread(x, axis):
    return [x] + [exchange(x, axis, s) for s in range(1, lax.axis_size(axis))]


def load_inverse(own, sibling, inverse, sems):
    copies = [
        pltpu.make_async_copy(own, inverse.at[0], sems.at[0]),
        pltpu.make_async_copy(sibling, inverse.at[1], sems.at[1]),
    ]
    for copy in copies:
        copy.start()
    return copies


def load_panels(pieces, panels, sems, at):
    group = pieces[0].shape[1]
    copies = []
    for s, piece in enumerate(pieces):
        place = pl.ds(pl.multiple_of((at ^ s) * group, group), group)
        copies.append(pltpu.make_async_copy(piece, panels.at[:, place], sems.at[2 + s]))
        copies[-1].start()
    return copies


def block_row(inverse, row, cols, core, width):
    tiles = [inverse[(col // width) ^ core, row, col % width] for col in cols]
    return jnp.concatenate(tiles, axis=1)


def level_one_kernel(
    nodes, group_rows, rows_one, own, sibling, *refs
):
    height, width = own.shape[0], own.shape[1]
    here, chip, core = lax.axis_index(ROW), lax.axis_index(CHIP), lax.axis_index(CORE)
    pieces, refs = refs[:group_rows], refs[group_rows:]
    whole, sends, (inverse, panels, sems) = refs[0], refs[1:nodes], refs[nodes:]
    per_row, tile = panels.shape[1], panels.shape[2]
    copies = load_inverse(own, sibling, inverse, sems) + load_panels(pieces, panels, sems, here)
    for copy in copies:
        copy.wait()
    for t in range(nodes):
        at = chip ^ t
        node = 2 * at + core
        cols = [rows_one[node, chip * per_row + n] - chip * 2 * width for n in range(per_row)]
        stacked = panels[at].reshape(per_row * tile, tile)
        for m in range(per_row):
            row = rows_one[node, here * per_row + m] - here * height
            part = jnp.dot(
                block_row(inverse, row, cols, core, width), stacked, preferred_element_type=F32
            ).astype(BF16)
            whole[t, m] = part
            if t:
                sends[t - 1][m] = part


def level_two_kernel(
    nodes, group_rows, rows_one, parent_two, order_two, own, sibling, ours, theirs, *refs
):
    height, width = own.shape[0], own.shape[1]
    here, chip, core = lax.axis_index(ROW), lax.axis_index(CHIP), lax.axis_index(CORE)
    pieces, refs = refs[:group_rows], refs[group_rows:]
    factors, refs = refs[:nodes], refs[nodes:]
    columns, smalls, refs = refs[:nodes], refs[nodes : 2 * nodes], refs[2 * nodes :]
    inverse, panels, near, sems = refs
    per_row, tile = panels.shape[1], panels.shape[2]
    copies = load_inverse(own, sibling, inverse, sems) + load_panels(pieces, panels, sems, here)
    for copy in copies:
        copy.wait()
    for t in range(nodes):
        at = chip ^ t
        node = 2 * at + core
        parent = parent_two[node]
        is_ours = parent % 2 == core
        parent_at = (parent // 2) ^ chip
        cols = [
            rows_one[parent, order_two[node, chip * per_row + n]] - chip * 2 * width
            for n in range(per_row)
        ]
        stacked = panels[at].reshape(per_row * tile, tile)
        link = factors[t][per_row]
        for m in range(per_row):
            place = order_two[node, here * per_row + m]
            row = rows_one[parent, place] - here * height
            local = place - here * per_row
            near_tile = jnp.where(is_ours, ours[parent_at, local], theirs[parent_at, local])
            near[m] = near_tile
            part = jnp.dot(
                block_row(inverse, row, cols, core, width), stacked, preferred_element_type=F32
            ) - jnp.dot(near_tile, link, preferred_element_type=F32)
            columns[t][m] = part.astype(BF16)
        factor = factors[t][:per_row].reshape(per_row * tile, tile)
        contract = (((0,), (0,)), ((), ()))
        smalls[t][0] = lax.dot_general(
            near[...].reshape(per_row * tile, tile), factor, contract, preferred_element_type=F32
        ).astype(BF16)
        smalls[t][1] = lax.dot_general(
            factor,
            columns[t][...].reshape(per_row * tile, tile),
            contract,
            preferred_element_type=F32,
        ).astype(BF16)


SMEM = pl.BlockSpec(memory_space=pltpu.SMEM)
VMEM = pl.BlockSpec(memory_space=pltpu.VMEM)
ANY = pl.BlockSpec(memory_space=pl.ANY)


def level_one(rows_one, own, sibling, pieces):
    nodes, group, tile = pieces[0].shape[0], pieces[0].shape[1], pieces[0].shape[2]
    count = len(pieces)
    per_row = group * count
    flops = 2 * nodes * per_row * per_row * tile**3
    return pl.pallas_call(
        functools.partial(level_one_kernel, nodes, count),
        out_shape=[jax.ShapeDtypeStruct((nodes, per_row, tile, tile), BF16)]
        + [jax.ShapeDtypeStruct((per_row, tile, tile), BF16)] * (nodes - 1),
        in_specs=[SMEM, ANY, ANY] + [ANY] * count,
        out_specs=[VMEM] * nodes,
        scratch_shapes=[
            pltpu.VMEM((2,) + own.shape, BF16),
            pltpu.VMEM((nodes, per_row, tile, tile), BF16),
            pltpu.SemaphoreType.DMA((2 + count,)),
        ],
        compiler_params=pltpu.CompilerParams(vmem_limit_bytes=48 << 20),
        cost_estimate=pl.CostEstimate(flops=flops, bytes_accessed=12 << 20, transcendentals=0),
        name="level_one",
    )(rows_one, own, sibling, *pieces)


def level_two(rows_one, parent_two, order_two, own, sibling, ours, theirs, pieces, factors):
    nodes, group, tile = pieces[0].shape[0], pieces[0].shape[1], pieces[0].shape[2]
    count = len(pieces)
    per_row = group * count
    flops = 2 * nodes * per_row * (per_row + 3) * tile**3
    return pl.pallas_call(
        functools.partial(level_two_kernel, nodes, count),
        out_shape=[jax.ShapeDtypeStruct((per_row, tile, tile), BF16)] * nodes
        + [jax.ShapeDtypeStruct((2, tile, tile), BF16)] * nodes,
        in_specs=[SMEM] * 3 + [ANY, ANY, VMEM, VMEM] + [ANY] * count + [VMEM] * nodes,
        out_specs=[VMEM] * (2 * nodes),
        scratch_shapes=[
            pltpu.VMEM((2,) + own.shape, BF16),
            pltpu.VMEM((nodes, per_row, tile, tile), BF16),
            pltpu.VMEM((per_row, tile, tile), BF16),
            pltpu.SemaphoreType.DMA((2 + count,)),
        ],
        compiler_params=pltpu.CompilerParams(vmem_limit_bytes=56 << 20),
        cost_estimate=pl.CostEstimate(flops=flops, bytes_accessed=16 << 20, transcendentals=0),
        name="level_two",
    )(rows_one, parent_two, order_two, own, sibling, ours, theirs, *pieces, *factors)


def distribute(panel):
    rows = lax.axis_size(ROW)
    quarters = panel.reshape((rows, panel.shape[0] // rows) + panel.shape[1:])
    quarters = lax.all_to_all(quarters, ROW, 0, 0, tiled=True)
    quarters = lax.all_to_all(quarters, CHIP, 0, 0, tiled=True)
    return spread(quarters, ROW)


def total(parts):
    return functools.reduce(jnp.add, [part.astype(F32) for part in parts])


def local(
    inverse_top, rows_one, panel_one, base_one, parent_two, order_two, panel_two, link_two, base_two
):
    chip, core = lax.axis_index(CHIP), lax.axis_index(CORE)
    sibling = exchange(inverse_top, CORE, 1)
    pieces_one = distribute(panel_one[0])
    pieces_two = distribute(panel_two[0])
    factors = spread(jnp.concatenate([panel_two[0], link_two], axis=0), CHIP)
    ours, *sends = level_one(rows_one, inverse_top, sibling, pieces_one)
    theirs = exchange(ours, CORE, 1)
    parts_one = [ours[0]] + [exchange(send, CHIP, t + 1) for t, send in enumerate(sends)]
    outs = level_two(
        rows_one, parent_two, order_two, inverse_top, sibling, ours, theirs, pieces_two, factors
    )
    nodes = len(outs) // 2
    parts_two = [outs[0]] + [exchange(outs[t], CHIP, t) for t in range(1, nodes)]
    parts_small = [outs[nodes]] + [exchange(outs[nodes + t], CHIP, t) for t in range(1, nodes)]
    column_one = (-total(parts_one)).astype(BF16)
    column_two = (-total(parts_two)).astype(BF16)
    sums = total(spread(total(parts_small).astype(BF16), ROW))
    part = jnp.einsum("mij,mil->jl", panel_one[0], column_one, preferred_element_type=F32)
    diagonal_one = (base_one[0] - total(spread(part.astype(BF16), ROW))).astype(BF16)
    pair = jnp.stack([diagonal_one, exchange(diagonal_one, CORE, 1)])
    diagonals = jnp.stack(spread(pair, CHIP))
    parent = parent_two[2 * chip + core]
    near_diagonal = diagonals[(parent // 2) ^ chip, (parent % 2) ^ core]
    link = link_two[0]
    upper = (sums[0] - jnp.dot(near_diagonal, link, preferred_element_type=F32)).astype(BF16)
    link_term = jnp.einsum("ij,il->jl", link, upper, preferred_element_type=F32)
    diagonal_two = (base_two[0] - link_term + sums[1]).astype(BF16)
    return (
        column_one[None],
        diagonal_one[None],
        column_two[None],
        upper[None],
        diagonal_two[None],
    )


def solution(mesh):
    rows, columns = mesh.devices.shape
    fine = Mesh(mesh.devices.reshape(rows, columns // 2, 2), (ROW, CHIP, CORE))
    col = (CHIP, CORE)
    return jax.shard_map(
        local,
        mesh=fine,
        in_specs=(
            P(ROW, col, None, None),
            P(),
            P(col, ROW, None, None),
            P(col, None, None),
            P(),
            P(),
            P(col, ROW, None, None),
            P(col, None, None),
            P(col, None, None),
        ),
        out_specs=(
            P(col, ROW, None, None),
            P(col, None, None),
            P(col, ROW, None, None),
            P(col, None, None),
            P(col, None, None),
        ),
        check_vma=False,
    )
```

time: 311 us -> 171 us (0.55)
  waiting for transfers between devices: 195 us -> 73.1 us
  starting transfers between devices: 8.58 us -> 44.5 us
  local copies, waits for them, and re-layouts: 38.6 us -> 2.89 us
  matrix products: 25.3 us -> 1.32 us
  Pallas kernels: 0 us -> 16.1 us
  between operations: 18.2 us -> 3.59 us
  blocking collectives: 14.3 us -> 23.8 us
  other arithmetic: 9.38 us -> 5.07 us
    reduce_scatter x2 -> x0, waiting for transfers between devices: 79.7 us -> none  [the longest x1 45.4 us: local(): lax.psum_scatter(tile_products(inverse_top, flat_one, row_one, col_one).a...]
    ppermute x0 -> x30, waiting for transfers between devices: none -> 73.1 us  [exchange(): return lax.ppermute(x, axis, [(i, i ^ step) for i in range(size)])]
    all_gather x3 -> x0, waiting for transfers between devices: 40.7 us -> none  [the longest x1 29.8 us: local(): full_one = lax.all_gather(panel_one, 'prow', axis=1, tiled=True)]
    psum x1 -> x0, waiting for transfers between devices: 40.6 us -> none  [local(): lax.psum(diag_part.astype(jnp.bfloat16), 'prow').astype(jnp.float32)]
    gather x15 -> x0, local copies, waits for them, and re-layouts: 36.5 us -> none  [the longest x2 26 us: tile_products(): blocks = inverse_local[row_local[:, :, None], col_local[:, None, :]]]
    ppermute x0 -> x30, starting transfers between devices: none -> 35.1 us  [exchange(): return lax.ppermute(x, axis, [(i, i ^ step) for i in range(size)])]
    all_to_all x2, waiting for transfers between devices: 33.1 us -> 0.01 us  [the longest x1 0.01 us: distribute(): quarters = lax.all_to_all(quarters, ROW, 0, 0, tiled=True)]
    dot_general x8 -> x3, matrix products: 25.3 us -> 1.32 us  [the longest x1 0.83 us: local(): link_term = jnp.einsum('ij,il->jl', link, upper, preferred_element_type=F32)]
  transfers between devices with their start and end apart: 8 -> 32, of which waited for: 7 -> 10; matrix products, arithmetic and copies ran while one was open for 21% -> 4% of each run, Pallas kernels for 0% -> 9%
where the time goes in v1:
time: 171 us; the launch traced here: 170 us
  waiting for transfers between devices  73.1 us (43%)
  starting transfers between devices  44.5 us (26%)
  blocking collectives  23.8 us (14%)
  Pallas kernels  16.1 us (9%)
  other arithmetic  5.07 us (3%)
  between operations  3.59 us (2%)
  local copies, waits for them, and re-layouts  2.89 us (2%)
    ppermute x30, waiting for transfers between devices, exchange(): return lax.ppermute(x, axis, [(i, i ^ step) for i in range(size)])  73.1 us
    ppermute x30, starting transfers between devices, exchange(): return lax.ppermute(x, axis, [(i, i ^ step) for i in range(size)])  35.1 us
    all_to_all x1, blocking collectives, distribute(): quarters = lax.all_to_all(quarters, CHIP, 0, 0, tiled=True)  12.7 us
    all_to_all x1, blocking collectives, distribute(): quarters = lax.all_to_all(quarters, ROW, 0, 0, tiled=True)  11.1 us
    pallas_call x1, Pallas kernels, level_two(): pl.pallas_call(functools.partial(level_two_kernel, nodes, count), out_sha...  9.64 us
    pallas_call x1, Pallas kernels, level_one(): pl.pallas_call(functools.partial(level_one_kernel, nodes, count), out_sha...  6.5 us
    all_to_all x1, starting transfers between devices, distribute(): quarters = lax.all_to_all(quarters, CHIP, 0, 0, tiled=True)  5.36 us
    all_to_all x1, starting transfers between devices, distribute(): quarters = lax.all_to_all(quarters, ROW, 0, 0, tiled=True)  4.04 us
  transfers between devices with their start and end apart: 32, of which 10 were waited for; matrix products, arithmetic and copies ran while one was open for 4% of the time, Pallas kernels for 9%

profile of v1, /device:TPU:0, one launch (start us, length us, event | category | flops | bytes accessed | tf_op | source)
XLA Modules:
  0.0 170.4 jit_solution(8589558521793094425)
XLA Ops:
  1.1 11.1 %all_to_all.20 = bf16[4,2,128,128]{3,2,1,0:T(8,128)(2,1)S(1)} all-to-all(bf16[4,2,128,128]{3,2,1,0:T(8,128)(2,1)} %bitcast.78), channel_id=1, replica_groups=mesh['prow'=4,'pchip'=4,'pcore'=2] {'prow'}, dimensions={0} | all-to-all | bytes 524288 | tf_op jit(solution)/shard_map/all_to_all | solution.py:176
  12.2 12.7 %all_to_all.21.refs_0_ = bf16[4,2,128,128]{3,2,1,0:T(8,128)(2,1)S(1)} all-to-all(bf16[4,2,128,128]{3,2,1,0:T(8,128)(2,1)S(1)} %all_to_all.20), channel_id=1, replica_groups=mesh['prow'=4,'pchip'=4,'pcore'=2] {'pchip'}, dimensions={0} | all-to-all | bytes 524288 | tf_op jit(solution)/shard_map/all_to_all | solution.py:177
  25.0 1.3 collective-permute-start.1
  26.8 1.7 collective-permute-start.3
  28.5 4.0 %all-to-all-start.2 = ((bf16[4,2,128,128]{3,2,1,0:T(8,128)(2,1)}), bf16[4,2,128,128]{3,2,1,0:T(8,128)(2,1)}, u32[]{:S(2)}, u32[]{:S(2)}) async-start(bf16[4,2,128,128]{3,2,1,0:T(8,128)(2,1)} %bitcast.76), calls=%async_computation.2 | async-start | bytes 524288 | tf_op jit(solution)/shard_map/all_to_all | solution.py:176
  34.1 4.5 %collective-permute-done.2.refs_2_ = bf16[4,2,128,128]{3,2,1,0:T(8,128)(2,1)S(1)} collective-permute-done((bf16[4,2,128,128]{3,2,1,0:T(8,128)(2,1)S(1)}, bf16[4,2,128,128]{3,2,1,0:T(8,128)(2,1)S(1)}, u32[]{:S(2)}, u32[]{:S(2)}) %collective-permute-start.2) | collective-permute-done | bytes 262176 | tf_op jit(solution)/shard_map/ppermute | solution.py:17
  39.3 6.5 %level_one.1 = (bf16[4,8,128,128]{3,2,1,0:T(8,128)(2,1)S(1)}, bf16[8,128,128]{2,1,0:T(8,128)(2,1)S(1)}, bf16[8,128,128]{2,1,0:T(8,128)(2,1)S(1)}, bf16[8,128,128]{2,1,0:T(8,128)(2,1)S(1)}) custom-call(s32[8,32]{1,0:T(8,128)S(1)} %copy-done.1, bf16[16,8,128,128]{3,2,1,0:T(8,128)(2,1)} %own.3, bf16[16,8,128,128]{3,2,1,0:T(8,128)(2,1)} %collective-permute-done.sibling, ...), custom_call_target="tpu_custom_call" | custom-call | flops 1073741824 | bytes 12582912 | tf_op jit(solution)/shard_map/level_one/pallas_call | solution.py:133
  46.0 5.4 %all-to-all-start.3 = ((bf16[4,2,128,128]{3,2,1,0:T(8,128)(2,1)}), bf16[4,2,128,128]{3,2,1,0:T(8,128)(2,1)S(1)}, u32[]{:S(2)}, u32[]{:S(2)}) async-start(bf16[4,2,128,128]{3,2,1,0:T(8,128)(2,1)} %all-to-all-done.2), calls=%async_computation.3 | async-start | bytes 524288 | tf_op jit(solution)/shard_map/all_to_all | solution.py:177
  51.3 2.9 %collective-permute-start.15 = (bf16[9,128,128]{2,1,0:T(8,128)(2,1)S(1)}, bf16[9,128,128]{2,1,0:T(8,128)(2,1)S(1)}, u32[]{:S(2)}, u32[]{:S(2)}) collective-permute-start(bf16[9,128,128]{2,1,0:T(8,128)(2,1)S(1)} %pad_maximum_fusion.refs_4_), channel_id=1, source_target_pairs={{0,4},{2,6},{4,0},{6,2},{1,5},{3,7},{5,1},{7,3},{8,12},{10,14},{12... | collective-permute-start | bytes 884744 | tf_op jit(solution)/shard_map/ppermute | solution.py:17
  54.2 1.5 collective-permute-start.6
  55.7 1.5 collective-permute-start.5
  57.2 1.5 collective-permute-start.4
  62.0 23.5 %collective-permute-done.15.refs_6_ = bf16[9,128,128]{2,1,0:T(8,128)(2,1)S(1)} collective-permute-done((bf16[9,128,128]{2,1,0:T(8,128)(2,1)S(1)}, bf16[9,128,128]{2,1,0:T(8,128)(2,1)S(1)}, u32[]{:S(2)}, u32[]{:S(2)}) %collective-permute-start.15) | collective-permute-done | bytes 294944 | tf_op jit(solution)/shard_map/ppermute | solution.py:17
  85.4 1.4 collective-permute-start.16
  87.0 16.1 %collective-permute-done.5 = bf16[8,128,128]{2,1,0:T(8,128)(2,1)} collective-permute-done((bf16[8,128,128]{2,1,0:T(8,128)(2,1)S(1)}, bf16[8,128,128]{2,1,0:T(8,128)(2,1)}, u32[]{:S(2)}, u32[]{:S(2)}) %collective-permute-start.5) | collective-permute-done | bytes 262176 | tf_op jit(solution)/shard_map/ppermute | solution.py:17
  104.3 1.3 fusion.6
  105.9 2.3 %collective-permute-start.9 = (bf16[128,128]{0,1:T(8,128)(2,1)S(1)}, bf16[128,128]{0,1:T(8,128)(2,1)S(1)}, u32[]{:S(2)}, u32[]{:S(2)}) collective-permute-start(bf16[128,128]{0,1:T(8,128)(2,1)S(1)} %fusion.2), channel_id=1, source_target_pairs={{0,24},{8,16},{16,8},{24,0},{1,25},{9,17},{17,9},{25,1},{2,26},{10... | collective-permute-start | bytes 98312 | tf_op jit(solution)/shard_map/ppermute | solution.py:17
  108.2 1.5 collective-permute-start.8
  109.7 6.9 %collective-permute-done.12.refs_2_ = bf16[4,2,128,128]{3,2,1,0:T(8,128)(2,1)S(1)} collective-permute-done((bf16[4,2,128,128]{3,2,1,0:T(8,128)(2,1)S(1)}, bf16[4,2,128,128]{3,2,1,0:T(8,128)(2,1)S(1)}, u32[]{:S(2)}, u32[]{:S(2)}) %collective-permute-start.12) | collective-permute-done | bytes 262176 | tf_op jit(solution)/shard_map/ppermute | solution.py:17
  117.4 9.6 %level_two.1 = (bf16[8,128,128]{2,1,0:T(8,128)(2,1)}, bf16[8,128,128]{2,1,0:T(8,128)(2,1)}, bf16[8,128,128]{2,1,0:T(8,128)(2,1)}, bf16[8,128,128]{2,1,0:T(8,128)...) custom-call(s32[8,32]{1,0:T(8,128)} %rows_one.3, ...), custom_call_target="tpu_custom_call" | custom-call | flops 1476395008 | bytes 16777216 | tf_op jit(solution)/shard_map/level_two/pallas_call | solution.py:155
  127.1 1.6 collective-permute-start.22
  128.7 2.9 %collective-permute-start.20 = (bf16[2,128,128]{2,1,0:T(8,128)(2,1)}, bf16[2,128,128]{2,1,0:T(8,128)(2,1)S(1)}, u32[]{:S(2)}, u32[]{:S(2)}) collective-permute-start(bf16[2,128,128]{2,1,0:T(8,128)(2,1)} %get-tuple-element.26), channel_id=1, source_target_pairs={{0,2},{2,0},{4,6},{6,4},{1,3},{3,1},{5,7},{7,5},{8,10},{10,8},{12,... | collective-permute-start | bytes 196616 | tf_op jit(solution)/shard_map/ppermute | solution.py:17
  133.5 1.4 collective-permute-done.21
  135.7 2.0 %collective-permute-start.25 = (bf16[2,128,128]{2,1,0:T(8,128)(2,1)S(1)}, bf16[2,128,128]{2,1,0:T(8,128)(2,1)S(1)}, u32[]{:S(2)}, u32[]{:S(2)}) collective-permute-start(bf16[2,128,128]{2,1,0:T(8,128)(2,1)S(1)} %add_convert_fusion), channel_id=1, source_target_pairs={{0,24},{8,16},{16,8},{24,0},{1,25},{9,17},{17,9},{25,1},{2,26},{10... | collective-permute-start | bytes 196616 | tf_op jit(solution)/shard_map/ppermute | solution.py:17
  137.7 1.5 collective-permute-start.24
  139.3 2.1 %collective-permute-start.29 = (bf16[2,128,128]{1,2,0:T(8,128)(2,1)S(1)}, bf16[2,128,128]{1,2,0:T(8,128)(2,1)S(1)}, u32[]{:S(2)}, u32[]{:S(2)}) collective-permute-start(bf16[2,128,128]{1,2,0:T(8,128)(2,1)S(1)} %get-tuple-element.35), channel_id=1, source_target_pairs={{0,6},{2,4},{4,2},{6,0},{1,7},{3,5},{5,3},{7,1},{8,14},{10,12},{12... | collective-permute-start | bytes 196616 | tf_op jit(solution)/shard_map/ppermute | solution.py:17
  142.0 1.7 %collective-permute-start.27 = (bf16[2,128,128]{1,2,0:T(8,128)(2,1)S(1)}, bf16[2,128,128]{1,2,0:T(8,128)(2,1)S(1)}, u32[]{:S(2)}, u32[]{:S(2)}) collective-permute-start(bf16[2,128,128]{1,2,0:T(8,128)(2,1)S(1)} %get-tuple-element.35), channel_id=1, source_target_pairs={{0,2},{2,0},{4,6},{6,4},{1,3},{3,1},{5,7},{7,5},{8,10},{10,8},{12,... | collective-permute-start | bytes 196616 | tf_op jit(solution)/shard_map/ppermute | solution.py:17
  143.8 2.0 %collective-permute-start.19 = (bf16[8,128,128]{2,1,0:T(8,128)(2,1)}, bf16[8,128,128]{2,1,0:T(8,128)(2,1)S(1)}, u32[]{:S(2)}, u32[]{:S(2)}) collective-permute-start(bf16[8,128,128]{2,1,0:T(8,128)(2,1)} %get-tuple-element.24), channel_id=1, source_target_pairs={{0,6},{2,4},{4,2},{6,0},{1,7},{3,5},{5,3},{7,1},{8,14},{10,12},{12... | collective-permute-start | bytes 786440 | tf_op jit(solution)/shard_map/ppermute | solution.py:17
  146.1 2.3 %collective-permute-start.17 = (bf16[8,128,128]{2,1,0:T(8,128)(2,1)}, bf16[8,128,128]{2,1,0:T(8,128)(2,1)S(1)}, u32[]{:S(2)}, u32[]{:S(2)}) collective-permute-start(bf16[8,128,128]{2,1,0:T(8,128)(2,1)} %get-tuple-element.22), channel_id=1, source_target_pairs={{0,2},{2,0},{4,6},{6,4},{1,3},{3,1},{5,7},{7,5},{8,10},{10,8},{12,... | collective-permute-start | bytes 786440 | tf_op jit(solution)/shard_map/ppermute | solution.py:17
  148.4 9.1 %collective-permute-done.28 = bf16[2,128,128]{1,2,0:T(8,128)(2,1)S(1)} collective-permute-done((bf16[2,128,128]{1,2,0:T(8,128)(2,1)S(1)}, bf16[2,128,128]{1,2,0:T(8,128)(2,1)S(1)}, u32[]{:S(2)}, u32[]{:S(2)}) %collective-permute-start.28) | collective-permute-done | bytes 65568 | tf_op jit(solution)/shard_map/ppermute | solution.py:17
  158.6 10.0 %collective-permute-done.18 = bf16[8,128,128]{2,1,0:T(8,128)(2,1)S(1)} collective-permute-done((bf16[8,128,128]{2,1,0:T(8,128)(2,1)}, bf16[8,128,128]{2,1,0:T(8,128)(2,1)S(1)}, u32[]{:S(2)}, u32[]{:S(2)}) %collective-permute-start.18) | collective-permute-done | bytes 262176 | tf_op jit(solution)/shard_map/ppermute | solution.py:17
  168.6 1.8 %fusion.7 = bf16[1,8,128,128]{3,2,1,0:T(8,128)(2,1)} fusion(bf16[8,128,128]{2,1,0:T(8,128)(2,1)S(1)} %collective-permute-done.19, bf16[8,128,128]{2,1,0:T(8,128)(2,1)S(1)} %collective-permute-done.18, bf16[8,128,128]{2,1,0:T(8,128)(2,1)S(1)} %collective-permute-done.17, bf16[8,128,128]{2,1,0:T(8,128)(2,1)} %get-tuple-element.21), kind=kLoop, calls=%fused_computation.12 | loop fusion | flops 1179648 | bytes 1310720 | tf_op jit(solution)/shard_map/broadcast_in_dim | solution.py:218
  (81 shorter events, 11.3 us)
Async XLA Ops:
  0.6 38.0 %collective-permute-start = (bf16[16,8,128,128]{3,2,1,0:T(8,128)(2,1)}, bf16[16,8,128,128]{3,2,1,0:T(8,128)(2,1)}, u32[]{:S(2)}, u32[]{:S(2)}) collective-permute-start(bf16[16,8,128,128]{3,2,1,0:T(8,128)(2,1)} %own.3), channel_id=1, source_target_pairs={{0,1},{1,0},{2,3},{3,2},{4,5},{5,4},{6,7},{7,6},{8,9},{9,8},{10,11... | collective-permute-start | bytes 12582920 | tf_op jit(solution)/shard_map/ppermute | solution.py:17
  25.0 9.2 %collective-permute-start.1 = (bf16[4,2,128,128]{3,2,1,0:T(8,128)(2,1)S(1)}, bf16[4,2,128,128]{3,2,1,0:T(8,128)(2,1)S(1)}, u32[]{:S(2)}, u32[]{:S(2)}) collective-permute-start(bf16[4,2,128,128]{3,2,1,0:T(8,128)(2,1)S(1)} %all_to_all.21.refs_0_), channel_id=1, source_target_pairs={{0,8},{8,0},{16,24},{24,16},{1,9},{9,1},{17,25},{25,17},{2,10},{10... | collective-permute-start | bytes 786440 | tf_op jit(solution)/shard_map/ppermute | solution.py:17
  26.2 12.4 %collective-permute-start.2 = (bf16[4,2,128,128]{3,2,1,0:T(8,128)(2,1)S(1)}, bf16[4,2,128,128]{3,2,1,0:T(8,128)(2,1)S(1)}, u32[]{:S(2)}, u32[]{:S(2)}) collective-permute-start(bf16[4,2,128,128]{3,2,1,0:T(8,128)(2,1)S(1)} %all_to_all.21.refs_0_), channel_id=1, source_target_pairs={{0,16},{8,24},{16,0},{24,8},{1,17},{9,25},{17,1},{25,9},{2,18},{10... | collective-permute-start | bytes 786440 | tf_op jit(solution)/shard_map/ppermute | solution.py:17
  26.8 11.9 %collective-permute-start.3 = (bf16[4,2,128,128]{3,2,1,0:T(8,128)(2,1)S(1)}, bf16[4,2,128,128]{3,2,1,0:T(8,128)(2,1)S(1)}, u32[]{:S(2)}, u32[]{:S(2)}) collective-permute-start(bf16[4,2,128,128]{3,2,1,0:T(8,128)(2,1)S(1)} %all_to_all.21.refs_0_), channel_id=1, source_target_pairs={{0,24},{8,16},{16,8},{24,0},{1,25},{9,17},{17,9},{25,1},{2,26},{10... | collective-permute-start | bytes 786440 | tf_op jit(solution)/shard_map/ppermute | solution.py:17
  28.5 17.5 %all-to-all-start.2 = ((bf16[4,2,128,128]{3,2,1,0:T(8,128)(2,1)}), bf16[4,2,128,128]{3,2,1,0:T(8,128)(2,1)}, u32[]{:S(2)}, u32[]{:S(2)}) async-start(bf16[4,2,128,128]{3,2,1,0:T(8,128)(2,1)} %bitcast.76), calls=%async_computation.2 | async-start | bytes 524288 | tf_op jit(solution)/shard_map/all_to_all | solution.py:176
  33.6 23.6 %collective-permute-start.14 = (bf16[9,128,128]{2,1,0:T(8,128)(2,1)S(1)}, bf16[9,128,128]{2,1,0:T(8,128)(2,1)}, u32[]{:S(2)}, u32[]{:S(2)}) collective-permute-start(bf16[9,128,128]{2,1,0:T(8,128)(2,1)S(1)} %pad_maximum_fusion.refs_4_), channel_id=1, source_target_pairs={{0,2},{2,0},{4,6},{6,4},{1,3},{3,1},{5,7},{7,5},{8,10},{10,8},{12,... | collective-permute-start | bytes 884744 | tf_op jit(solution)/shard_map/ppermute | solution.py:17
  45.9 70.8 %collective-permute-start.10 = (bf16[4,8,128,128]{3,2,1,0:T(8,128)(2,1)S(1)}, bf16[4,8,128,128]{3,2,1,0:T(8,128)(2,1)}, u32[]{:S(2)}, u32[]{:S(2)}) collective-permute-start(bf16[4,8,128,128]{3,2,1,0:T(8,128)(2,1)S(1)} %get-tuple-element.17.ours), channel_id=1, source_target_pairs={{0,1},{1,0},{2,3},{3,2},{4,5},{5,4},{6,7},{7,6},{8,9},{9,8},{10,11... | collective-permute-start | bytes 3145736 | tf_op jit(solution)/shard_map/ppermute | solution.py:17
  46.0 40.9 %all-to-all-start.3 = ((bf16[4,2,128,128]{3,2,1,0:T(8,128)(2,1)}), bf16[4,2,128,128]{3,2,1,0:T(8,128)(2,1)S(1)}, u32[]{:S(2)}, u32[]{:S(2)}) async-start(bf16[4,2,128,128]{3,2,1,0:T(8,128)(2,1)} %all-to-all-done.2), calls=%async_computation.3 | async-start | bytes 524288 | tf_op jit(solution)/shard_map/all_to_all | solution.py:177
  51.3 34.1 %collective-permute-start.15 = (bf16[9,128,128]{2,1,0:T(8,128)(2,1)S(1)}, bf16[9,128,128]{2,1,0:T(8,128)(2,1)S(1)}, u32[]{:S(2)}, u32[]{:S(2)}) collective-permute-start(bf16[9,128,128]{2,1,0:T(8,128)(2,1)S(1)} %pad_maximum_fusion.refs_4_), channel_id=1, source_target_pairs={{0,4},{2,6},{4,0},{6,2},{1,5},{3,7},{5,1},{7,3},{8,12},{10,14},{12... | collective-permute-start | bytes 884744 | tf_op jit(solution)/shard_map/ppermute | solution.py:17
  54.2 32.6 %collective-permute-start.6 = (bf16[8,128,128]{2,1,0:T(8,128)(2,1)S(1)}, bf16[8,128,128]{2,1,0:T(8,128)(2,1)}, u32[]{:S(2)}, u32[]{:S(2)}) collective-permute-start(bf16[8,128,128]{2,1,0:T(8,128)(2,1)S(1)} %get-tuple-element.20), channel_id=1, source_target_pairs={{0,6},{2,4},{4,2},{6,0},{1,7},{3,5},{5,3},{7,1},{8,14},{10,12},{12... | collective-permute-start | bytes 786440 | tf_op jit(solution)/shard_map/ppermute | solution.py:17
  55.7 47.4 %collective-permute-start.5 = (bf16[8,128,128]{2,1,0:T(8,128)(2,1)S(1)}, bf16[8,128,128]{2,1,0:T(8,128)(2,1)}, u32[]{:S(2)}, u32[]{:S(2)}) collective-permute-start(bf16[8,128,128]{2,1,0:T(8,128)(2,1)S(1)} %get-tuple-element.19), channel_id=1, source_target_pairs={{0,4},{2,6},{4,0},{6,2},{1,5},{3,7},{5,1},{7,3},{8,12},{10,14},{12... | collective-permute-start | bytes 786440 | tf_op jit(solution)/shard_map/ppermute | solution.py:17
  57.2 46.5 %collective-permute-start.4 = (bf16[8,128,128]{2,1,0:T(8,128)(2,1)S(1)}, bf16[8,128,128]{2,1,0:T(8,128)(2,1)}, u32[]{:S(2)}, u32[]{:S(2)}) collective-permute-start(bf16[8,128,128]{2,1,0:T(8,128)(2,1)S(1)} %get-tuple-element.18), channel_id=1, source_target_pairs={{0,2},{2,0},{4,6},{6,4},{1,3},{3,1},{5,7},{7,5},{8,10},{10,8},{12,... | collective-permute-start | bytes 786440 | tf_op jit(solution)/shard_map/ppermute | solution.py:17
  85.4 20.5 %collective-permute-start.16 = (bf16[9,128,128]{2,1,0:T(8,128)(2,1)S(1)}, bf16[9,128,128]{2,1,0:T(8,128)(2,1)S(1)}, u32[]{:S(2)}, u32[]{:S(2)}) collective-permute-start(bf16[9,128,128]{2,1,0:T(8,128)(2,1)S(1)} %pad_maximum_fusion.refs_4_), channel_id=1, source_target_pairs={{0,6},{2,4},{4,2},{6,0},{1,7},{3,5},{5,3},{7,1},{8,14},{10,12},{12... | collective-permute-start | bytes 884744 | tf_op jit(solution)/shard_map/ppermute | solution.py:17
  86.9 21.3 %collective-permute-start.11 = (bf16[4,2,128,128]{3,2,1,0:T(8,128)(2,1)S(1)}, bf16[4,2,128,128]{3,2,1,0:T(8,128)(2,1)S(1)}, u32[]{:S(2)}, u32[]{:S(2)}) collective-permute-start(bf16[4,2,128,128]{3,2,1,0:T(8,128)(2,1)S(1)} %all-to-all-done.3.refs_0_), channel_id=1, source_target_pairs={{0,8},{8,0},{16,24},{24,16},{1,9},{9,1},{17,25},{25,17},{2,10},{10... | collective-permute-start | bytes 786440 | tf_op jit(solution)/shard_map/ppermute | solution.py:17
  103.1 13.5 %collective-permute-start.12 = (bf16[4,2,128,128]{3,2,1,0:T(8,128)(2,1)S(1)}, bf16[4,2,128,128]{3,2,1,0:T(8,128)(2,1)S(1)}, u32[]{:S(2)}, u32[]{:S(2)}) collective-permute-start(bf16[4,2,128,128]{3,2,1,0:T(8,128)(2,1)S(1)} %all-to-all-done.3.refs_0_), channel_id=1, source_target_pairs={{0,16},{8,24},{16,0},{24,8},{1,17},{9,25},{17,1},{25,9},{2,18},{10... | collective-permute-start | bytes 786440 | tf_op jit(solution)/shard_map/ppermute | solution.py:17
  103.6 13.0 %collective-permute-start.13 = (bf16[4,2,128,128]{3,2,1,0:T(8,128)(2,1)S(1)}, bf16[4,2,128,128]{3,2,1,0:T(8,128)(2,1)S(1)}, u32[]{:S(2)}, u32[]{:S(2)}) collective-permute-start(bf16[4,2,128,128]{3,2,1,0:T(8,128)(2,1)S(1)} %all-to-all-done.3.refs_0_), channel_id=1, source_target_pairs={{0,24},{8,16},{16,8},{24,0},{1,25},{9,17},{17,9},{25,1},{2,26},{10... | collective-permute-start | bytes 786440 | tf_op jit(solution)/shard_map/ppermute | solution.py:17
  105.9 22.7 %collective-permute-start.9 = (bf16[128,128]{0,1:T(8,128)(2,1)S(1)}, bf16[128,128]{0,1:T(8,128)(2,1)S(1)}, u32[]{:S(2)}, u32[]{:S(2)}) collective-permute-start(bf16[128,128]{0,1:T(8,128)(2,1)S(1)} %fusion.2), channel_id=1, source_target_pairs={{0,24},{8,16},{16,8},{24,0},{1,25},{9,17},{17,9},{25,1},{2,26},{10... | collective-permute-start | bytes 98312 | tf_op jit(solution)/shard_map/ppermute | solution.py:17
  108.2 23.3 %collective-permute-start.8 = (bf16[128,128]{0,1:T(8,128)(2,1)S(1)}, bf16[128,128]{0,1:T(8,128)(2,1)S(1)}, u32[]{:S(2)}, u32[]{:S(2)}) collective-permute-start(bf16[128,128]{0,1:T(8,128)(2,1)S(1)} %fusion.2), channel_id=1, source_target_pairs={{0,16},{8,24},{16,0},{24,8},{1,17},{9,25},{17,1},{25,9},{2,18},{10... | collective-permute-start | bytes 98312 | tf_op jit(solution)/shard_map/ppermute | solution.py:17
  116.6 14.9 %collective-permute-start.7 = (bf16[128,128]{0,1:T(8,128)(2,1)S(1)}, bf16[128,128]{0,1:T(8,128)(2,1)S(1)}, u32[]{:S(2)}, u32[]{:S(2)}) collective-permute-start(bf16[128,128]{0,1:T(8,128)(2,1)S(1)} %fusion.2), channel_id=1, source_target_pairs={{0,8},{8,0},{16,24},{24,16},{1,9},{9,1},{17,25},{25,17},{2,10},{10... | collective-permute-start | bytes 98312 | tf_op jit(solution)/shard_map/ppermute | solution.py:17
  127.1 6.4 %collective-permute-start.22 = (bf16[2,128,128]{2,1,0:T(8,128)(2,1)}, bf16[2,128,128]{2,1,0:T(8,128)(2,1)S(1)}, u32[]{:S(2)}, u32[]{:S(2)}) collective-permute-start(bf16[2,128,128]{2,1,0:T(8,128)(2,1)} %get-tuple-element.28), channel_id=1, source_target_pairs={{0,6},{2,4},{4,2},{6,0},{1,7},{3,5},{5,3},{7,1},{8,14},{10,12},{12... | collective-permute-start | bytes 196616 | tf_op jit(solution)/shard_map/ppermute | solution.py:17
  128.7 6.2 %collective-permute-start.21 = (bf16[2,128,128]{2,1,0:T(8,128)(2,1)}, bf16[2,128,128]{2,1,0:T(8,128)(2,1)S(1)}, u32[]{:S(2)}, u32[]{:S(2)}) collective-permute-start(bf16[2,128,128]{2,1,0:T(8,128)(2,1)} %get-tuple-element.27), channel_id=1, source_target_pairs={{0,4},{2,6},{4,0},{6,2},{1,5},{3,7},{5,1},{7,3},{8,12},{10,14},{12... | collective-permute-start | bytes 196616 | tf_op jit(solution)/shard_map/ppermute | solution.py:17
  128.7 6.2 %collective-permute-start.20 = (bf16[2,128,128]{2,1,0:T(8,128)(2,1)}, bf16[2,128,128]{2,1,0:T(8,128)(2,1)S(1)}, u32[]{:S(2)}, u32[]{:S(2)}) collective-permute-start(bf16[2,128,128]{2,1,0:T(8,128)(2,1)} %get-tuple-element.26), channel_id=1, source_target_pairs={{0,2},{2,0},{4,6},{6,4},{1,3},{3,1},{5,7},{7,5},{8,10},{10,8},{12,... | collective-permute-start | bytes 196616 | tf_op jit(solution)/shard_map/ppermute | solution.py:17
  131.6 7.7 %collective-permute-start.26 = (bf16[128,128]{0,1:T(8,128)(2,1)S(1)}, bf16[128,128]{0,1:T(8,128)(2,1)S(1)}, u32[]{:S(2)}, u32[]{:S(2)}) collective-permute-start(bf16[128,128]{0,1:T(8,128)(2,1)S(1)} %fusion.14), channel_id=1, source_target_pairs={{0,1},{1,0},{2,3},{3,2},{4,5},{5,4},{6,7},{7,6},{8,9},{9,8},{10,11... | collective-permute-start | bytes 98312 | tf_op jit(solution)/shard_map/ppermute | solution.py:17
  135.7 6.3 %collective-permute-start.25 = (bf16[2,128,128]{2,1,0:T(8,128)(2,1)S(1)}, bf16[2,128,128]{2,1,0:T(8,128)(2,1)S(1)}, u32[]{:S(2)}, u32[]{:S(2)}) collective-permute-start(bf16[2,128,128]{2,1,0:T(8,128)(2,1)S(1)} %add_convert_fusion), channel_id=1, source_target_pairs={{0,24},{8,16},{16,8},{24,0},{1,25},{9,17},{17,9},{25,1},{2,26},{10... | collective-permute-start | bytes 196616 | tf_op jit(solution)/shard_map/ppermute | solution.py:17
  137.7 6.1 %collective-permute-start.24 = (bf16[2,128,128]{2,1,0:T(8,128)(2,1)S(1)}, bf16[2,128,128]{2,1,0:T(8,128)(2,1)S(1)}, u32[]{:S(2)}, u32[]{:S(2)}) collective-permute-start(bf16[2,128,128]{2,1,0:T(8,128)(2,1)S(1)} %add_convert_fusion), channel_id=1, source_target_pairs={{0,16},{8,24},{16,0},{24,8},{1,17},{9,25},{17,1},{25,9},{2,18},{10... | collective-permute-start | bytes 196616 | tf_op jit(solution)/shard_map/ppermute | solution.py:17
  139.2 6.6 %collective-permute-start.23 = (bf16[2,128,128]{2,1,0:T(8,128)(2,1)S(1)}, bf16[2,128,128]{2,1,0:T(8,128)(2,1)S(1)}, u32[]{:S(2)}, u32[]{:S(2)}) collective-permute-start(bf16[2,128,128]{2,1,0:T(8,128)(2,1)S(1)} %add_convert_fusion), channel_id=1, source_target_pairs={{0,8},{8,0},{16,24},{24,16},{1,9},{9,1},{17,25},{25,17},{2,10},{10... | collective-permute-start | bytes 196616 | tf_op jit(solution)/shard_map/ppermute | solution.py:17
  139.3 6.8 %collective-permute-start.29 = (bf16[2,128,128]{1,2,0:T(8,128)(2,1)S(1)}, bf16[2,128,128]{1,2,0:T(8,128)(2,1)S(1)}, u32[]{:S(2)}, u32[]{:S(2)}) collective-permute-start(bf16[2,128,128]{1,2,0:T(8,128)(2,1)S(1)} %get-tuple-element.35), channel_id=1, source_target_pairs={{0,6},{2,4},{4,2},{6,0},{1,7},{3,5},{5,3},{7,1},{8,14},{10,12},{12... | collective-permute-start | bytes 196616 | tf_op jit(solution)/shard_map/ppermute | solution.py:17
  141.4 16.1 %collective-permute-start.28 = (bf16[2,128,128]{1,2,0:T(8,128)(2,1)S(1)}, bf16[2,128,128]{1,2,0:T(8,128)(2,1)S(1)}, u32[]{:S(2)}, u32[]{:S(2)}) collective-permute-start(bf16[2,128,128]{1,2,0:T(8,128)(2,1)S(1)} %get-tuple-element.35), channel_id=1, source_target_pairs={{0,4},{2,6},{4,0},{6,2},{1,5},{3,7},{5,1},{7,3},{8,12},{10,14},{12... | collective-permute-start | bytes 196616 | tf_op jit(solution)/shard_map/ppermute | solution.py:17
  142.0 15.5 %collective-permute-start.27 = (bf16[2,128,128]{1,2,0:T(8,128)(2,1)S(1)}, bf16[2,128,128]{1,2,0:T(8,128)(2,1)S(1)}, u32[]{:S(2)}, u32[]{:S(2)}) collective-permute-start(bf16[2,128,128]{1,2,0:T(8,128)(2,1)S(1)} %get-tuple-element.35), channel_id=1, source_target_pairs={{0,2},{2,0},{4,6},{6,4},{1,3},{3,1},{5,7},{7,5},{8,10},{10,8},{12,... | collective-permute-start | bytes 196616 | tf_op jit(solution)/shard_map/ppermute | solution.py:17
  143.8 14.8 %collective-permute-start.19 = (bf16[8,128,128]{2,1,0:T(8,128)(2,1)}, bf16[8,128,128]{2,1,0:T(8,128)(2,1)S(1)}, u32[]{:S(2)}, u32[]{:S(2)}) collective-permute-start(bf16[8,128,128]{2,1,0:T(8,128)(2,1)} %get-tuple-element.24), channel_id=1, source_target_pairs={{0,6},{2,4},{4,2},{6,0},{1,7},{3,5},{5,3},{7,1},{8,14},{10,12},{12... | collective-permute-start | bytes 786440 | tf_op jit(solution)/shard_map/ppermute | solution.py:17
  145.8 22.8 %collective-permute-start.18 = (bf16[8,128,128]{2,1,0:T(8,128)(2,1)}, bf16[8,128,128]{2,1,0:T(8,128)(2,1)S(1)}, u32[]{:S(2)}, u32[]{:S(2)}) collective-permute-start(bf16[8,128,128]{2,1,0:T(8,128)(2,1)} %get-tuple-element.23), channel_id=1, source_target_pairs={{0,4},{2,6},{4,0},{6,2},{1,5},{3,7},{5,1},{7,3},{8,12},{10,14},{12... | collective-permute-start | bytes 786440 | tf_op jit(solution)/shard_map/ppermute | solution.py:17
  146.1 22.5 %collective-permute-start.17 = (bf16[8,128,128]{2,1,0:T(8,128)(2,1)}, bf16[8,128,128]{2,1,0:T(8,128)(2,1)S(1)}, u32[]{:S(2)}, u32[]{:S(2)}) collective-permute-start(bf16[8,128,128]{2,1,0:T(8,128)(2,1)} %get-tuple-element.22), channel_id=1, source_target_pairs={{0,2},{2,0},{4,6},{6,4},{1,3},{3,1},{5,7},{7,5},{8,10},{10,8},{12,... | collective-permute-start | bytes 786440 | tf_op jit(solution)/shard_map/ppermute | solution.py:17
  (16 other events, 471.2 us)

commit v2 on v1

--- a/solution.py
+++ b/solution.py
@@ -52,35 +52,36 @@
     height, width = own.shape[0], own.shape[1]
     here, chip, core = lax.axis_index(ROW), lax.axis_index(CHIP), lax.axis_index(CORE)
     pieces, refs = refs[:group_rows], refs[group_rows:]
-    whole, sends, (inverse, panels, sems) = refs[0], refs[1:nodes], refs[nodes:]
+    whole, inverse, panels, sems = refs
     per_row, tile = panels.shape[1], panels.shape[2]
     copies = load_inverse(own, sibling, inverse, sems) + load_panels(pieces, panels, sems, here)
     for copy in copies:
         copy.wait()
-    for t in range(nodes):
-        at = chip ^ t
+    for at in range(nodes):
         node = 2 * at + core
         cols = [rows_one[node, chip * per_row + n] - chip * 2 * width for n in range(per_row)]
         stacked = panels[at].reshape(per_row * tile, tile)
         for m in range(per_row):
             row = rows_one[node, here * per_row + m] - here * height
-            part = jnp.dot(
+            whole[at, m] = jnp.dot(
                 block_row(inverse, row, cols, core, width), stacked, preferred_element_type=F32
             ).astype(BF16)
-            whole[t, m] = part
-            if t:
-                sends[t - 1][m] = part
 
 
 def level_two_kernel(
-    nodes, group_rows, rows_one, parent_two, order_two, own, sibling, ours, theirs, *refs
+    nodes, group_rows, choices, rows_one, parent_two, order_two, own, sibling, ours, theirs, *refs
 ):
     height, width = own.shape[0], own.shape[1]
     here, chip, core = lax.axis_index(ROW), lax.axis_index(CHIP), lax.axis_index(CORE)
     pieces, refs = refs[:group_rows], refs[group_rows:]
-    factors, refs = refs[:nodes], refs[nodes:]
+    inputs, refs = refs[: sum(choices)], refs[sum(choices) :]
     columns, smalls, refs = refs[:nodes], refs[nodes : 2 * nodes], refs[2 * nodes :]
     inverse, panels, near, sems = refs
+    is_end = jnp.logical_or(chip == 0, chip == nodes - 1)
+    factors = []
+    for count in choices:
+        factors.append(inputs[:count])
+        inputs = inputs[count:]
     per_row, tile = panels.shape[1], panels.shape[2]
     copies = load_inverse(own, sibling, inverse, sems) + load_panels(pieces, panels, sems, here)
     for copy in copies:
@@ -90,13 +91,16 @@
         node = 2 * at + core
         parent = parent_two[node]
         is_ours = parent % 2 == core
-        parent_at = (parent // 2) ^ chip
+        parent_at = parent // 2
         cols = [
             rows_one[parent, order_two[node, chip * per_row + n]] - chip * 2 * width
             for n in range(per_row)
         ]
         stacked = panels[at].reshape(per_row * tile, tile)
-        link = factors[t][per_row]
+        factor = factors[t][0][...]
+        if len(factors[t]) > 1:
+            factor = jnp.where(is_end, factors[t][1][...], factor)
+        link = factor[per_row]
         for m in range(per_row):
             place = order_two[node, here * per_row + m]
             row = rows_one[parent, place] - here * height
@@ -107,7 +111,7 @@
                 block_row(inverse, row, cols, core, width), stacked, preferred_element_type=F32
             ) - jnp.dot(near_tile, link, preferred_element_type=F32)
             columns[t][m] = part.astype(BF16)
-        factor = factors[t][:per_row].reshape(per_row * tile, tile)
+        factor = factor[:per_row].reshape(per_row * tile, tile)
         contract = (((0,), (0,)), ((), ()))
         smalls[t][0] = lax.dot_general(
             near[...].reshape(per_row * tile, tile), factor, contract, preferred_element_type=F32
@@ -132,10 +136,9 @@
     flops = 2 * nodes * per_row * per_row * tile**3
     return pl.pallas_call(
         functools.partial(level_one_kernel, nodes, count),
-        out_shape=[jax.ShapeDtypeStruct((nodes, per_row, tile, tile), BF16)]
-        + [jax.ShapeDtypeStruct((per_row, tile, tile), BF16)] * (nodes - 1),
+        out_shape=jax.ShapeDtypeStruct((nodes, per_row, tile, tile), BF16),
         in_specs=[SMEM, ANY, ANY] + [ANY] * count,
-        out_specs=[VMEM] * nodes,
+        out_specs=VMEM,
         scratch_shapes=[
             pltpu.VMEM((2,) + own.shape, BF16),
             pltpu.VMEM((nodes, per_row, tile, tile), BF16),
@@ -153,10 +156,10 @@
     per_row = group * count
     flops = 2 * nodes * per_row * (per_row + 3) * tile**3
     return pl.pallas_call(
-        functools.partial(level_two_kernel, nodes, count),
+        functools.partial(level_two_kernel, nodes, count, [len(f) for f in factors]),
         out_shape=[jax.ShapeDtypeStruct((per_row, tile, tile), BF16)] * nodes
         + [jax.ShapeDtypeStruct((2, tile, tile), BF16)] * nodes,
-        in_specs=[SMEM] * 3 + [ANY, ANY, VMEM, VMEM] + [ANY] * count + [VMEM] * nodes,
+        in_specs=[SMEM] * 3 + [ANY, ANY, VMEM, VMEM] + [ANY] * count + [VMEM] * sum(len(f) for f in factors),
         out_specs=[VMEM] * (2 * nodes),
         scratch_shapes=[
             pltpu.VMEM((2,) + own.shape, BF16),
@@ -167,15 +170,24 @@
         compiler_params=pltpu.CompilerParams(vmem_limit_bytes=56 << 20),
         cost_estimate=pl.CostEstimate(flops=flops, bytes_accessed=16 << 20, transcendentals=0),
         name="level_two",
-    )(rows_one, parent_two, order_two, own, sibling, ours, theirs, *pieces, *factors)
-
-
-def distribute(panel):
-    rows = lax.axis_size(ROW)
-    quarters = panel.reshape((rows, panel.shape[0] // rows) + panel.shape[1:])
-    quarters = lax.all_to_all(quarters, ROW, 0, 0, tiled=True)
-    quarters = lax.all_to_all(quarters, CHIP, 0, 0, tiled=True)
-    return spread(quarters, ROW)
+    )(rows_one, parent_two, order_two, own, sibling, ours, theirs, *pieces, *sum(factors, []))
+
+
+def after(x, *others):
+    return lax.optimization_barrier((x,) + others)[0]
+
+
+def halves(panel, axis):
+    rows = lax.axis_size(axis)
+    return panel.reshape((rows, panel.shape[0] // rows) + panel.shape[1:])
+
+
+def send(x, axis, pairs):
+    return lax.ppermute(x, axis, pairs)
+
+
+def swap(blocks, axis):
+    return lax.all_to_all(blocks, axis, 0, 0, tiled=True)
 
 
 def total(parts):
@@ -186,28 +198,71 @@
     inverse_top, rows_one, panel_one, base_one, parent_two, order_two, panel_two, link_two, base_two
 ):
     chip, core = lax.axis_index(CHIP), lax.axis_index(CORE)
+    nodes = lax.axis_size(CHIP)
+    line = nodes == 4
+    payload = jnp.concatenate([panel_two[0], link_two], axis=0)
+    near = exchange(payload, CHIP, 1)
+    if line:
+        inner = send(payload, CHIP, [(1, 2), (2, 1)])
+    else:
+        inner = [exchange(payload, CHIP, t) for t in range(2, nodes)]
     sibling = exchange(inverse_top, CORE, 1)
-    pieces_one = distribute(panel_one[0])
-    pieces_two = distribute(panel_two[0])
-    factors = spread(jnp.concatenate([panel_two[0], link_two], axis=0), CHIP)
-    ours, *sends = level_one(rows_one, inverse_top, sibling, pieces_one)
-    theirs = exchange(ours, CORE, 1)
-    parts_one = [ours[0]] + [exchange(send, CHIP, t + 1) for t, send in enumerate(sends)]
+    both = jnp.concatenate([halves(panel_one[0], ROW), halves(panel_two[0], ROW)], axis=1)
+    quarters = swap(both, ROW)
+    quarters, near, inner = lax.optimization_barrier((quarters, near, inner))
+    group = quarters.shape[1] // 2
+    blocks_one = swap(quarters[:, :group], CHIP)
+    pieces_one = spread(blocks_one, ROW)
+    quarters_two, near_late, inner_late, blocks_one = lax.optimization_barrier(
+        (quarters[:, group:], near, inner, blocks_one)
+    )
+    blocks_two = swap(quarters_two, CHIP)
+    over = out_one = ()
+    if line:
+        over = send(near_late, CHIP, [(1, 2), (2, 1)])
+        out_one = send(inner_late, CHIP, [(1, 0), (2, 3)])
+    pieces_one = lax.optimization_barrier(pieces_one)
+    pieces_one, blocks_two, over, out_one = lax.optimization_barrier(
+        (pieces_one, blocks_two, over, out_one)
+    )
+    out_two = send(over, CHIP, [(1, 0), (2, 3)]) if line else ()
+    pieces_two = spread(blocks_two, ROW)
+    ours = level_one(rows_one, inverse_top, sibling, pieces_one)
+    ours, out_two, pieces_two = lax.optimization_barrier((ours, out_two, pieces_two))
+    ours_too = ours
+    theirs = exchange(ours_too, CORE, 1)
+    parts_one = swap(ours, CHIP)
+    if line:
+        factors = [[payload], [near], [over, out_one], [inner, out_two]]
+    else:
+        factors = [[f] for f in [payload, near, *inner]]
     outs = level_two(
         rows_one, parent_two, order_two, inverse_top, sibling, ours, theirs, pieces_two, factors
     )
-    nodes = len(outs) // 2
-    parts_two = [outs[0]] + [exchange(outs[t], CHIP, t) for t in range(1, nodes)]
-    parts_small = [outs[nodes]] + [exchange(outs[nodes + t], CHIP, t) for t in range(1, nodes)]
-    column_one = (-total(parts_one)).astype(BF16)
-    column_two = (-total(parts_two)).astype(BF16)
-    sums = total(spread(total(parts_small).astype(BF16), ROW))
+    columns, smalls = outs[:nodes], outs[nodes:]
+    parts_small = [smalls[0]] + [exchange(smalls[t], CHIP, t) for t in range(1, nodes)]
+    columns, parts_small = lax.optimization_barrier((columns, parts_small))
+    column_one = (-jnp.sum(parts_one.astype(F32), axis=0)).astype(BF16)
     part = jnp.einsum("mij,mil->jl", panel_one[0], column_one, preferred_element_type=F32)
-    diagonal_one = (base_one[0] - total(spread(part.astype(BF16), ROW))).astype(BF16)
-    pair = jnp.stack([diagonal_one, exchange(diagonal_one, CORE, 1)])
-    diagonals = jnp.stack(spread(pair, CHIP))
+    base = jnp.where(lax.axis_index(ROW) == 0, base_one[0], 0)
+    share = (base - part).astype(BF16)
+    first = [exchange(columns[t], CHIP, t) for t in range(nodes // 2 + 1, nodes)]
+    pair = jnp.stack([share, exchange(share, CORE, 1)])
+    last, pair = lax.optimization_barrier((columns[1 : nodes // 2 + 1], pair))
+    shares = spread(pair, CHIP)
+    shares, first = lax.optimization_barrier((shares, first))
+    shares = jnp.stack(shares)
+    last = [exchange(last[t - 1], CHIP, t) for t in range(1, nodes // 2 + 1)]
     parent = parent_two[2 * chip + core]
-    near_diagonal = diagonals[(parent // 2) ^ chip, (parent % 2) ^ core]
+    parent_share = shares[(parent // 2) ^ chip, (parent % 2) ^ core]
+    small = jnp.concatenate(
+        [total(parts_small).astype(BF16), share[None], parent_share[None]], axis=0
+    )
+    sums, last = lax.optimization_barrier((spread(small, ROW), last))
+    sums = total(sums)
+    column_two = (-total([columns[0], *first, *last])).astype(BF16)
+    diagonal_one = sums[2].astype(BF16)
+    near_diagonal = sums[3].astype(BF16)
     link = link_two[0]
     upper = (sums[0] - jnp.dot(near_diagonal, link, preferred_element_type=F32)).astype(BF16)
     link_term = jnp.einsum("ij,il->jl", link, upper, preferred_element_type=F32)

time: 171 us -> 140 us (0.82)
  waiting for transfers between devices: 73.1 us -> 42.9 us
  blocking collectives: 23.8 us -> 15 us
  starting transfers between devices: 44.5 us -> 48.7 us
    ppermute x30 -> x22, waiting for transfers between devices: 73.1 us -> 33.8 us  [exchange(): return lax.ppermute(x, axis, [(i, i ^ step) for i in range(size)])]
    all_to_all x2 -> x3, waiting for transfers between devices: 0.01 us -> 9.13 us  [swap(): return lax.all_to_all(blocks, axis, 0, 0, tiled=True)]
    all_to_all x2 -> x1, blocking collectives: 23.8 us -> 15 us  [swap(): return lax.all_to_all(blocks, axis, 0, 0, tiled=True)]
    all_to_all x2 -> x3, starting transfers between devices: 9.4 us -> 13.9 us  [swap(): return lax.all_to_all(blocks, axis, 0, 0, tiled=True)]
    ppermute x30 -> x22, starting transfers between devices: 35.1 us -> 30.9 us  [exchange(): return lax.ppermute(x, axis, [(i, i ^ step) for i in range(size)])]
    ppermute x0 -> x4, starting transfers between devices: none -> 3.93 us  [send(): return lax.ppermute(x, axis, pairs)]
    concatenate x1 -> x3, other arithmetic: 1.05 us -> 2.89 us  [the longest x1 1.88 us: local(): jnp.concatenate([halves(panel_one[0], ROW), halves(panel_two[0], ROW)], a...]
  transfers between devices with their start and end apart: 32 -> 29, of which waited for: 10 -> 12; matrix products, arithmetic and copies ran while one was open for 4% -> 5% of each run, Pallas kernels for 9% -> 13%
where the time goes in v2:
time: 140 us; the launch traced here: 139 us
  starting transfers between devices  48.7 us (35%)
  waiting for transfers between devices  42.9 us (31%)
  Pallas kernels  17.4 us (12%)
  blocking collectives  15 us (11%)
  other arithmetic  5.66 us (4%)
  local copies, waits for them, and re-layouts  4.54 us (3%)
  between operations  3.62 us (3%)
    ppermute x22, waiting for transfers between devices, exchange(): return lax.ppermute(x, axis, [(i, i ^ step) for i in range(size)])  33.8 us
    ppermute x22, starting transfers between devices, exchange(): return lax.ppermute(x, axis, [(i, i ^ step) for i in range(size)])  30.9 us
    all_to_all x1, blocking collectives, swap(): return lax.all_to_all(blocks, axis, 0, 0, tiled=True)  15 us
    all_to_all x3, starting transfers between devices, swap(): return lax.all_to_all(blocks, axis, 0, 0, tiled=True)  13.9 us
    pallas_call x1, Pallas kernels, level_two(): pl.pallas_call(functools.partial(level_two_kernel, nodes, count, [len(f)...  9.91 us
    all_to_all x3, waiting for transfers between devices, swap(): return lax.all_to_all(blocks, axis, 0, 0, tiled=True)  9.13 us
    pallas_call x1, Pallas kernels, level_one(): pl.pallas_call(functools.partial(level_one_kernel, nodes, count), out_sha...  7.51 us
    ppermute x4, starting transfers between devices, send(): return lax.ppermute(x, axis, pairs)  3.93 us
  transfers between devices with their start and end apart: 29, of which 12 were waited for; matrix products, arithmetic and copies ran while one was open for 5% of the time, Pallas kernels for 13%

profile of v2, /device:TPU:0, one launch (start us, length us, event | category | flops | bytes accessed | tf_op | source)
XLA Modules:
  0.0 139.1 jit_solution(12796048373274150884)
XLA Ops:
  1.2 1.9 %pad_maximum_fusion = bf16[4,4,128,128]{3,2,1,0:T(8,128)(2,1)} fusion(bf16[4,2,128,128]{3,2,1,0:T(8,128)(2,1)} %bitcast.62, bf16[4,2,128,128]{3,2,1,0:T(8,128)(2,1)} %bitcast.61), kind=kLoop, calls=%fused_computation.11 | loop fusion | flops 262144 | bytes 1048576 | tf_op jit(solution)/shard_map/concatenate | solution.py:210
  3.0 4.7 %all-to-all-start = ((bf16[4,4,128,128]{3,2,1,0:T(8,128)(2,1)}), bf16[4,4,128,128]{3,2,1,0:T(8,128)(2,1)S(1)}, u32[]{:S(2)}, u32[]{:S(2)}) async-start(bf16[4,4,128,128]{3,2,1,0:T(8,128)(2,1)} %pad_maximum_fusion), calls=%async_computation | async-start | bytes 1048576 | tf_op jit(solution)/shard_map/all_to_all | solution.py:190
  8.8 1.6 %collective-permute-start.1 = (bf16[9,128,128]{2,1,0:T(8,128)(2,1)S(1)}, bf16[9,128,128]{2,1,0:T(8,128)(2,1)S(1)}, u32[]{:S(2)}, u32[]{:S(2)}) collective-permute-start(bf16[9,128,128]{2,1,0:T(8,128)(2,1)S(1)} %pad_maximum_fusion.1.refs_4_), channel_id=1, source_target_pairs={{0,2},{2,0},{4,6},{6,4},{1,3},{3,1},{5,7},{7,5},{8,10},{10,8},{12,... | collective-permute-start | bytes 884744 | tf_op jit(solution)/shard_map/ppermute | solution.py:17
  11.1 6.9 %collective-permute-done.1.refs_5_ = bf16[9,128,128]{2,1,0:T(8,128)(2,1)S(1)} collective-permute-done((bf16[9,128,128]{2,1,0:T(8,128)(2,1)S(1)}, bf16[9,128,128]{2,1,0:T(8,128)(2,1)S(1)}, u32[]{:S(2)}, u32[]{:S(2)}) %collective-permute-start.1) | collective-permute-done | bytes 294944 | tf_op jit(solution)/shard_map/ppermute | solution.py:17
  18.8 15.0 %all_to_all.20.refs_0_ = bf16[4,2,128,128]{3,2,1,0:T(8,128)(2,1)S(1)} all-to-all(bf16[4,2,128,128]{3,2,1,0:T(8,128)(2,1)S(1)} %get-tuple-element.114), channel_id=1, replica_groups=mesh['prow'=4,'pchip'=4,'pcore'=2] {'pchip'}, dimensions={0} | all-to-all | bytes 524288 | tf_op jit(solution)/shard_map/all_to_all | solution.py:190
  33.8 1.4 collective-permute-start.3
  35.2 3.4 %all-to-all-start.2 = ((bf16[4,2,128,128]{3,2,1,0:T(8,128)(2,1)}), bf16[4,2,128,128]{3,2,1,0:T(8,128)(2,1)S(1)}, u32[]{:S(2)}, u32[]{:S(2)}) async-start(bf16[4,2,128,128]{3,2,1,0:T(8,128)(2,1)} %get-tuple-element.65), calls=%async_computation.2 | async-start | bytes 524288 | tf_op jit(solution)/shard_map/all_to_all | solution.py:190
  39.3 1.3 collective-permute-start.7
  40.6 1.5 %collective-permute-start.4 = (bf16[4,2,128,128]{3,2,1,0:T(8,128)(2,1)S(1)}, bf16[4,2,128,128]{3,2,1,0:T(8,128)(2,1)S(1)}, u32[]{:S(2)}, u32[]{:S(2)}) collective-permute-start(bf16[4,2,128,128]{3,2,1,0:T(8,128)(2,1)S(1)} %all_to_all.20.refs_0_), channel_id=1, source_target_pairs={{0,16},{8,24},{16,0},{24,8},{1,17},{9,25},{17,1},{25,9},{2,18},{10... | collective-permute-start | bytes 786440 | tf_op jit(solution)/shard_map/ppermute | solution.py:17
  42.7 9.2 %collective-permute-done.4.refs_2_ = bf16[4,2,128,128]{3,2,1,0:T(8,128)(2,1)S(1)} collective-permute-done((bf16[4,2,128,128]{3,2,1,0:T(8,128)(2,1)S(1)}, bf16[4,2,128,128]{3,2,1,0:T(8,128)(2,1)S(1)}, u32[]{:S(2)}, u32[]{:S(2)}) %collective-permute-start.4) | collective-permute-done | bytes 262176 | tf_op jit(solution)/shard_map/ppermute | solution.py:17
  52.0 1.3 collective-permute-start.8
  53.3 1.8 %collective-permute-start.10 = (bf16[4,2,128,128]{3,2,1,0:T(8,128)(2,1)S(1)}, bf16[4,2,128,128]{3,2,1,0:T(8,128)(2,1)S(1)}, u32[]{:S(2)}, u32[]{:S(2)}) collective-permute-start(bf16[4,2,128,128]{3,2,1,0:T(8,128)(2,1)S(1)} %all-to-all-done.2.refs_0_), channel_id=1, source_target_pairs={{0,16},{8,24},{16,0},{24,8},{1,17},{9,25},{17,1},{25,9},{2,18},{10... | collective-permute-start | bytes 786440 | tf_op jit(solution)/shard_map/ppermute | solution.py:17
  56.9 7.5 %level_one.1.ours = bf16[4,8,128,128]{3,2,1,0:T(8,128)(2,1)} custom-call(s32[8,32]{1,0:T(8,128)S(1)} %copy-done, bf16[16,8,128,128]{3,2,1,0:T(8,128)(2,1)} %own.3, bf16[16,8,128,128]{3,2,1,0:T(8,128)(2,1)} %collective-permute-done.sibling, bf16[4,2,128,128]{3,2,1,0:T(8,128)(2,1)S(1)} %all_to_all.20.refs_0_, ...), custom_call_target="tpu_custom_call" | custom-call | flops 1073741824 | bytes 12582912 | tf_op jit(solution)/shard_map/level_one/pallas_call | solution.py:137
  64.5 1.7 %collective-permute-done.10.refs_2_ = bf16[4,2,128,128]{3,2,1,0:T(8,128)(2,1)S(1)} collective-permute-done((bf16[4,2,128,128]{3,2,1,0:T(8,128)(2,1)S(1)}, bf16[4,2,128,128]{3,2,1,0:T(8,128)(2,1)S(1)}, u32[]{:S(2)}, u32[]{:S(2)}) %collective-permute-start.10) | collective-permute-done | bytes 262176 | tf_op jit(solution)/shard_map/ppermute | solution.py:17
  66.2 1.3 collective-permute-done.9.refs_1_
  68.9 5.7 %all-to-all-start.3 = ((bf16[4,8,128,128]{3,2,1,0:T(8,128)(2,1)}), bf16[4,8,128,128]{3,2,1,0:T(8,128)(2,1)S(1)}, u32[]{:S(2)}, u32[]{:S(2)}) async-start(bf16[4,8,128,128]{3,2,1,0:T(8,128)(2,1)} %level_one.1.ours), calls=%async_computation.3 | async-start | bytes 2097152 | tf_op jit(solution)/shard_map/all_to_all | solution.py:190
  74.7 2.8 %collective-permute-done.12.theirs = bf16[4,8,128,128]{3,2,1,0:T(8,128)(2,1)S(1)} collective-permute-done((bf16[4,8,128,128]{3,2,1,0:T(8,128)(2,1)}, bf16[4,8,128,128]{3,2,1,0:T(8,128)(2,1)S(1)}, u32[]{:S(2)}, u32[]{:S(2)}) %collective-permute-start.12) | collective-permute-done | bytes 1048608 | tf_op jit(solution)/shard_map/ppermute | solution.py:17
  78.5 9.9 %level_two.1 = (bf16[8,128,128]{2,1,0:T(8,128)(2,1)}, bf16[8,128,128]{2,1,0:T(8,128)(2,1)}, bf16[8,128,128]{2,1,0:T(8,128)(2,1)}, bf16[8,128,128]{2,1,0:T(8,128)...) custom-call(s32[8,32]{1,0:T(8,128)} %rows_one.3, ...), custom_call_target="tpu_custom_call" | custom-call | flops 1476395008 | bytes 16777216 | tf_op jit(solution)/shard_map/level_two/pallas_call | solution.py:158
  88.5 2.1 %collective-permute-start.13 = (bf16[2,128,128]{2,1,0:T(8,128)(2,1)}, bf16[2,128,128]{2,1,0:T(8,128)(2,1)S(1)}, u32[]{:S(2)}, u32[]{:S(2)}) collective-permute-start(bf16[2,128,128]{2,1,0:T(8,128)(2,1)} %get-tuple-element.86), channel_id=1, source_target_pairs={{0,2},{2,0},{4,6},{6,4},{1,3},{3,1},{5,7},{7,5},{8,10},{10,8},{12,... | collective-permute-start | bytes 196616 | tf_op jit(solution)/shard_map/ppermute | solution.py:17
  90.6 2.4 %collective-permute-start.14 = (bf16[2,128,128]{2,1,0:T(8,128)(2,1)}, bf16[2,128,128]{2,1,0:T(8,128)(2,1)S(1)}, u32[]{:S(2)}, u32[]{:S(2)}) collective-permute-start(bf16[2,128,128]{2,1,0:T(8,128)(2,1)} %get-tuple-element.87), channel_id=1, source_target_pairs={{0,4},{2,6},{4,0},{6,2},{1,5},{3,7},{5,1},{7,3},{8,12},{10,14},{12... | collective-permute-start | bytes 196616 | tf_op jit(solution)/shard_map/ppermute | solution.py:17
  93.0 9.1 %all-to-all-done.3 = bf16[4,8,128,128]{3,2,1,0:T(8,128)(2,1)S(1)} async-done(((bf16[4,8,128,128]{3,2,1,0:T(8,128)(2,1)}), bf16[4,8,128,128]{3,2,1,0:T(8,128)(2,1)S(1)}, u32[]{:S(2)}, u32[]{:S(2)}) %all-to-all-start.3) | async-done | bytes 1048608 | tf_op jit(solution)/shard_map/all_to_all | solution.py:190
  105.9 2.5 %collective-permute-start.20 = (bf16[8,128,128]{2,1,0:T(8,128)(2,1)}, bf16[8,128,128]{2,1,0:T(8,128)(2,1)S(1)}, u32[]{:S(2)}, u32[]{:S(2)}) collective-permute-start(bf16[8,128,128]{2,1,0:T(8,128)(2,1)} %get-tuple-element.96), channel_id=1, source_target_pairs={{0,6},{2,4},{4,2},{6,0},{1,7},{3,5},{5,3},{7,1},{8,14},{10,12},{12... | collective-permute-start | bytes 786440 | tf_op jit(solution)/shard_map/ppermute | solution.py:17
  108.5 1.9 %collective-permute-start.18 = (bf16[2,128,128]{2,1,0:T(8,128)(2,1)S(1)}, bf16[2,128,128]{2,1,0:T(8,128)(2,1)S(1)}, u32[]{:S(2)}, u32[]{:S(2)}) collective-permute-start(bf16[2,128,128]{2,1,0:T(8,128)(2,1)S(1)} %pad_maximum_fusion.3), channel_id=1, source_target_pairs={{0,4},{2,6},{4,0},{6,2},{1,5},{3,7},{5,1},{7,3},{8,12},{10,14},{12... | collective-permute-start | bytes 196616 | tf_op jit(solution)/shard_map/ppermute | solution.py:17
  110.5 2.4 %collective-permute-start.19 = (bf16[2,128,128]{2,1,0:T(8,128)(2,1)S(1)}, bf16[2,128,128]{2,1,0:T(8,128)(2,1)S(1)}, u32[]{:S(2)}, u32[]{:S(2)}) collective-permute-start(bf16[2,128,128]{2,1,0:T(8,128)(2,1)S(1)} %pad_maximum_fusion.3), channel_id=1, source_target_pairs={{0,6},{2,4},{4,2},{6,0},{1,7},{3,5},{5,3},{7,1},{8,14},{10,12},{12... | collective-permute-start | bytes 196616 | tf_op jit(solution)/shard_map/ppermute | solution.py:17
  113.9 3.3 %collective-permute-done.20 = bf16[8,128,128]{2,1,0:T(8,128)(2,1)S(1)} collective-permute-done((bf16[8,128,128]{2,1,0:T(8,128)(2,1)}, bf16[8,128,128]{2,1,0:T(8,128)(2,1)S(1)}, u32[]{:S(2)}, u32[]{:S(2)}) %collective-permute-start.20) | collective-permute-done | bytes 262176 | tf_op jit(solution)/shard_map/ppermute | solution.py:17
  117.2 6.2 %collective-permute-start.25 = (bf16[8,128,128]{2,1,0:T(8,128)(2,1)}, bf16[8,128,128]{2,1,0:T(8,128)(2,1)S(1)}, u32[]{:S(2)}, u32[]{:S(2)}) collective-permute-start(bf16[8,128,128]{2,1,0:T(8,128)(2,1)} %get-tuple-element.102), channel_id=1, source_target_pairs={{0,4},{2,6},{4,0},{6,2},{1,5},{3,7},{5,1},{7,3},{8,12},{10,14},{12... | collective-permute-start | bytes 786440 | tf_op jit(solution)/shard_map/ppermute | solution.py:17
  124.4 1.3 collective-permute-start.21
  126.8 1.4 collective-permute-start.23
  129.0 1.5 %collective-permute-done.21 = bf16[4,128,128]{2,1,0:T(8,128)(2,1)S(1)} collective-permute-done((bf16[4,128,128]{2,1,0:T(8,128)(2,1)S(1)}, bf16[4,128,128]{2,1,0:T(8,128)(2,1)S(1)}, u32[]{:S(2)}, u32[]{:S(2)}) %collective-permute-start.21) | collective-permute-done | bytes 131104 | tf_op jit(solution)/shard_map/ppermute | solution.py:17
  130.5 1.6 %collective-permute-done.22 = bf16[4,128,128]{2,1,0:T(8,128)(2,1)S(1)} collective-permute-done((bf16[4,128,128]{2,1,0:T(8,128)(2,1)S(1)}, bf16[4,128,128]{2,1,0:T(8,128)(2,1)S(1)}, u32[]{:S(2)}, u32[]{:S(2)}) %collective-permute-start.22) | collective-permute-done | bytes 131104 | tf_op jit(solution)/shard_map/ppermute | solution.py:17
  132.1 1.6 %collective-permute-done.23 = bf16[4,128,128]{2,1,0:T(8,128)(2,1)S(1)} collective-permute-done((bf16[4,128,128]{2,1,0:T(8,128)(2,1)S(1)}, bf16[4,128,128]{2,1,0:T(8,128)(2,1)S(1)}, u32[]{:S(2)}, u32[]{:S(2)}) %collective-permute-start.23) | collective-permute-done | bytes 131104 | tf_op jit(solution)/shard_map/ppermute | solution.py:17
  133.7 2.8 %collective-permute-done.25 = bf16[8,128,128]{2,1,0:T(8,128)(2,1)S(1)} collective-permute-done((bf16[8,128,128]{2,1,0:T(8,128)(2,1)}, bf16[8,128,128]{2,1,0:T(8,128)(2,1)S(1)}, u32[]{:S(2)}, u32[]{:S(2)}) %collective-permute-start.25) | collective-permute-done | bytes 262176 | tf_op jit(solution)/shard_map/ppermute | solution.py:17
  (83 shorter events, 16.2 us)
Async XLA Ops:
  0.6 56.3 %copy-start = (s32[8,32]{1,0:T(8,128)S(1)}, s32[8,32]{1,0:T(8,128)}, u32[]{:S(2)}) copy-start(s32[8,32]{1,0:T(8,128)} %rows_one.3) | copy-start | bytes 3076
  0.6 56.2 %collective-permute-start = (bf16[16,8,128,128]{3,2,1,0:T(8,128)(2,1)}, bf16[16,8,128,128]{3,2,1,0:T(8,128)(2,1)}, u32[]{:S(2)}, u32[]{:S(2)}) collective-permute-start(bf16[16,8,128,128]{3,2,1,0:T(8,128)(2,1)} %own.3), channel_id=1, source_target_pairs={{0,1},{1,0},{2,3},{3,2},{4,5},{5,4},{6,7},{7,6},{8,9},{9,8},{10,11... | collective-permute-start | bytes 12582920 | tf_op jit(solution)/shard_map/ppermute | solution.py:17
  3.0 14.9 %all-to-all-start = ((bf16[4,4,128,128]{3,2,1,0:T(8,128)(2,1)}), bf16[4,4,128,128]{3,2,1,0:T(8,128)(2,1)S(1)}, u32[]{:S(2)}, u32[]{:S(2)}) async-start(bf16[4,4,128,128]{3,2,1,0:T(8,128)(2,1)} %pad_maximum_fusion), calls=%async_computation | async-start | bytes 1048576 | tf_op jit(solution)/shard_map/all_to_all | solution.py:190
  8.8 55.6 %copy-start.1 = (bf16[9,128,128]{2,1,0:T(8,128)(2,1)}, bf16[9,128,128]{2,1,0:T(8,128)(2,1)S(1)}, u32[]{:S(2)}) copy-start(bf16[9,128,128]{2,1,0:T(8,128)(2,1)S(1)} %pad_maximum_fusion.1.refs_4_) | copy-start | bytes 884740
  8.8 9.2 %collective-permute-start.1 = (bf16[9,128,128]{2,1,0:T(8,128)(2,1)S(1)}, bf16[9,128,128]{2,1,0:T(8,128)(2,1)S(1)}, u32[]{:S(2)}, u32[]{:S(2)}) collective-permute-start(bf16[9,128,128]{2,1,0:T(8,128)(2,1)S(1)} %pad_maximum_fusion.1.refs_4_), channel_id=1, source_target_pairs={{0,2},{2,0},{4,6},{6,4},{1,3},{3,1},{5,7},{7,5},{8,10},{10,8},{12,... | collective-permute-start | bytes 884744 | tf_op jit(solution)/shard_map/ppermute | solution.py:17
  10.4 7.5 %collective-permute-start.2 = (bf16[9,128,128]{2,1,0:T(8,128)(2,1)S(1)}, bf16[9,128,128]{2,1,0:T(8,128)(2,1)S(1)}, u32[]{:S(2)}, u32[]{:S(2)}) collective-permute-start(bf16[9,128,128]{2,1,0:T(8,128)(2,1)S(1)} %pad_maximum_fusion.1.refs_4_), channel_id=1, source_target_pairs={{2,4},{4,2},{3,5},{5,3},{10,12},{12,10},{11,13},{13,11},{18,20},{2... | collective-permute-start | bytes 884744 | tf_op jit(solution)/shard_map/ppermute | solution.py:186
  33.8 8.3 %collective-permute-start.3 = (bf16[4,2,128,128]{3,2,1,0:T(8,128)(2,1)S(1)}, bf16[4,2,128,128]{3,2,1,0:T(8,128)(2,1)S(1)}, u32[]{:S(2)}, u32[]{:S(2)}) collective-permute-start(bf16[4,2,128,128]{3,2,1,0:T(8,128)(2,1)S(1)} %all_to_all.20.refs_0_), channel_id=1, source_target_pairs={{0,8},{8,0},{16,24},{24,16},{1,9},{9,1},{17,25},{25,17},{2,10},{10... | collective-permute-start | bytes 786440 | tf_op jit(solution)/shard_map/ppermute | solution.py:17
  35.2 16.8 %all-to-all-start.2 = ((bf16[4,2,128,128]{3,2,1,0:T(8,128)(2,1)}), bf16[4,2,128,128]{3,2,1,0:T(8,128)(2,1)S(1)}, u32[]{:S(2)}, u32[]{:S(2)}) async-start(bf16[4,2,128,128]{3,2,1,0:T(8,128)(2,1)} %get-tuple-element.65), calls=%async_computation.2 | async-start | bytes 524288 | tf_op jit(solution)/shard_map/all_to_all | solution.py:190
  38.6 13.4 %collective-permute-start.6 = (bf16[9,128,128]{2,1,0:T(8,128)(2,1)S(1)}, bf16[9,128,128]{2,1,0:T(8,128)(2,1)S(1)}, u32[]{:S(2)}, u32[]{:S(2)}) collective-permute-start(bf16[9,128,128]{2,1,0:T(8,128)(2,1)S(1)} %collective-permute-done.1.refs_5_), channel_id=1, source_target_pairs={{2,4},{4,2},{3,5},{5,3},{10,12},{12,10},{11,13},{13,11},{18,20},{2... | collective-permute-start | bytes 884744 | tf_op jit(solution)/shard_map/ppermute | solution.py:186
  39.3 12.7 %collective-permute-start.7 = (bf16[9,128,128]{2,1,0:T(8,128)(2,1)S(1)}, bf16[9,128,128]{2,1,0:T(8,128)(2,1)S(1)}, u32[]{:S(2)}, u32[]{:S(2)}) collective-permute-start(bf16[9,128,128]{2,1,0:T(8,128)(2,1)S(1)} %collective-permute-done.2.refs_8_), channel_id=1, source_target_pairs={{2,0},{4,6},{3,1},{5,7},{10,8},{12,14},{11,9},{13,15},{18,16},{20,... | collective-permute-start | bytes 884744 | tf_op jit(solution)/shard_map/ppermute | solution.py:186
  40.6 11.4 %collective-permute-start.4 = (bf16[4,2,128,128]{3,2,1,0:T(8,128)(2,1)S(1)}, bf16[4,2,128,128]{3,2,1,0:T(8,128)(2,1)S(1)}, u32[]{:S(2)}, u32[]{:S(2)}) collective-permute-start(bf16[4,2,128,128]{3,2,1,0:T(8,128)(2,1)S(1)} %all_to_all.20.refs_0_), channel_id=1, source_target_pairs={{0,16},{8,24},{16,0},{24,8},{1,17},{9,25},{17,1},{25,9},{2,18},{10... | collective-permute-start | bytes 786440 | tf_op jit(solution)/shard_map/ppermute | solution.py:17
  42.1 9.9 %collective-permute-start.5 = (bf16[4,2,128,128]{3,2,1,0:T(8,128)(2,1)S(1)}, bf16[4,2,128,128]{3,2,1,0:T(8,128)(2,1)S(1)}, u32[]{:S(2)}, u32[]{:S(2)}) collective-permute-start(bf16[4,2,128,128]{3,2,1,0:T(8,128)(2,1)S(1)} %all_to_all.20.refs_0_), channel_id=1, source_target_pairs={{0,24},{8,16},{16,8},{24,0},{1,25},{9,17},{17,9},{25,1},{2,26},{10... | collective-permute-start | bytes 786440 | tf_op jit(solution)/shard_map/ppermute | solution.py:17
  52.0 16.2 %collective-permute-start.8 = (bf16[9,128,128]{2,1,0:T(8,128)(2,1)S(1)}, bf16[9,128,128]{2,1,0:T(8,128)(2,1)S(1)}, u32[]{:S(2)}, u32[]{:S(2)}) collective-permute-start(bf16[9,128,128]{2,1,0:T(8,128)(2,1)S(1)} %collective-permute-done.6.refs_6_), channel_id=1, source_target_pairs={{2,0},{4,6},{3,1},{5,7},{10,8},{12,14},{11,9},{13,15},{18,16},{20,... | collective-permute-start | bytes 884744 | tf_op jit(solution)/shard_map/ppermute | solution.py:186
  53.3 12.9 %collective-permute-start.10 = (bf16[4,2,128,128]{3,2,1,0:T(8,128)(2,1)S(1)}, bf16[4,2,128,128]{3,2,1,0:T(8,128)(2,1)S(1)}, u32[]{:S(2)}, u32[]{:S(2)}) collective-permute-start(bf16[4,2,128,128]{3,2,1,0:T(8,128)(2,1)S(1)} %all-to-all-done.2.refs_0_), channel_id=1, source_target_pairs={{0,16},{8,24},{16,0},{24,8},{1,17},{9,25},{17,1},{25,9},{2,18},{10... | collective-permute-start | bytes 786440 | tf_op jit(solution)/shard_map/ppermute | solution.py:17
  55.1 11.1 %collective-permute-start.11 = (bf16[4,2,128,128]{3,2,1,0:T(8,128)(2,1)S(1)}, bf16[4,2,128,128]{3,2,1,0:T(8,128)(2,1)S(1)}, u32[]{:S(2)}, u32[]{:S(2)}) collective-permute-start(bf16[4,2,128,128]{3,2,1,0:T(8,128)(2,1)S(1)} %all-to-all-done.2.refs_0_), channel_id=1, source_target_pairs={{0,24},{8,16},{16,8},{24,0},{1,25},{9,17},{17,9},{25,1},{2,26},{10... | collective-permute-start | bytes 786440 | tf_op jit(solution)/shard_map/ppermute | solution.py:17
  56.0 11.4 %collective-permute-start.9 = (bf16[4,2,128,128]{3,2,1,0:T(8,128)(2,1)S(1)}, bf16[4,2,128,128]{3,2,1,0:T(8,128)(2,1)S(1)}, u32[]{:S(2)}, u32[]{:S(2)}) collective-permute-start(bf16[4,2,128,128]{3,2,1,0:T(8,128)(2,1)S(1)} %all-to-all-done.2.refs_0_), channel_id=1, source_target_pairs={{0,8},{8,0},{16,24},{24,16},{1,9},{9,1},{17,25},{25,17},{2,10},{10... | collective-permute-start | bytes 786440 | tf_op jit(solution)/shard_map/ppermute | solution.py:17
  68.9 33.2 %all-to-all-start.3 = ((bf16[4,8,128,128]{3,2,1,0:T(8,128)(2,1)}), bf16[4,8,128,128]{3,2,1,0:T(8,128)(2,1)S(1)}, u32[]{:S(2)}, u32[]{:S(2)}) async-start(bf16[4,8,128,128]{3,2,1,0:T(8,128)(2,1)} %level_one.1.ours), calls=%async_computation.3 | async-start | bytes 2097152 | tf_op jit(solution)/shard_map/all_to_all | solution.py:190
  74.7 2.9 %collective-permute-start.12 = (bf16[4,8,128,128]{3,2,1,0:T(8,128)(2,1)}, bf16[4,8,128,128]{3,2,1,0:T(8,128)(2,1)S(1)}, u32[]{:S(2)}, u32[]{:S(2)}) collective-permute-start(bf16[4,8,128,128]{3,2,1,0:T(8,128)(2,1)} %level_one.1.ours), channel_id=1, source_target_pairs={{0,1},{1,0},{2,3},{3,2},{4,5},{5,4},{6,7},{7,6},{8,9},{9,8},{10,11... | collective-permute-start | bytes 3145736 | tf_op jit(solution)/shard_map/ppermute | solution.py:17
  88.5 49.8 %copy-start.11 = (bf16[8,128,128]{2,1,0:T(8,128)(2,1)S(1)}, bf16[8,128,128]{2,1,0:T(8,128)(2,1)}, u32[]{:S(2)}) copy-start(bf16[8,128,128]{2,1,0:T(8,128)(2,1)} %get-tuple-element.107) | copy-start | bytes 786436
  88.5 17.4 %collective-permute-start.13 = (bf16[2,128,128]{2,1,0:T(8,128)(2,1)}, bf16[2,128,128]{2,1,0:T(8,128)(2,1)S(1)}, u32[]{:S(2)}, u32[]{:S(2)}) collective-permute-start(bf16[2,128,128]{2,1,0:T(8,128)(2,1)} %get-tuple-element.86), channel_id=1, source_target_pairs={{0,2},{2,0},{4,6},{6,4},{1,3},{3,1},{5,7},{7,5},{8,10},{10,8},{12,... | collective-permute-start | bytes 196616 | tf_op jit(solution)/shard_map/ppermute | solution.py:17
  90.6 15.4 %collective-permute-start.14 = (bf16[2,128,128]{2,1,0:T(8,128)(2,1)}, bf16[2,128,128]{2,1,0:T(8,128)(2,1)S(1)}, u32[]{:S(2)}, u32[]{:S(2)}) collective-permute-start(bf16[2,128,128]{2,1,0:T(8,128)(2,1)} %get-tuple-element.87), channel_id=1, source_target_pairs={{0,4},{2,6},{4,0},{6,2},{1,5},{3,7},{5,1},{7,3},{8,12},{10,14},{12... | collective-permute-start | bytes 196616 | tf_op jit(solution)/shard_map/ppermute | solution.py:17
  92.9 13.0 %collective-permute-start.15 = (bf16[2,128,128]{2,1,0:T(8,128)(2,1)}, bf16[2,128,128]{2,1,0:T(8,128)(2,1)S(1)}, u32[]{:S(2)}, u32[]{:S(2)}) collective-permute-start(bf16[2,128,128]{2,1,0:T(8,128)(2,1)} %get-tuple-element.88), channel_id=1, source_target_pairs={{0,6},{2,4},{4,2},{6,0},{1,7},{3,5},{5,3},{7,1},{8,14},{10,12},{12... | collective-permute-start | bytes 196616 | tf_op jit(solution)/shard_map/ppermute | solution.py:17
  102.6 5.9 %collective-permute-start.16 = (bf16[128,128]{1,0:T(8,128)(2,1)S(1)}, bf16[128,128]{1,0:T(8,128)(2,1)S(1)}, u32[]{:S(2)}, u32[]{:S(2)}) collective-permute-start(bf16[128,128]{1,0:T(8,128)(2,1)S(1)} %fusion.5), channel_id=1, source_target_pairs={{0,1},{1,0},{2,3},{3,2},{4,5},{5,4},{6,7},{7,6},{8,9},{9,8},{10,11... | collective-permute-start | bytes 98312 | tf_op jit(solution)/shard_map/ppermute | solution.py:17
  105.9 11.3 %collective-permute-start.20 = (bf16[8,128,128]{2,1,0:T(8,128)(2,1)}, bf16[8,128,128]{2,1,0:T(8,128)(2,1)S(1)}, u32[]{:S(2)}, u32[]{:S(2)}) collective-permute-start(bf16[8,128,128]{2,1,0:T(8,128)(2,1)} %get-tuple-element.96), channel_id=1, source_target_pairs={{0,6},{2,4},{4,2},{6,0},{1,7},{3,5},{5,3},{7,1},{8,14},{10,12},{12... | collective-permute-start | bytes 786440 | tf_op jit(solution)/shard_map/ppermute | solution.py:17
  108.5 14.9 %collective-permute-start.17 = (bf16[2,128,128]{2,1,0:T(8,128)(2,1)S(1)}, bf16[2,128,128]{2,1,0:T(8,128)(2,1)S(1)}, u32[]{:S(2)}, u32[]{:S(2)}) collective-permute-start(bf16[2,128,128]{2,1,0:T(8,128)(2,1)S(1)} %pad_maximum_fusion.3), channel_id=1, source_target_pairs={{0,2},{2,0},{4,6},{6,4},{1,3},{3,1},{5,7},{7,5},{8,10},{10,8},{12,... | collective-permute-start | bytes 196616 | tf_op jit(solution)/shard_map/ppermute | solution.py:17
  108.5 15.8 %collective-permute-start.18 = (bf16[2,128,128]{2,1,0:T(8,128)(2,1)S(1)}, bf16[2,128,128]{2,1,0:T(8,128)(2,1)S(1)}, u32[]{:S(2)}, u32[]{:S(2)}) collective-permute-start(bf16[2,128,128]{2,1,0:T(8,128)(2,1)S(1)} %pad_maximum_fusion.3), channel_id=1, source_target_pairs={{0,4},{2,6},{4,0},{6,2},{1,5},{3,7},{5,1},{7,3},{8,12},{10,14},{12... | collective-permute-start | bytes 196616 | tf_op jit(solution)/shard_map/ppermute | solution.py:17
  110.5 13.8 %collective-permute-start.19 = (bf16[2,128,128]{2,1,0:T(8,128)(2,1)S(1)}, bf16[2,128,128]{2,1,0:T(8,128)(2,1)S(1)}, u32[]{:S(2)}, u32[]{:S(2)}) collective-permute-start(bf16[2,128,128]{2,1,0:T(8,128)(2,1)S(1)} %pad_maximum_fusion.3), channel_id=1, source_target_pairs={{0,6},{2,4},{4,2},{6,0},{1,7},{3,5},{5,3},{7,1},{8,14},{10,12},{12... | collective-permute-start | bytes 196616 | tf_op jit(solution)/shard_map/ppermute | solution.py:17
  113.8 19.9 %collective-permute-start.24 = (bf16[8,128,128]{2,1,0:T(8,128)(2,1)}, bf16[8,128,128]{2,1,0:T(8,128)(2,1)S(1)}, u32[]{:S(2)}, u32[]{:S(2)}) collective-permute-start(bf16[8,128,128]{2,1,0:T(8,128)(2,1)} %get-tuple-element.101), channel_id=1, source_target_pairs={{0,2},{2,0},{4,6},{6,4},{1,3},{3,1},{5,7},{7,5},{8,10},{10,8},{12,... | collective-permute-start | bytes 786440 | tf_op jit(solution)/shard_map/ppermute | solution.py:17
  117.2 19.3 %collective-permute-start.25 = (bf16[8,128,128]{2,1,0:T(8,128)(2,1)}, bf16[8,128,128]{2,1,0:T(8,128)(2,1)S(1)}, u32[]{:S(2)}, u32[]{:S(2)}) collective-permute-start(bf16[8,128,128]{2,1,0:T(8,128)(2,1)} %get-tuple-element.102), channel_id=1, source_target_pairs={{0,4},{2,6},{4,0},{6,2},{1,5},{3,7},{5,1},{7,3},{8,12},{10,14},{12... | collective-permute-start | bytes 786440 | tf_op jit(solution)/shard_map/ppermute | solution.py:17
  124.4 6.1 %collective-permute-start.21 = (bf16[4,128,128]{2,1,0:T(8,128)(2,1)S(1)}, bf16[4,128,128]{2,1,0:T(8,128)(2,1)S(1)}, u32[]{:S(2)}, u32[]{:S(2)}) collective-permute-start(bf16[4,128,128]{2,1,0:T(8,128)(2,1)S(1)} %pad_maximum_fusion.2), channel_id=1, source_target_pairs={{0,8},{8,0},{16,24},{24,16},{1,9},{9,1},{17,25},{25,17},{2,10},{10... | collective-permute-start | bytes 393224 | tf_op jit(solution)/shard_map/ppermute | solution.py:17
  125.7 6.4 %collective-permute-start.22 = (bf16[4,128,128]{2,1,0:T(8,128)(2,1)S(1)}, bf16[4,128,128]{2,1,0:T(8,128)(2,1)S(1)}, u32[]{:S(2)}, u32[]{:S(2)}) collective-permute-start(bf16[4,128,128]{2,1,0:T(8,128)(2,1)S(1)} %pad_maximum_fusion.2), channel_id=1, source_target_pairs={{0,16},{8,24},{16,0},{24,8},{1,17},{9,25},{17,1},{25,9},{2,18},{10... | collective-permute-start | bytes 393224 | tf_op jit(solution)/shard_map/ppermute | solution.py:17
  126.8 6.8 %collective-permute-start.23 = (bf16[4,128,128]{2,1,0:T(8,128)(2,1)S(1)}, bf16[4,128,128]{2,1,0:T(8,128)(2,1)S(1)}, u32[]{:S(2)}, u32[]{:S(2)}) collective-permute-start(bf16[4,128,128]{2,1,0:T(8,128)(2,1)S(1)} %pad_maximum_fusion.2), channel_id=1, source_target_pairs={{0,24},{8,16},{16,8},{24,0},{1,25},{9,17},{17,9},{25,1},{2,26},{10... | collective-permute-start | bytes 393224 | tf_op jit(solution)/shard_map/ppermute | solution.py:17
  (16 other events, 318.0 us)

commit v3 on v0

v3 whole, which is shorter than its diff:
```python
import functools

import jax
import jax.numpy as jnp
from jax import lax
from jax.experimental import pallas as pl
from jax.experimental.pallas import tpu as pltpu
from jax.sharding import Mesh, PartitionSpec as P

ROW, CHIP, CORE = "prow", "pchip", "pcore"
F32 = jnp.float32
BF16 = jnp.bfloat16
SMEM = pl.BlockSpec(memory_space=pltpu.SMEM)
VMEM = pl.BlockSpec(memory_space=pltpu.VMEM)
LIMIT = 24 << 20
MOST = 56 << 20


HBM = pl.BlockSpec(memory_space=pltpu.HBM)


def begin(copies):
    for copy in copies:
        copy.start()
    return copies


def finish(copies):
    for copy in copies:
        copy.wait()


def load(own, sibling, inverse, sems):
    core = lax.axis_index(CORE)
    return begin(
        [
            pltpu.make_async_copy(own, inverse.at[core], sems.at[0]),
            pltpu.make_async_copy(sibling, inverse.at[1 - core], sems.at[1]),
        ]
    )


def load_panels(pieces, panels, sems):
    here, group = lax.axis_index(ROW), pieces[0].shape[1]
    copies = []
    for s, piece in enumerate(pieces):
        place = pl.ds(pl.multiple_of((here ^ s) * group, group), group)
        copies.append(pltpu.make_async_copy(piece, panels.at[:, place], sems.at[s]))
    return begin(copies)


def block(inverse, rows, cols):
    width = inverse.shape[2]
    lines = []
    for row in rows:
        tiles = [inverse[col // width, row, col % width] for col in cols]
        lines.append(jnp.concatenate(tiles, axis=1))
    return jnp.concatenate(lines, axis=0)


def level_one_kernel(nodes, count, rows_one, own, sibling, *refs):
    here, chip, core = lax.axis_index(ROW), lax.axis_index(CHIP), lax.axis_index(CORE)
    pieces, refs = refs[:count], refs[count:]
    whole, sends, (inverse, panels, held, sems, out_sems) = refs[0], refs[1:nodes], refs[nodes:]
    per_row, tile = panels.shape[1], panels.shape[2]
    height, width = inverse.shape[1], 2 * inverse.shape[2]
    finish(load(own, sibling, inverse, sems) + load_panels(pieces, panels, sems.at[2:]))
    copies = []
    for t in reversed(range(nodes)):
        at = chip ^ t
        node = 2 * at + core
        rows = [rows_one[node, here * per_row + m] - here * height for m in range(per_row)]
        cols = [rows_one[node, chip * per_row + n] - chip * width for n in range(per_row)]
        panel = panels[at].reshape(per_row * tile, tile)
        part = jnp.dot(block(inverse, rows, cols), panel, preferred_element_type=F32)
        held[t] = part.astype(BF16).reshape(per_row, tile, tile)
        copies += begin([pltpu.make_async_copy(held.at[t], whole.at[at], out_sems.at[t])])
        if t:
            copies += begin(
                [pltpu.make_async_copy(held.at[t], sends[t - 1], out_sems.at[nodes + t])]
            )
    finish(copies)


def level_two_kernel(
    nodes, count, choices, rows_one, parent_two, order_two, own, sibling, ours, theirs, *refs
):
    here, chip, core = lax.axis_index(ROW), lax.axis_index(CHIP), lax.axis_index(CORE)
    pieces, refs = refs[:count], refs[count:]
    inputs, refs = refs[: sum(choices)], refs[sum(choices) :]
    columns, smalls, refs = refs[:nodes], refs[nodes : 2 * nodes], refs[2 * nodes :]
    inverse, panels, blocks, factors, held, sems, in_sems, out_sems = refs
    per_row, tile = panels.shape[1], panels.shape[2]
    height, width = inverse.shape[1], 2 * inverse.shape[2]
    first = begin(
        [
            pltpu.make_async_copy(ours, blocks.at[core], in_sems.at[nodes]),
            pltpu.make_async_copy(theirs, blocks.at[1 - core], in_sems.at[nodes + 1]),
        ]
    )
    is_end = jnp.logical_or(chip == 0, chip == nodes - 1)
    for t in range(nodes):
        mine, inputs = inputs[: choices[t]], inputs[choices[t] :]
        copies = [pltpu.make_async_copy(ref, factors.at[t], in_sems.at[t]) for ref in mine]
        first.append(copies[0])
        if len(copies) == 1:
            copies[0].start()
        else:
            pl.when(is_end)(copies[1].start)
            pl.when(jnp.logical_not(is_end))(copies[0].start)
    second = load(own, sibling, inverse, sems) + load_panels(pieces, panels, sems.at[2:])
    finish(first)
    contract = (((0,), (0,)), ((), ()))
    parts = []
    for t in range(nodes):
        node = 2 * (chip ^ t) + core
        parent = parent_two[node]
        near = [
            blocks[parent % 2, parent // 2, order_two[node, here * per_row + m] - here * per_row]
            for m in range(per_row)
        ]
        near = jnp.concatenate(near, axis=0)
        factor = factors[t, :per_row].reshape(per_row * tile, tile)
        smalls[t][0] = lax.dot_general(near, factor, contract, preferred_element_type=F32).astype(
            BF16
        )
        parts.append(jnp.dot(near, factors[t, per_row], preferred_element_type=F32))
    finish(second)
    copies = []
    for t in reversed(range(nodes)):
        node = 2 * (chip ^ t) + core
        parent = parent_two[node]
        rows = [
            rows_one[parent, order_two[node, here * per_row + m]] - here * height
            for m in range(per_row)
        ]
        cols = [
            rows_one[parent, order_two[node, chip * per_row + n]] - chip * width
            for n in range(per_row)
        ]
        panel = panels[chip ^ t].reshape(per_row * tile, tile)
        part = jnp.dot(block(inverse, rows, cols), panel, preferred_element_type=F32)
        part = (part - parts[t]).astype(BF16)
        held[t] = part.reshape(per_row, tile, tile)
        copies += begin([pltpu.make_async_copy(held.at[t], columns[t], out_sems.at[t])])
        factor = factors[t, :per_row].reshape(per_row * tile, tile)
        smalls[t][1] = lax.dot_general(factor, part, contract, preferred_element_type=F32).astype(
            BF16
        )
    finish(copies)


def column_kernel(parts, panel, column, part):
    column[...] = (-jnp.sum(parts[...].astype(F32), axis=0)).astype(BF16)
    shape = (panel.shape[0] * panel.shape[1], panel.shape[2])
    part[...] = lax.dot_general(
        panel[...].reshape(shape),
        column[...].reshape(shape),
        (((0,), (0,)), ((), ())),
        preferred_element_type=F32,
    ).astype(BF16)


def form_column(parts, panel):
    return pl.pallas_call(
        column_kernel,
        out_shape=[
            jax.ShapeDtypeStruct(panel.shape, BF16),
            jax.ShapeDtypeStruct(panel.shape[1:], BF16),
        ],
        in_specs=[VMEM] * 2,
        out_specs=[VMEM] * 2,
        compiler_params=pltpu.CompilerParams(vmem_limit_bytes=LIMIT),
        name="form_column",
    )(parts, panel)


def choose_kernel(nodes, parent_two, ours, theirs, *outs):
    chip, core = lax.axis_index(CHIP), lax.axis_index(CORE)
    for t in range(nodes):
        parent = parent_two[2 * (chip ^ t) + core]
        outs[t][...] = jnp.where(parent % 2 == core, ours[...], theirs[...])


def choose(nodes, parent_two, ours, theirs):
    return pl.pallas_call(
        functools.partial(choose_kernel, nodes),
        out_shape=[jax.ShapeDtypeStruct(ours.shape, BF16)] * nodes,
        in_specs=[SMEM] + [VMEM] * 2,
        out_specs=[VMEM] * nodes,
        compiler_params=pltpu.CompilerParams(vmem_limit_bytes=LIMIT),
        name="choose",
    )(parent_two, ours, theirs)


def last_kernel(nodes, parent_two, link, base, *refs):
    diagonals, parts, (upper, diagonal_two) = refs[:nodes], refs[nodes:-2], refs[-2:]
    chip, core = lax.axis_index(CHIP), lax.axis_index(CORE)
    step = (parent_two[2 * chip + core] // 2) ^ chip
    near = diagonals[0][...]
    for t in range(1, nodes):
        near = jnp.where(step == t, diagonals[t][...], near)
    sums = total([part[...] for part in parts])
    parent_term = jnp.dot(near, link[...], preferred_element_type=F32)
    upper[...] = (sums[0] - parent_term).astype(BF16)
    term = lax.dot_general(
        link[...], upper[...], (((0,), (0,)), ((), ())), preferred_element_type=F32
    )
    diagonal_two[...] = (base[...] - term + sums[1]).astype(BF16)


def form_last(parent_two, link, base, diagonals, parts):
    return pl.pallas_call(
        functools.partial(last_kernel, len(diagonals)),
        out_shape=[jax.ShapeDtypeStruct(link.shape, BF16)] * 2,
        in_specs=[SMEM] + [VMEM] * (2 + len(diagonals) + len(parts)),
        out_specs=[VMEM] * 2,
        compiler_params=pltpu.CompilerParams(vmem_limit_bytes=LIMIT),
        name="form_last",
    )(parent_two, link, base, *diagonals, *parts)


def level_one(rows_one, own, sibling, pieces):
    nodes, group, tile = pieces[0].shape[0], pieces[0].shape[1], pieces[0].shape[2]
    count = len(pieces)
    per_row = group * count
    flops = 2 * nodes * per_row * per_row * tile**3
    tiles = (per_row, tile, tile)
    return pl.pallas_call(
        functools.partial(level_one_kernel, nodes, count),
        out_shape=[jax.ShapeDtypeStruct((nodes,) + tiles, BF16)]
        + [jax.ShapeDtypeStruct(tiles, BF16)] * (nodes - 1),
        in_specs=[SMEM] + [HBM] * (2 + count),
        out_specs=[HBM] * nodes,
        scratch_shapes=[
            pltpu.VMEM((2,) + own.shape, BF16),
            pltpu.VMEM((nodes,) + tiles, BF16),
            pltpu.VMEM((nodes,) + tiles, BF16),
            pltpu.SemaphoreType.DMA((2 + count,)),
            pltpu.SemaphoreType.DMA((2 * nodes,)),
        ],
        compiler_params=pltpu.CompilerParams(vmem_limit_bytes=MOST),
        cost_estimate=pl.CostEstimate(flops=flops, bytes_accessed=12 << 20, transcendentals=0),
        name="level_one",
    )(rows_one, own, sibling, *pieces)


def level_two(rows_one, parent_two, order_two, own, sibling, ours, theirs, pieces, factors):
    nodes, group, tile = pieces[0].shape[0], pieces[0].shape[1], pieces[0].shape[2]
    count = len(pieces)
    per_row = group * count
    flops = 2 * nodes * per_row * (per_row + 3) * tile**3
    choices = [len(f) for f in factors]
    tiles = (per_row, tile, tile)
    return pl.pallas_call(
        functools.partial(level_two_kernel, nodes, count, choices),
        out_shape=[jax.ShapeDtypeStruct(tiles, BF16)] * nodes
        + [jax.ShapeDtypeStruct((2, tile, tile), BF16)] * nodes,
        in_specs=[SMEM] * 3 + [HBM] * (4 + count + sum(choices)),
        out_specs=[HBM] * nodes + [VMEM] * nodes,
        scratch_shapes=[
            pltpu.VMEM((2,) + own.shape, BF16),
            pltpu.VMEM((nodes,) + tiles, BF16),
            pltpu.VMEM((2, nodes) + tiles, BF16),
            pltpu.VMEM((nodes, per_row + 1, tile, tile), BF16),
            pltpu.VMEM((nodes,) + tiles, BF16),
            pltpu.SemaphoreType.DMA((2 + count,)),
            pltpu.SemaphoreType.DMA((nodes + 2,)),
            pltpu.SemaphoreType.DMA((nodes,)),
        ],
        compiler_params=pltpu.CompilerParams(vmem_limit_bytes=MOST),
        cost_estimate=pl.CostEstimate(flops=flops, bytes_accessed=16 << 20, transcendentals=0),
        name="level_two",
    )(rows_one, parent_two, order_two, own, sibling, ours, theirs, *pieces, *sum(factors, []))


def exchange(x, axis, step):
    size = lax.axis_size(axis)
    return lax.ppermute(x, axis, [(i, i ^ step) for i in range(size)])


def spread(x, axis):
    return [x] + [exchange(x, axis, s) for s in range(1, lax.axis_size(axis))]


def after(x, *others):
    return lax.optimization_barrier((x,) + others)[0]


def together(*arrays):
    return lax.optimization_barrier(arrays)


def halves(panel, axis):
    rows = lax.axis_size(axis)
    return panel.reshape((rows, panel.shape[0] // rows) + panel.shape[1:])


def swap(blocks, axis):
    return lax.all_to_all(blocks, axis, 0, 0, tiled=True)


def total(parts):
    return functools.reduce(jnp.add, [part.astype(F32) for part in parts])


def local(
    inverse_top, rows_one, panel_one, base_one, parent_two, order_two, panel_two, link_two, base_two
):
    chip, core = lax.axis_index(CHIP), lax.axis_index(CORE)
    nodes = lax.axis_size(CHIP)
    line = nodes == 4
    payload = jnp.concatenate([panel_two[0], link_two], axis=0)
    near = exchange(payload, CHIP, 1)
    if line:
        inner = lax.ppermute(payload, CHIP, [(1, 2), (2, 1)])
    else:
        inner = [exchange(payload, CHIP, t) for t in range(2, nodes)]
    sibling = exchange(inverse_top, CORE, 1)
    both = jnp.concatenate([halves(panel_one[0], ROW), halves(panel_two[0], ROW)], axis=1)
    quarters = swap(both, ROW)
    quarters, near, inner = together(quarters, near, inner)
    group = quarters.shape[1] // 2
    blocks_one = swap(quarters[:, :group], CHIP)
    pieces_one = spread(blocks_one, ROW)
    quarters_two, payload_late, near_late, inner_late = together(
        quarters[:, group:], payload, near, inner, blocks_one
    )[:4]
    blocks_two = swap(quarters_two, CHIP)
    over = out_one = out_two = ()
    if line:
        over = lax.ppermute(near_late, CHIP, [(1, 2), (2, 1)])
        out_one = lax.ppermute(inner_late, CHIP, [(1, 0), (2, 3)])
        out_two = lax.ppermute(payload_late, CHIP, [(0, 3), (3, 0)])
    ours, *sends = level_one(rows_one, inverse_top, sibling, pieces_one)
    pieces_two = spread(blocks_two, ROW)
    ours, over, out_one, out_two, pieces_two = together(ours, over, out_one, out_two, pieces_two)
    theirs = exchange(ours, CORE, 1)
    parts_one = swap(ours, CHIP)
    if line:
        factors = [[payload], [near], [over, out_one], [inner, out_two]]
    else:
        factors = [[f] for f in [payload, near, *inner]]
    outs = level_two(
        rows_one, parent_two, order_two, inverse_top, sibling, ours, theirs, pieces_two, factors
    )
    columns, smalls = outs[:nodes], outs[nodes:]
    first = [exchange(columns[t], CHIP, t) for t in range(nodes // 2 + 1, nodes)]
    parts_small = [smalls[0]] + [exchange(smalls[t], CHIP, t) for t in range(1, nodes)]
    *last, token = together(*columns[1 : nodes // 2 + 1], parts_small)
    last = [exchange(column, CHIP, t + 1) for t, column in enumerate(last)]
    column_one, part = form_column(parts_one, panel_one[0])
    diagonal_one = (base_one[0] - total(spread(part, ROW))).astype(BF16)
    chosen = choose(nodes, parent_two, diagonal_one, exchange(diagonal_one, CORE, 1))
    diagonals = [chosen[0]] + [exchange(chosen[t], CHIP, t) for t in range(1, nodes)]
    parts_last = spread(total(parts_small).astype(BF16), ROW)
    upper, diagonal_two = form_last(parent_two, link_two[0], base_two[0], diagonals, parts_last)
    column_two = (-total([columns[0], *first, *last])).astype(BF16)
    return (
        column_one[None],
        diagonal_one[None],
        column_two[None],
        upper[None],
        diagonal_two[None],
    )


def solution(mesh):
    rows, columns = mesh.devices.shape
    fine = Mesh(mesh.devices.reshape(rows, columns // 2, 2), (ROW, CHIP, CORE))
    col = (CHIP, CORE)
    return jax.shard_map(
        local,
        mesh=fine,
        in_specs=(
            P(ROW, col, None, None),
            P(),
            P(col, ROW, None, None),
            P(col, None, None),
            P(),
            P(),
            P(col, ROW, None, None),
            P(col, None, None),
            P(col, None, None),
        ),
        out_specs=(
            P(col, ROW, None, None),
            P(col, None, None),
            P(col, ROW, None, None),
            P(col, None, None),
            P(col, None, None),
        ),
        check_vma=False,
    )
```

time: 311 us -> 131 us (0.42)
  waiting for transfers between devices: 195 us -> 26.2 us
  starting transfers between devices: 8.58 us -> 56.9 us
  local copies, waits for them, and re-layouts: 38.6 us -> 2.8 us
  matrix products: 25.3 us -> 0 us
  Pallas kernels: 0 us -> 23 us
  between operations: 18.2 us -> 1.02 us
  other arithmetic: 9.38 us -> 5.59 us
    reduce_scatter x2 -> x0, waiting for transfers between devices: 79.7 us -> none  [the longest x1 45.4 us: local(): lax.psum_scatter(tile_products(inverse_top, flat_one, row_one, col_one).a...]
    ppermute x0 -> x29, starting transfers between devices: none -> 45.2 us  [the longest x25 37 us: exchange(): return lax.ppermute(x, axis, [(i, i ^ step) for i in range(size)])]
    all_gather x3 -> x0, waiting for transfers between devices: 40.7 us -> none  [the longest x1 29.8 us: local(): full_one = lax.all_gather(panel_one, 'prow', axis=1, tiled=True)]
    psum x1 -> x0, waiting for transfers between devices: 40.6 us -> none  [local(): lax.psum(diag_part.astype(jnp.bfloat16), 'prow').astype(jnp.float32)]
    gather x15 -> x0, local copies, waits for them, and re-layouts: 36.5 us -> none  [the longest x2 26 us: tile_products(): blocks = inverse_local[row_local[:, :, None], col_local[:, None, :]]]
    all_to_all x2 -> x3, waiting for transfers between devices: 33.1 us -> 0.01 us  [swap(): return lax.all_to_all(blocks, axis, 0, 0, tiled=True)]
    ppermute x0 -> x29, waiting for transfers between devices: none -> 26.2 us  [the longest x25 26.2 us: exchange(): return lax.ppermute(x, axis, [(i, i ^ step) for i in range(size)])]
    dot_general x8 -> x0, matrix products: 25.3 us -> none  [the longest x2 19.7 us: tile_products(): jnp.einsum('kabij,kbjl->kail', blocks, received, preferred_element_type=j...]
  transfers between devices with their start and end apart: 8 -> 32, of which waited for: 7 -> 8; matrix products, arithmetic and copies ran while one was open for 21% -> 5% of each run, Pallas kernels for 0% -> 17%
where the time goes in v3:
time: 131 us; the launch traced here: 130 us
  starting transfers between devices  56.9 us (43%)
  waiting for transfers between devices  26.2 us (20%)
  Pallas kernels  23 us (18%)
  blocking collectives  15 us (11%)
  other arithmetic  5.59 us (4%)
  local copies, waits for them, and re-layouts  2.8 us (2%)
    ppermute x25, starting transfers between devices, exchange(): return lax.ppermute(x, axis, [(i, i ^ step) for i in range(size)])  37 us
    ppermute x25, waiting for transfers between devices, exchange(): return lax.ppermute(x, axis, [(i, i ^ step) for i in range(size)])  26.2 us
    all_to_all x1, blocking collectives, swap(): return lax.all_to_all(blocks, axis, 0, 0, tiled=True)  15 us
    pallas_call x1, Pallas kernels, level_two(): pl.pallas_call(functools.partial(level_two_kernel, nodes, count, choices)...  12.3 us
    all_to_all x3, starting transfers between devices, swap(): return lax.all_to_all(blocks, axis, 0, 0, tiled=True)  11.7 us
    pallas_call x1, Pallas kernels, level_one(): pl.pallas_call(functools.partial(level_one_kernel, nodes, count), out_sha...  7.72 us
    ppermute x1, starting transfers between devices, local(): out_two = lax.ppermute(payload_late, CHIP, [(0, 3), (3, 0)])  5.62 us
  transfers between devices with their start and end apart: 32, of which 8 were waited for; matrix products, arithmetic and copies ran while one was open for 5% of the time, Pallas kernels for 17%

profile of v3, /device:TPU:0, one launch (start us, length us, event | category | flops | bytes accessed | tf_op | source)
XLA Modules:
  0.0 130.5 jit_solution(4732573867279635406)
XLA Ops:
  1.1 1.9 %pad_maximum_fusion = bf16[4,4,128,128]{3,2,1,0:T(8,128)(2,1)} fusion(bf16[4,2,128,128]{3,2,1,0:T(8,128)(2,1)} %bitcast.21, bf16[4,2,128,128]{3,2,1,0:T(8,128)(2,1)} %bitcast.16), kind=kLoop, calls=%fused_computation | loop fusion | flops 262144 | bytes 1048576 | tf_op jit(solution)/shard_map/concatenate | solution.py:320
  3.0 4.7 %all-to-all-start = ((bf16[4,4,128,128]{3,2,1,0:T(8,128)(2,1)}), bf16[4,4,128,128]{3,2,1,0:T(8,128)(2,1)S(1)}, u32[]{:S(2)}, u32[]{:S(2)}) async-start(bf16[4,4,128,128]{3,2,1,0:T(8,128)(2,1)} %pad_maximum_fusion), calls=%async_computation | async-start | bytes 1048576 | tf_op jit(solution)/shard_map/all_to_all | solution.py:300
  8.8 1.6 %collective-permute-start.1 = (bf16[9,128,128]{2,1,0:T(8,128)(2,1)S(1)}, bf16[9,128,128]{2,1,0:T(8,128)(2,1)S(1)}, u32[]{:S(2)}, u32[]{:S(2)}) collective-permute-start(bf16[9,128,128]{2,1,0:T(8,128)(2,1)S(1)} %pad_maximum_fusion.1.refs_4_), channel_id=1, source_target_pairs={{0,2},{2,0},{4,6},{6,4},{1,3},{3,1},{5,7},{7,5},{8,10},{10,8},{12,... | collective-permute-start | bytes 884744 | tf_op jit(solution)/shard_map/ppermute | solution.py:279
  11.1 6.9 %collective-permute-done.1.refs_5_ = bf16[9,128,128]{2,1,0:T(8,128)(2,1)S(1)} collective-permute-done((bf16[9,128,128]{2,1,0:T(8,128)(2,1)S(1)}, bf16[9,128,128]{2,1,0:T(8,128)(2,1)S(1)}, u32[]{:S(2)}, u32[]{:S(2)}) %collective-permute-start.1) | collective-permute-done | bytes 294944 | tf_op jit(solution)/shard_map/ppermute | solution.py:279
  18.8 15.0 %all_to_all.20.refs_0_ = bf16[4,2,128,128]{3,2,1,0:T(8,128)(2,1)S(1)} all-to-all(bf16[4,2,128,128]{3,2,1,0:T(8,128)(2,1)S(1)} %get-tuple-element.74), channel_id=1, replica_groups=mesh['prow'=4,'pchip'=4,'pcore'=2] {'pchip'}, dimensions={0} | all-to-all | bytes 524288 | tf_op jit(solution)/shard_map/all_to_all | solution.py:300
  33.8 3.4 %all-to-all-start.2 = ((bf16[4,2,128,128]{3,2,1,0:T(8,128)(2,1)}), bf16[4,2,128,128]{3,2,1,0:T(8,128)(2,1)S(1)}, u32[]{:S(2)}, u32[]{:S(2)}) async-start(bf16[4,2,128,128]{3,2,1,0:T(8,128)(2,1)} %get-tuple-element.46), calls=%async_computation.2 | async-start | bytes 524288 | tf_op jit(solution)/shard_map/all_to_all | solution.py:300
  37.2 1.4 %collective-permute-start.3 = (bf16[4,2,128,128]{3,2,1,0:T(8,128)(2,1)S(1)}, bf16[4,2,128,128]{3,2,1,0:T(8,128)(2,1)S(1)}, u32[]{:S(2)}, u32[]{:S(2)}) collective-permute-start(bf16[4,2,128,128]{3,2,1,0:T(8,128)(2,1)S(1)} %all_to_all.20.refs_0_), channel_id=1, source_target_pairs={{0,8},{8,0},{16,24},{24,16},{1,9},{9,1},{17,25},{25,17},{2,10},{10... | collective-permute-start | bytes 786440 | tf_op jit(solution)/shard_map/ppermute | solution.py:279
  38.6 1.5 %collective-permute-start.4 = (bf16[4,2,128,128]{3,2,1,0:T(8,128)(2,1)S(1)}, bf16[4,2,128,128]{3,2,1,0:T(8,128)(2,1)S(1)}, u32[]{:S(2)}, u32[]{:S(2)}) collective-permute-start(bf16[4,2,128,128]{3,2,1,0:T(8,128)(2,1)S(1)} %all_to_all.20.refs_0_), channel_id=1, source_target_pairs={{0,16},{8,24},{16,0},{24,8},{1,17},{9,25},{17,1},{25,9},{2,18},{10... | collective-permute-start | bytes 786440 | tf_op jit(solution)/shard_map/ppermute | solution.py:279
  41.5 5.0 %collective-permute-done.3.refs_1_ = bf16[4,2,128,128]{3,2,1,0:T(8,128)(2,1)S(1)} collective-permute-done((bf16[4,2,128,128]{3,2,1,0:T(8,128)(2,1)S(1)}, bf16[4,2,128,128]{3,2,1,0:T(8,128)(2,1)S(1)}, u32[]{:S(2)}, u32[]{:S(2)}) %collective-permute-start.3) | collective-permute-done | bytes 262176 | tf_op jit(solution)/shard_map/ppermute | solution.py:279
  46.5 1.3 collective-permute-start.7
  47.8 2.6 %collective-permute-done.4.refs_2_ = bf16[4,2,128,128]{3,2,1,0:T(8,128)(2,1)S(1)} collective-permute-done((bf16[4,2,128,128]{3,2,1,0:T(8,128)(2,1)S(1)}, bf16[4,2,128,128]{3,2,1,0:T(8,128)(2,1)S(1)}, u32[]{:S(2)}, u32[]{:S(2)}) %collective-permute-start.4) | collective-permute-done | bytes 262176 | tf_op jit(solution)/shard_map/ppermute | solution.py:279
  50.4 5.6 %collective-permute-start.8 = (bf16[9,128,128]{2,1,0:T(8,128)(2,1)S(1)}, bf16[9,128,128]{2,1,0:T(8,128)(2,1)S(1)}, u32[]{:S(2)}, u32[]{:S(2)}) collective-permute-start(bf16[9,128,128]{2,1,0:T(8,128)(2,1)S(1)} %pad_maximum_fusion.1.refs_4_), channel_id=1, source_target_pairs={{0,6},{6,0},{1,7},{7,1},{8,14},{14,8},{9,15},{15,9},{16,22},{22,16... | collective-permute-start | bytes 884744 | tf_op jit(solution)/shard_map/ppermute | solution.py:334
  56.1 1.8 %collective-permute-start.10 = (bf16[4,2,128,128]{3,2,1,0:T(8,128)(2,1)S(1)}, bf16[4,2,128,128]{3,2,1,0:T(8,128)(2,1)S(1)}, u32[]{:S(2)}, u32[]{:S(2)}) collective-permute-start(bf16[4,2,128,128]{3,2,1,0:T(8,128)(2,1)S(1)} %all-to-all-done.2.refs_0_), channel_id=1, source_target_pairs={{0,16},{8,24},{16,0},{24,8},{1,17},{9,25},{17,1},{25,9},{2,18},{10... | collective-permute-start | bytes 786440 | tf_op jit(solution)/shard_map/ppermute | solution.py:279
  58.0 2.0 %collective-permute-start.9 = (bf16[4,2,128,128]{3,2,1,0:T(8,128)(2,1)S(1)}, bf16[4,2,128,128]{3,2,1,0:T(8,128)(2,1)S(1)}, u32[]{:S(2)}, u32[]{:S(2)}) collective-permute-start(bf16[4,2,128,128]{3,2,1,0:T(8,128)(2,1)S(1)} %all-to-all-done.2.refs_0_), channel_id=1, source_target_pairs={{0,8},{8,0},{16,24},{24,16},{1,9},{9,1},{17,25},{25,17},{2,10},{10... | collective-permute-start | bytes 786440 | tf_op jit(solution)/shard_map/ppermute | solution.py:279
  60.0 7.7 %level_one.1 = (bf16[4,8,128,128]{3,2,1,0:T(8,128)(2,1)}, bf16[8,128,128]{2,1,0:T(8,128)(2,1)}, bf16[8,128,128]{2,1,0:T(8,128)(2,1)}, bf16[8,128,128]{2,1,0:T(8,128)(2,1)}) custom-call(s32[8,32]{1,0:T(8,128)} %rows_one.3, bf16[16,8,128,128]{3,2,1,0:T(8,128)(2,1)} %own.3, bf16[16,8,128,128]{3,2,1,0:T(8,128)(2,1)} %collective-permute-done.sibling, ...), custom_call_target="tpu_custom_call" | custom-call | flops 1073741824 | bytes 12582912 | tf_op jit(solution)/shard_map/level_one/pallas_call | solution.py:229
  68.8 3.5 %all-to-all-start.3 = ((bf16[4,8,128,128]{3,2,1,0:T(8,128)(2,1)}), bf16[4,8,128,128]{3,2,1,0:T(8,128)(2,1)S(1)}, u32[]{:S(2)}, u32[]{:S(2)}) async-start(bf16[4,8,128,128]{3,2,1,0:T(8,128)(2,1)} %get-tuple-element.47.ours), calls=%async_computation.3 | async-start | bytes 2097152 | tf_op jit(solution)/shard_map/all_to_all | solution.py:300
  72.5 2.9 %collective-permute-done.15.theirs = bf16[4,8,128,128]{3,2,1,0:T(8,128)(2,1)S(1)} collective-permute-done((bf16[4,8,128,128]{3,2,1,0:T(8,128)(2,1)}, bf16[4,8,128,128]{3,2,1,0:T(8,128)(2,1)S(1)}, u32[]{:S(2)}, u32[]{:S(2)}) %collective-permute-start.15) | collective-permute-done | bytes 1048608 | tf_op jit(solution)/shard_map/ppermute | solution.py:279
  76.3 12.3 %level_two.1 = (bf16[8,128,128]{2,1,0:T(8,128)(2,1)}, bf16[8,128,128]{2,1,0:T(8,128)(2,1)}, bf16[8,128,128]{2,1,0:T(8,128)(2,1)}, bf16[8,128,128]{2,1,0:T(8,128)...) custom-call(s32[8,32]{1,0:T(8,128)} %rows_one.3, ...), custom_call_target="tpu_custom_call" | custom-call | flops 1476395008 | bytes 16777216 | tf_op jit(solution)/shard_map/level_two/pallas_call | solution.py:255
  88.7 2.2 %collective-permute-start.17 = (bf16[2,128,128]{2,1,0:T(8,128)(2,1)}, bf16[2,128,128]{2,1,0:T(8,128)(2,1)S(1)}, u32[]{:S(2)}, u32[]{:S(2)}) collective-permute-start(bf16[2,128,128]{2,1,0:T(8,128)(2,1)} %get-tuple-element.62), channel_id=1, source_target_pairs={{0,2},{2,0},{4,6},{6,4},{1,3},{3,1},{5,7},{7,5},{8,10},{10,8},{12,... | collective-permute-start | bytes 196616 | tf_op jit(solution)/shard_map/ppermute | solution.py:279
  90.9 2.1 %collective-permute-start.18 = (bf16[2,128,128]{2,1,0:T(8,128)(2,1)}, bf16[2,128,128]{2,1,0:T(8,128)(2,1)S(1)}, u32[]{:S(2)}, u32[]{:S(2)}) collective-permute-start(bf16[2,128,128]{2,1,0:T(8,128)(2,1)} %get-tuple-element.63), channel_id=1, source_target_pairs={{0,4},{2,6},{4,0},{6,2},{1,5},{3,7},{5,1},{7,3},{8,12},{10,14},{12... | collective-permute-start | bytes 196616 | tf_op jit(solution)/shard_map/ppermute | solution.py:279
  93.3 3.5 %collective-permute-start.16 = (bf16[8,128,128]{2,1,0:T(8,128)(2,1)}, bf16[8,128,128]{2,1,0:T(8,128)(2,1)S(1)}, u32[]{:S(2)}, u32[]{:S(2)}) collective-permute-start(bf16[8,128,128]{2,1,0:T(8,128)(2,1)} %get-tuple-element.58), channel_id=1, source_target_pairs={{0,6},{2,4},{4,2},{6,0},{1,7},{3,5},{5,3},{7,1},{8,14},{10,12},{12... | collective-permute-start | bytes 786440 | tf_op jit(solution)/shard_map/ppermute | solution.py:279
  97.8 7.8 %collective-permute-start.12 = (bf16[128,128]{1,0:T(8,128)(2,1)S(1)}, bf16[128,128]{1,0:T(8,128)(2,1)S(1)}, u32[]{:S(2)}, u32[]{:S(2)}) collective-permute-start(bf16[128,128]{1,0:T(8,128)(2,1)S(1)} %get-tuple-element.49), channel_id=1, source_target_pairs={{0,8},{8,0},{16,24},{24,16},{1,9},{9,1},{17,25},{25,17},{2,10},{10... | collective-permute-start | bytes 98312 | tf_op jit(solution)/shard_map/ppermute | solution.py:279
  105.6 1.5 %collective-permute-start.14 = (bf16[128,128]{1,0:T(8,128)(2,1)S(1)}, bf16[128,128]{1,0:T(8,128)(2,1)S(1)}, u32[]{:S(2)}, u32[]{:S(2)}) collective-permute-start(bf16[128,128]{1,0:T(8,128)(2,1)S(1)} %get-tuple-element.49), channel_id=1, source_target_pairs={{0,24},{8,16},{16,8},{24,0},{1,25},{9,17},{17,9},{25,1},{2,26},{10... | collective-permute-start | bytes 98312 | tf_op jit(solution)/shard_map/ppermute | solution.py:279
  107.9 2.1 %collective-permute-start.26 = (bf16[2,128,128]{2,1,0:T(8,128)(2,1)S(1)}, bf16[2,128,128]{2,1,0:T(8,128)(2,1)S(1)}, u32[]{:S(2)}, u32[]{:S(2)}) collective-permute-start(bf16[2,128,128]{2,1,0:T(8,128)(2,1)S(1)} %add_convert_fusion.refs_4_), channel_id=1, source_target_pairs={{0,8},{8,0},{16,24},{24,16},{1,9},{9,1},{17,25},{25,17},{2,10},{10... | collective-permute-start | bytes 196616 | tf_op jit(solution)/shard_map/ppermute | solution.py:279
  110.0 2.6 %collective-permute-start.21 = (bf16[8,128,128]{2,1,0:T(8,128)(2,1)}, bf16[8,128,128]{2,1,0:T(8,128)(2,1)S(1)}, u32[]{:S(2)}, u32[]{:S(2)}) collective-permute-start(bf16[8,128,128]{2,1,0:T(8,128)(2,1)} %get-tuple-element.66), channel_id=1, source_target_pairs={{0,4},{2,6},{4,0},{6,2},{1,5},{3,7},{5,1},{7,3},{8,12},{10,14},{12... | collective-permute-start | bytes 786440 | tf_op jit(solution)/shard_map/ppermute | solution.py:279
  112.7 1.2 collective-permute-done.22.theirs
  114.6 1.5 %collective-permute-start.28 = (bf16[2,128,128]{2,1,0:T(8,128)(2,1)S(1)}, bf16[2,128,128]{2,1,0:T(8,128)(2,1)S(1)}, u32[]{:S(2)}, u32[]{:S(2)}) collective-permute-start(bf16[2,128,128]{2,1,0:T(8,128)(2,1)S(1)} %add_convert_fusion.refs_4_), channel_id=1, source_target_pairs={{0,24},{8,16},{16,8},{24,0},{1,25},{9,17},{17,9},{25,1},{2,26},{10... | collective-permute-start | bytes 196616 | tf_op jit(solution)/shard_map/ppermute | solution.py:279
  116.4 3.6 %collective-permute-done.20 = bf16[8,128,128]{2,1,0:T(8,128)(2,1)S(1)} collective-permute-done((bf16[8,128,128]{2,1,0:T(8,128)(2,1)}, bf16[8,128,128]{2,1,0:T(8,128)(2,1)S(1)}, u32[]{:S(2)}, u32[]{:S(2)}) %collective-permute-start.20) | collective-permute-done | bytes 262176 | tf_op jit(solution)/shard_map/ppermute | solution.py:279
  120.2 3.1 %collective-permute-done.21 = bf16[8,128,128]{2,1,0:T(8,128)(2,1)S(1)} collective-permute-done((bf16[8,128,128]{2,1,0:T(8,128)(2,1)}, bf16[8,128,128]{2,1,0:T(8,128)(2,1)S(1)}, u32[]{:S(2)}, u32[]{:S(2)}) %collective-permute-start.21) | collective-permute-done | bytes 262176 | tf_op jit(solution)/shard_map/ppermute | solution.py:279
  123.3 3.1 %collective-permute-start.25 = (bf16[128,128]{1,0:T(8,128)(2,1)S(1)}, bf16[128,128]{1,0:T(8,128)(2,1)S(1)}, u32[]{:S(2)}, u32[]{:S(2)}) collective-permute-start(bf16[128,128]{1,0:T(8,128)(2,1)S(1)} %get-tuple-element.70), channel_id=1, source_target_pairs={{0,6},{2,4},{4,2},{6,0},{1,7},{3,5},{5,3},{7,1},{8,14},{10,12},{12... | collective-permute-start | bytes 98312 | tf_op jit(solution)/shard_map/ppermute | solution.py:279
  126.4 1.8 %fusion = bf16[1,8,128,128]{3,2,1,0:T(8,128)(2,1)} fusion(bf16[8,128,128]{2,1,0:T(8,128)(2,1)S(1)} %collective-permute-done.21, bf16[8,128,128]{2,1,0:T(8,128)(2,1)S(1)} %collective-permute-done.20, bf16[8,128,128]{2,1,0:T(8,128)(2,1)S(1)} %collective-permute-done.16, bf16[8,128,128]{2,1,0:T(8,128)(2,1)} %get-tuple-element.57), kind=kLoop, calls=%fused_computation.3 | loop fusion | flops 1179648 | bytes 1310720 | tf_op jit(solution)/shard_map/broadcast_in_dim | solution.py:362
  129.0 1.5 %form_last.1 = (bf16[128,128]{1,0:T(8,128)(2,1)}, bf16[128,128]{1,0:T(8,128)(2,1)}) custom-call(s32[8]{0:T(128)S(1)} %copy-done.4, bf16[128,128]{1,0:T(8,128)(2,1)S(1)} %bitcast.18, f32[128,128]{1,0:T(8,128)S(1)} %bitcast.20, bf16[128,128]{1,0:T(8,128)(2,1)S(1)} %get-tuple-element.67.refs_0_, bf16[128,128]{1,0:T(8,128)(2,1)S(1)} %collective-permute-done.23.refs_1_, ...), custom_call_target="tpu_custom_call" | custom-call | tf_op jit(solution)/shard_map/form_last/pallas_call | solution.py:213
  (86 shorter events, 10.6 us)
Async XLA Ops:
  0.6 57.4 %collective-permute-start = (bf16[16,8,128,128]{3,2,1,0:T(8,128)(2,1)}, bf16[16,8,128,128]{3,2,1,0:T(8,128)(2,1)}, u32[]{:S(2)}, u32[]{:S(2)}) collective-permute-start(bf16[16,8,128,128]{3,2,1,0:T(8,128)(2,1)} %own.3), channel_id=1, source_target_pairs={{0,1},{1,0},{2,3},{3,2},{4,5},{5,4},{6,7},{7,6},{8,9},{9,8},{10,11... | collective-permute-start | bytes 12582920 | tf_op jit(solution)/shard_map/ppermute | solution.py:279
  3.0 14.9 %all-to-all-start = ((bf16[4,4,128,128]{3,2,1,0:T(8,128)(2,1)}), bf16[4,4,128,128]{3,2,1,0:T(8,128)(2,1)S(1)}, u32[]{:S(2)}, u32[]{:S(2)}) async-start(bf16[4,4,128,128]{3,2,1,0:T(8,128)(2,1)} %pad_maximum_fusion), calls=%async_computation | async-start | bytes 1048576 | tf_op jit(solution)/shard_map/all_to_all | solution.py:300
  8.8 9.2 %collective-permute-start.1 = (bf16[9,128,128]{2,1,0:T(8,128)(2,1)S(1)}, bf16[9,128,128]{2,1,0:T(8,128)(2,1)S(1)}, u32[]{:S(2)}, u32[]{:S(2)}) collective-permute-start(bf16[9,128,128]{2,1,0:T(8,128)(2,1)S(1)} %pad_maximum_fusion.1.refs_4_), channel_id=1, source_target_pairs={{0,2},{2,0},{4,6},{6,4},{1,3},{3,1},{5,7},{7,5},{8,10},{10,8},{12,... | collective-permute-start | bytes 884744 | tf_op jit(solution)/shard_map/ppermute | solution.py:279
  10.4 7.5 %collective-permute-start.2 = (bf16[9,128,128]{2,1,0:T(8,128)(2,1)S(1)}, bf16[9,128,128]{2,1,0:T(8,128)(2,1)S(1)}, u32[]{:S(2)}, u32[]{:S(2)}) collective-permute-start(bf16[9,128,128]{2,1,0:T(8,128)(2,1)S(1)} %pad_maximum_fusion.1.refs_4_), channel_id=1, source_target_pairs={{2,4},{4,2},{3,5},{5,3},{10,12},{12,10},{11,13},{13,11},{18,20},{2... | collective-permute-start | bytes 884744 | tf_op jit(solution)/shard_map/ppermute | solution.py:316
  33.8 22.3 %all-to-all-start.2 = ((bf16[4,2,128,128]{3,2,1,0:T(8,128)(2,1)}), bf16[4,2,128,128]{3,2,1,0:T(8,128)(2,1)S(1)}, u32[]{:S(2)}, u32[]{:S(2)}) async-start(bf16[4,2,128,128]{3,2,1,0:T(8,128)(2,1)} %get-tuple-element.46), calls=%async_computation.2 | async-start | bytes 524288 | tf_op jit(solution)/shard_map/all_to_all | solution.py:300
  37.2 9.3 %collective-permute-start.3 = (bf16[4,2,128,128]{3,2,1,0:T(8,128)(2,1)S(1)}, bf16[4,2,128,128]{3,2,1,0:T(8,128)(2,1)S(1)}, u32[]{:S(2)}, u32[]{:S(2)}) collective-permute-start(bf16[4,2,128,128]{3,2,1,0:T(8,128)(2,1)S(1)} %all_to_all.20.refs_0_), channel_id=1, source_target_pairs={{0,8},{8,0},{16,24},{24,16},{1,9},{9,1},{17,25},{25,17},{2,10},{10... | collective-permute-start | bytes 786440 | tf_op jit(solution)/shard_map/ppermute | solution.py:279
  38.6 11.8 %collective-permute-start.4 = (bf16[4,2,128,128]{3,2,1,0:T(8,128)(2,1)S(1)}, bf16[4,2,128,128]{3,2,1,0:T(8,128)(2,1)S(1)}, u32[]{:S(2)}, u32[]{:S(2)}) collective-permute-start(bf16[4,2,128,128]{3,2,1,0:T(8,128)(2,1)S(1)} %all_to_all.20.refs_0_), channel_id=1, source_target_pairs={{0,16},{8,24},{16,0},{24,8},{1,17},{9,25},{17,1},{25,9},{2,18},{10... | collective-permute-start | bytes 786440 | tf_op jit(solution)/shard_map/ppermute | solution.py:279
  40.1 17.8 %collective-permute-start.6 = (bf16[9,128,128]{2,1,0:T(8,128)(2,1)S(1)}, bf16[9,128,128]{2,1,0:T(8,128)(2,1)S(1)}, u32[]{:S(2)}, u32[]{:S(2)}) collective-permute-start(bf16[9,128,128]{2,1,0:T(8,128)(2,1)S(1)} %collective-permute-done.1.refs_5_), channel_id=1, source_target_pairs={{2,4},{4,2},{3,5},{5,3},{10,12},{12,10},{11,13},{13,11},{18,20},{2... | collective-permute-start | bytes 884744 | tf_op jit(solution)/shard_map/ppermute | solution.py:332
  40.8 15.3 %collective-permute-start.5 = (bf16[4,2,128,128]{3,2,1,0:T(8,128)(2,1)S(1)}, bf16[4,2,128,128]{3,2,1,0:T(8,128)(2,1)S(1)}, u32[]{:S(2)}, u32[]{:S(2)}) collective-permute-start(bf16[4,2,128,128]{3,2,1,0:T(8,128)(2,1)S(1)} %all_to_all.20.refs_0_), channel_id=1, source_target_pairs={{0,24},{8,16},{16,8},{24,0},{1,25},{9,17},{17,9},{25,1},{2,26},{10... | collective-permute-start | bytes 786440 | tf_op jit(solution)/shard_map/ppermute | solution.py:279
  46.5 21.3 %collective-permute-start.7 = (bf16[9,128,128]{2,1,0:T(8,128)(2,1)S(1)}, bf16[9,128,128]{2,1,0:T(8,128)(2,1)S(1)}, u32[]{:S(2)}, u32[]{:S(2)}) collective-permute-start(bf16[9,128,128]{2,1,0:T(8,128)(2,1)S(1)} %collective-permute-done.2.refs_8_), channel_id=1, source_target_pairs={{2,0},{4,6},{3,1},{5,7},{10,8},{12,14},{11,9},{13,15},{18,16},{20,... | collective-permute-start | bytes 884744 | tf_op jit(solution)/shard_map/ppermute | solution.py:333
  50.4 17.4 %collective-permute-start.8 = (bf16[9,128,128]{2,1,0:T(8,128)(2,1)S(1)}, bf16[9,128,128]{2,1,0:T(8,128)(2,1)S(1)}, u32[]{:S(2)}, u32[]{:S(2)}) collective-permute-start(bf16[9,128,128]{2,1,0:T(8,128)(2,1)S(1)} %pad_maximum_fusion.1.refs_4_), channel_id=1, source_target_pairs={{0,6},{6,0},{1,7},{7,1},{8,14},{14,8},{9,15},{15,9},{16,22},{22,16... | collective-permute-start | bytes 884744 | tf_op jit(solution)/shard_map/ppermute | solution.py:334
  56.1 11.7 %collective-permute-start.10 = (bf16[4,2,128,128]{3,2,1,0:T(8,128)(2,1)S(1)}, bf16[4,2,128,128]{3,2,1,0:T(8,128)(2,1)S(1)}, u32[]{:S(2)}, u32[]{:S(2)}) collective-permute-start(bf16[4,2,128,128]{3,2,1,0:T(8,128)(2,1)S(1)} %all-to-all-done.2.refs_0_), channel_id=1, source_target_pairs={{0,16},{8,24},{16,0},{24,8},{1,17},{9,25},{17,1},{25,9},{2,18},{10... | collective-permute-start | bytes 786440 | tf_op jit(solution)/shard_map/ppermute | solution.py:279
  57.9 9.9 %collective-permute-start.11 = (bf16[4,2,128,128]{3,2,1,0:T(8,128)(2,1)S(1)}, bf16[4,2,128,128]{3,2,1,0:T(8,128)(2,1)S(1)}, u32[]{:S(2)}, u32[]{:S(2)}) collective-permute-start(bf16[4,2,128,128]{3,2,1,0:T(8,128)(2,1)S(1)} %all-to-all-done.2.refs_0_), channel_id=1, source_target_pairs={{0,24},{8,16},{16,8},{24,0},{1,25},{9,17},{17,9},{25,1},{2,26},{10... | collective-permute-start | bytes 786440 | tf_op jit(solution)/shard_map/ppermute | solution.py:279
  58.0 9.9 %collective-permute-start.9 = (bf16[4,2,128,128]{3,2,1,0:T(8,128)(2,1)S(1)}, bf16[4,2,128,128]{3,2,1,0:T(8,128)(2,1)S(1)}, u32[]{:S(2)}, u32[]{:S(2)}) collective-permute-start(bf16[4,2,128,128]{3,2,1,0:T(8,128)(2,1)S(1)} %all-to-all-done.2.refs_0_), channel_id=1, source_target_pairs={{0,8},{8,0},{16,24},{24,16},{1,9},{9,1},{17,25},{25,17},{2,10},{10... | collective-permute-start | bytes 786440 | tf_op jit(solution)/shard_map/ppermute | solution.py:279
  68.8 28.1 %all-to-all-start.3 = ((bf16[4,8,128,128]{3,2,1,0:T(8,128)(2,1)}), bf16[4,8,128,128]{3,2,1,0:T(8,128)(2,1)S(1)}, u32[]{:S(2)}, u32[]{:S(2)}) async-start(bf16[4,8,128,128]{3,2,1,0:T(8,128)(2,1)} %get-tuple-element.47.ours), calls=%async_computation.3 | async-start | bytes 2097152 | tf_op jit(solution)/shard_map/all_to_all | solution.py:300
  72.4 2.9 %collective-permute-start.15 = (bf16[4,8,128,128]{3,2,1,0:T(8,128)(2,1)}, bf16[4,8,128,128]{3,2,1,0:T(8,128)(2,1)S(1)}, u32[]{:S(2)}, u32[]{:S(2)}) collective-permute-start(bf16[4,8,128,128]{3,2,1,0:T(8,128)(2,1)} %get-tuple-element.47.ours), channel_id=1, source_target_pairs={{0,1},{1,0},{2,3},{3,2},{4,5},{5,4},{6,7},{7,6},{8,9},{9,8},{10,11... | collective-permute-start | bytes 3145736 | tf_op jit(solution)/shard_map/ppermute | solution.py:279
  88.7 16.9 %collective-permute-start.17 = (bf16[2,128,128]{2,1,0:T(8,128)(2,1)}, bf16[2,128,128]{2,1,0:T(8,128)(2,1)S(1)}, u32[]{:S(2)}, u32[]{:S(2)}) collective-permute-start(bf16[2,128,128]{2,1,0:T(8,128)(2,1)} %get-tuple-element.62), channel_id=1, source_target_pairs={{0,2},{2,0},{4,6},{6,4},{1,3},{3,1},{5,7},{7,5},{8,10},{10,8},{12,... | collective-permute-start | bytes 196616 | tf_op jit(solution)/shard_map/ppermute | solution.py:279
  90.9 14.7 %collective-permute-start.18 = (bf16[2,128,128]{2,1,0:T(8,128)(2,1)}, bf16[2,128,128]{2,1,0:T(8,128)(2,1)S(1)}, u32[]{:S(2)}, u32[]{:S(2)}) collective-permute-start(bf16[2,128,128]{2,1,0:T(8,128)(2,1)} %get-tuple-element.63), channel_id=1, source_target_pairs={{0,4},{2,6},{4,0},{6,2},{1,5},{3,7},{5,1},{7,3},{8,12},{10,14},{12... | collective-permute-start | bytes 196616 | tf_op jit(solution)/shard_map/ppermute | solution.py:279
  93.1 14.0 %collective-permute-start.19 = (bf16[2,128,128]{2,1,0:T(8,128)(2,1)}, bf16[2,128,128]{2,1,0:T(8,128)(2,1)S(1)}, u32[]{:S(2)}, u32[]{:S(2)}) collective-permute-start(bf16[2,128,128]{2,1,0:T(8,128)(2,1)} %get-tuple-element.64), channel_id=1, source_target_pairs={{0,6},{2,4},{4,2},{6,0},{1,7},{3,5},{5,3},{7,1},{8,14},{10,12},{12... | collective-permute-start | bytes 196616 | tf_op jit(solution)/shard_map/ppermute | solution.py:279
  93.3 22.8 %collective-permute-start.16 = (bf16[8,128,128]{2,1,0:T(8,128)(2,1)}, bf16[8,128,128]{2,1,0:T(8,128)(2,1)S(1)}, u32[]{:S(2)}, u32[]{:S(2)}) collective-permute-start(bf16[8,128,128]{2,1,0:T(8,128)(2,1)} %get-tuple-element.58), channel_id=1, source_target_pairs={{0,6},{2,4},{4,2},{6,0},{1,7},{3,5},{5,3},{7,1},{8,14},{10,12},{12... | collective-permute-start | bytes 786440 | tf_op jit(solution)/shard_map/ppermute | solution.py:279
  97.8 12.2 %collective-permute-start.12 = (bf16[128,128]{1,0:T(8,128)(2,1)S(1)}, bf16[128,128]{1,0:T(8,128)(2,1)S(1)}, u32[]{:S(2)}, u32[]{:S(2)}) collective-permute-start(bf16[128,128]{1,0:T(8,128)(2,1)S(1)} %get-tuple-element.49), channel_id=1, source_target_pairs={{0,8},{8,0},{16,24},{24,16},{1,9},{9,1},{17,25},{25,17},{2,10},{10... | collective-permute-start | bytes 98312 | tf_op jit(solution)/shard_map/ppermute | solution.py:279
  105.6 4.5 %collective-permute-start.13 = (bf16[128,128]{1,0:T(8,128)(2,1)S(1)}, bf16[128,128]{1,0:T(8,128)(2,1)S(1)}, u32[]{:S(2)}, u32[]{:S(2)}) collective-permute-start(bf16[128,128]{1,0:T(8,128)(2,1)S(1)} %get-tuple-element.49), channel_id=1, source_target_pairs={{0,16},{8,24},{16,0},{24,8},{1,17},{9,25},{17,1},{25,9},{2,18},{10... | collective-permute-start | bytes 98312 | tf_op jit(solution)/shard_map/ppermute | solution.py:279
  105.6 7.0 %collective-permute-start.14 = (bf16[128,128]{1,0:T(8,128)(2,1)S(1)}, bf16[128,128]{1,0:T(8,128)(2,1)S(1)}, u32[]{:S(2)}, u32[]{:S(2)}) collective-permute-start(bf16[128,128]{1,0:T(8,128)(2,1)S(1)} %get-tuple-element.49), channel_id=1, source_target_pairs={{0,24},{8,16},{16,8},{24,0},{1,25},{9,17},{17,9},{25,1},{2,26},{10... | collective-permute-start | bytes 98312 | tf_op jit(solution)/shard_map/ppermute | solution.py:279
  107.9 6.7 %collective-permute-start.26 = (bf16[2,128,128]{2,1,0:T(8,128)(2,1)S(1)}, bf16[2,128,128]{2,1,0:T(8,128)(2,1)S(1)}, u32[]{:S(2)}, u32[]{:S(2)}) collective-permute-start(bf16[2,128,128]{2,1,0:T(8,128)(2,1)S(1)} %add_convert_fusion.refs_4_), channel_id=1, source_target_pairs={{0,8},{8,0},{16,24},{24,16},{1,9},{9,1},{17,25},{25,17},{2,10},{10... | collective-permute-start | bytes 196616 | tf_op jit(solution)/shard_map/ppermute | solution.py:279
  110.0 10.0 %collective-permute-start.20 = (bf16[8,128,128]{2,1,0:T(8,128)(2,1)}, bf16[8,128,128]{2,1,0:T(8,128)(2,1)S(1)}, u32[]{:S(2)}, u32[]{:S(2)}) collective-permute-start(bf16[8,128,128]{2,1,0:T(8,128)(2,1)} %get-tuple-element.65), channel_id=1, source_target_pairs={{0,2},{2,0},{4,6},{6,4},{1,3},{3,1},{5,7},{7,5},{8,10},{10,8},{12,... | collective-permute-start | bytes 786440 | tf_op jit(solution)/shard_map/ppermute | solution.py:279
  110.0 13.3 %collective-permute-start.21 = (bf16[8,128,128]{2,1,0:T(8,128)(2,1)}, bf16[8,128,128]{2,1,0:T(8,128)(2,1)S(1)}, u32[]{:S(2)}, u32[]{:S(2)}) collective-permute-start(bf16[8,128,128]{2,1,0:T(8,128)(2,1)} %get-tuple-element.66), channel_id=1, source_target_pairs={{0,4},{2,6},{4,0},{6,2},{1,5},{3,7},{5,1},{7,3},{8,12},{10,14},{12... | collective-permute-start | bytes 786440 | tf_op jit(solution)/shard_map/ppermute | solution.py:279
  112.7 1.3 collective-permute-start.22
  113.9 14.3 %collective-permute-start.27 = (bf16[2,128,128]{2,1,0:T(8,128)(2,1)S(1)}, bf16[2,128,128]{2,1,0:T(8,128)(2,1)S(1)}, u32[]{:S(2)}, u32[]{:S(2)}) collective-permute-start(bf16[2,128,128]{2,1,0:T(8,128)(2,1)S(1)} %add_convert_fusion.refs_4_), channel_id=1, source_target_pairs={{0,16},{8,24},{16,0},{24,8},{1,17},{9,25},{17,1},{25,9},{2,18},{10... | collective-permute-start | bytes 196616 | tf_op jit(solution)/shard_map/ppermute | solution.py:279
  114.6 13.6 %collective-permute-start.28 = (bf16[2,128,128]{2,1,0:T(8,128)(2,1)S(1)}, bf16[2,128,128]{2,1,0:T(8,128)(2,1)S(1)}, u32[]{:S(2)}, u32[]{:S(2)}) collective-permute-start(bf16[2,128,128]{2,1,0:T(8,128)(2,1)S(1)} %add_convert_fusion.refs_4_), channel_id=1, source_target_pairs={{0,24},{8,16},{16,8},{24,0},{1,25},{9,17},{17,9},{25,1},{2,26},{10... | collective-permute-start | bytes 196616 | tf_op jit(solution)/shard_map/ppermute | solution.py:279
  116.2 12.0 %collective-permute-start.23 = (bf16[128,128]{1,0:T(8,128)(2,1)S(1)}, bf16[128,128]{1,0:T(8,128)(2,1)S(1)}, u32[]{:S(2)}, u32[]{:S(2)}) collective-permute-start(bf16[128,128]{1,0:T(8,128)(2,1)S(1)} %get-tuple-element.68), channel_id=1, source_target_pairs={{0,2},{2,0},{4,6},{6,4},{1,3},{3,1},{5,7},{7,5},{8,10},{10,8},{12,... | collective-permute-start | bytes 98312 | tf_op jit(solution)/shard_map/ppermute | solution.py:279
  120.0 8.2 %collective-permute-start.24 = (bf16[128,128]{1,0:T(8,128)(2,1)S(1)}, bf16[128,128]{1,0:T(8,128)(2,1)S(1)}, u32[]{:S(2)}, u32[]{:S(2)}) collective-permute-start(bf16[128,128]{1,0:T(8,128)(2,1)S(1)} %get-tuple-element.69), channel_id=1, source_target_pairs={{0,4},{2,6},{4,0},{6,2},{1,5},{3,7},{5,1},{7,3},{8,12},{10,14},{12... | collective-permute-start | bytes 98312 | tf_op jit(solution)/shard_map/ppermute | solution.py:279
  123.3 5.7 %collective-permute-start.25 = (bf16[128,128]{1,0:T(8,128)(2,1)S(1)}, bf16[128,128]{1,0:T(8,128)(2,1)S(1)}, u32[]{:S(2)}, u32[]{:S(2)}) collective-permute-start(bf16[128,128]{1,0:T(8,128)(2,1)S(1)} %get-tuple-element.70), channel_id=1, source_target_pairs={{0,6},{2,4},{4,2},{6,0},{1,7},{3,5},{5,3},{7,1},{8,14},{10,12},{12... | collective-permute-start | bytes 98312 | tf_op jit(solution)/shard_map/ppermute | solution.py:279
  (21 other events, 483.7 us)

commit v4 on v3

v4 whole, which is shorter than its diff:
```python
import functools

import jax
import jax.numpy as jnp
from jax import lax
from jax.experimental import pallas as pl
from jax.experimental.pallas import tpu as pltpu
from jax.sharding import Mesh, PartitionSpec as P

ROW, CHIP, CORE = "prow", "pchip", "pcore"
F32 = jnp.float32
BF16 = jnp.bfloat16
SMEM = pl.BlockSpec(memory_space=pltpu.SMEM)
VMEM = pl.BlockSpec(memory_space=pltpu.VMEM)
LIMIT = 24 << 20
PARTS = 4


HBM = pl.BlockSpec(memory_space=pltpu.HBM)
ANY = pl.BlockSpec(memory_space=pl.ANY)


def begin(copies):
    for copy in copies:
        copy.start()
    return copies


def finish(copies):
    for copy in copies:
        copy.wait()


def load(own, sibling, inverse, sems):
    core, step = lax.axis_index(CORE), own.shape[0] // PARTS
    copies = []
    for n in range(PARTS):
        rows = pl.ds(n * step, step)
        for k, (ref, at) in enumerate(((own, core), (sibling, 1 - core))):
            copies.append(
                pltpu.make_async_copy(ref.at[rows], inverse.at[at, rows], sems.at[2 * n + k])
            )
    return begin(copies)


def pair_kernel(own, sibling, inverse, sems):
    finish(load(own, sibling, inverse, sems))


def pair(own, sibling):
    return pl.pallas_call(
        pair_kernel,
        out_shape=jax.ShapeDtypeStruct((2,) + own.shape, BF16),
        in_specs=[ANY] * 2,
        out_specs=VMEM,
        scratch_shapes=[pltpu.SemaphoreType.DMA((2 * PARTS,))],
        compiler_params=pltpu.CompilerParams(vmem_limit_bytes=LIMIT),
        name="pair",
    )(own, sibling)


def positions(count, group, here):
    return [(here ^ s) * group + g for s in range(count) for g in range(group)]


def block(inverse, rows, cols):
    width = inverse.shape[2]
    lines = []
    for row in rows:
        tiles = [inverse[col // width, row, col % width] for col in cols]
        lines.append(jnp.concatenate(tiles, axis=1))
    return jnp.concatenate(lines, axis=0)


def level_one_kernel(nodes, count, rows_one, inverse, *refs):
    here, chip, core = lax.axis_index(ROW), lax.axis_index(CHIP), lax.axis_index(CORE)
    pieces, whole = refs[:count], refs[count]
    group, tile = pieces[0].shape[1], pieces[0].shape[2]
    per_row = group * count
    height, width = inverse.shape[1], 2 * inverse.shape[2]
    for at in range(nodes):
        node = 2 * at + core
        rows = [rows_one[node, here * per_row + m] - here * height for m in range(per_row)]
        cols = [
            rows_one[node, chip * per_row + n] - chip * width
            for n in positions(count, group, here)
        ]
        panel = jnp.concatenate([piece[at].reshape(group * tile, tile) for piece in pieces], axis=0)
        part = jnp.dot(block(inverse, rows, cols), panel, preferred_element_type=F32)
        whole[at] = part.astype(BF16).reshape(per_row, tile, tile)


def near_kernel(
    nodes, choices, parent_two, order_two, own, sibling, ours, theirs, *refs
):
    here, chip, core = lax.axis_index(ROW), lax.axis_index(CHIP), lax.axis_index(CORE)
    inputs, (near, smalls, inverse, sems) = refs[: sum(choices)], refs[sum(choices) :]
    per_row, tile = near.shape[1], near.shape[2]
    copies = load(own, sibling, inverse, sems)
    is_end = jnp.logical_or(chip == 0, chip == nodes - 1)
    for t in range(nodes):
        mine, inputs = inputs[: choices[t]], inputs[choices[t] :]
        factor = mine[0][:per_row]
        if len(mine) > 1:
            factor = jnp.where(is_end, mine[1][:per_row], factor)
        node = 2 * (chip ^ t) + core
        parent = parent_two[node]
        is_ours = parent % 2 == core
        for m in range(per_row):
            at = order_two[node, here * per_row + m] - here * per_row
            near[t, m] = jnp.where(is_ours, ours[parent // 2, at], theirs[parent // 2, at])
        smalls[t] = lax.dot_general(
            near[t].reshape(per_row * tile, tile),
            factor.reshape(per_row * tile, tile),
            (((0,), (0,)), ((), ())),
            preferred_element_type=F32,
        ).astype(BF16)
    finish(copies)


def level_two_kernel(
    nodes, count, choices, rows_one, parent_two, order_two, inverse, near, upper, *refs
):
    here, chip, core = lax.axis_index(ROW), lax.axis_index(CHIP), lax.axis_index(CORE)
    pieces, refs = refs[:count], refs[count:]
    inputs, refs = refs[: sum(choices)], refs[sum(choices) :]
    columns, smalls = refs[:nodes], refs[nodes:]
    group, tile = pieces[0].shape[1], pieces[0].shape[2]
    per_row = group * count
    height, width = inverse.shape[1], 2 * inverse.shape[2]
    is_end = jnp.logical_or(chip == 0, chip == nodes - 1)
    factors = []
    for t in range(nodes):
        mine, inputs = inputs[: choices[t]], inputs[choices[t] :]
        factor = mine[0][...]
        if len(mine) > 1:
            factor = jnp.where(is_end, mine[1][...], factor)
        factors.append(factor[:per_row].reshape(per_row * tile, tile))
        node = 2 * (chip ^ t) + core
        parent = parent_two[node]
        rows = [
            rows_one[parent, order_two[node, here * per_row + m]] - here * height
            for m in range(per_row)
        ]
        cols = [
            rows_one[parent, order_two[node, chip * per_row + n]] - chip * width
            for n in positions(count, group, here)
        ]
        panel = [piece[chip ^ t].reshape(group * tile, tile) for piece in pieces]
        panel = jnp.concatenate(panel, axis=0)
        carried = jnp.dot(
            near[t].reshape(per_row * tile, tile), factor[per_row], preferred_element_type=F32
        )
        part = jnp.dot(block(inverse, rows, cols), panel, preferred_element_type=F32)
        columns[t][...] = (part - carried).astype(BF16).reshape(per_row, tile, tile)
        smalls[t][0] = upper[t]
    for t in range(nodes):
        smalls[t][1] = lax.dot_general(
            factors[t],
            columns[t][...].reshape(per_row * tile, tile),
            (((0,), (0,)), ((), ())),
            preferred_element_type=F32,
        ).astype(BF16)


def cut_kernel(panel, *outs):
    here = lax.axis_index(ROW)
    for s, out in enumerate(outs):
        group = out.shape[0]
        out[...] = panel[pl.ds(pl.multiple_of((here ^ s) * group, group), group)]


def cut_groups(panel, count):
    group = (panel.shape[0] // count,) + panel.shape[1:]
    return pl.pallas_call(
        cut_kernel,
        out_shape=[jax.ShapeDtypeStruct(group, BF16)] * count,
        in_specs=[VMEM],
        out_specs=[VMEM] * count,
        compiler_params=pltpu.CompilerParams(vmem_limit_bytes=LIMIT),
        name="cut_groups",
    )(panel)


def join_kernel(*refs):
    here = lax.axis_index(ROW)
    for s, ref in enumerate(refs[:-1]):
        refs[-1][here ^ s] = ref[...]


def join_groups(groups):
    return pl.pallas_call(
        join_kernel,
        out_shape=jax.ShapeDtypeStruct((len(groups),) + groups[0].shape, BF16),
        in_specs=[VMEM] * len(groups),
        out_specs=VMEM,
        compiler_params=pltpu.CompilerParams(vmem_limit_bytes=LIMIT),
        name="join_groups",
    )(*groups)


def column_kernel(parts, panel, *refs):
    smalls, (column, small) = refs[:-2], refs[-2:]
    column[...] = (-jnp.sum(parts[...].astype(F32), axis=0)).astype(BF16)
    shape = (panel.shape[0] * panel.shape[1], panel.shape[2])
    small[0] = lax.dot_general(
        panel[...].reshape(shape),
        column[...].reshape(shape),
        (((0,), (0,)), ((), ())),
        preferred_element_type=F32,
    ).astype(BF16)
    small[1:] = total([ref[...] for ref in smalls]).astype(BF16)


def form_column(parts, panel, smalls):
    return pl.pallas_call(
        column_kernel,
        out_shape=[
            jax.ShapeDtypeStruct(panel.shape, BF16),
            jax.ShapeDtypeStruct((3,) + panel.shape[1:], BF16),
        ],
        in_specs=[VMEM] * (2 + len(smalls)),
        out_specs=[VMEM] * 2,
        compiler_params=pltpu.CompilerParams(vmem_limit_bytes=LIMIT),
        name="form_column",
    )(parts, panel, *smalls)


def diagonal_kernel(base, *refs):
    parts, (diagonal, sums) = refs[:-2], refs[-2:]
    sums[...] = total([part[1:] for part in parts])
    diagonal[...] = (base[...] - total([part[0] for part in parts])).astype(BF16)


def form_diagonal(base, parts):
    return pl.pallas_call(
        diagonal_kernel,
        out_shape=[
            jax.ShapeDtypeStruct(base.shape, BF16),
            jax.ShapeDtypeStruct((2,) + base.shape, F32),
        ],
        in_specs=[VMEM] * (1 + len(parts)),
        out_specs=[VMEM] * 2,
        compiler_params=pltpu.CompilerParams(vmem_limit_bytes=LIMIT),
        name="form_diagonal",
    )(base, *parts)


def sum_kernel(*refs):
    refs[-1][...] = (-total([ref[...] for ref in refs[:-1]])).astype(BF16)


def form_sum(parts):
    return pl.pallas_call(
        sum_kernel,
        out_shape=jax.ShapeDtypeStruct(parts[0].shape, BF16),
        in_specs=[VMEM] * len(parts),
        out_specs=VMEM,
        compiler_params=pltpu.CompilerParams(vmem_limit_bytes=LIMIT),
        name="form_sum",
    )(*parts)


def choose_kernel(parent_two, ours, theirs, out):
    core = lax.axis_index(CORE)
    for at in range(out.shape[0]):
        out[at] = jnp.where(parent_two[2 * at + core] % 2 == core, ours[...], theirs[...])


def choose(nodes, parent_two, ours, theirs):
    return pl.pallas_call(
        choose_kernel,
        out_shape=jax.ShapeDtypeStruct((nodes,) + ours.shape, BF16),
        in_specs=[SMEM] + [VMEM] * 2,
        out_specs=VMEM,
        compiler_params=pltpu.CompilerParams(vmem_limit_bytes=LIMIT),
        name="choose",
    )(parent_two, ours, theirs)


def last_kernel(parent_two, link, base, diagonals, sums, upper, diagonal_two):
    chip, core = lax.axis_index(CHIP), lax.axis_index(CORE)
    near = diagonals[parent_two[2 * chip + core] // 2]
    parent_term = jnp.dot(near, link[...], preferred_element_type=F32)
    upper[...] = (sums[0] - parent_term).astype(BF16)
    term = lax.dot_general(
        link[...], upper[...], (((0,), (0,)), ((), ())), preferred_element_type=F32
    )
    diagonal_two[...] = (base[...] - term + sums[1]).astype(BF16)


def form_last(parent_two, link, base, diagonals, sums):
    return pl.pallas_call(
        last_kernel,
        out_shape=[jax.ShapeDtypeStruct(link.shape, BF16)] * 2,
        in_specs=[SMEM] + [VMEM] * 4,
        out_specs=[VMEM] * 2,
        compiler_params=pltpu.CompilerParams(vmem_limit_bytes=LIMIT),
        name="form_last",
    )(parent_two, link, base, diagonals, sums)


def level_one(rows_one, inverse, pieces):
    nodes, group, tile = pieces[0].shape[0], pieces[0].shape[1], pieces[0].shape[2]
    count = len(pieces)
    per_row = group * count
    flops = 2 * nodes * per_row * per_row * tile**3
    return pl.pallas_call(
        functools.partial(level_one_kernel, nodes, count),
        out_shape=jax.ShapeDtypeStruct((nodes, per_row, tile, tile), BF16),
        in_specs=[SMEM] + [VMEM] * (1 + count),
        out_specs=VMEM,
        compiler_params=pltpu.CompilerParams(vmem_limit_bytes=LIMIT),
        cost_estimate=pl.CostEstimate(flops=flops, bytes_accessed=12 << 20, transcendentals=0),
        name="level_one",
    )(rows_one, inverse, *pieces)


def form_near(parent_two, order_two, own, sibling, ours, theirs, factors):
    nodes, tiles = ours.shape[0], ours.shape[1:]
    choices = [len(f) for f in factors]
    return pl.pallas_call(
        functools.partial(near_kernel, nodes, choices),
        out_shape=[
            jax.ShapeDtypeStruct(ours.shape, BF16),
            jax.ShapeDtypeStruct((nodes,) + tiles[1:], BF16),
            jax.ShapeDtypeStruct((2,) + own.shape, BF16),
        ],
        in_specs=[SMEM] * 2 + [ANY] * 2 + [VMEM] * (2 + sum(choices)),
        out_specs=[VMEM] * 3,
        scratch_shapes=[pltpu.SemaphoreType.DMA((2 * PARTS,))],
        compiler_params=pltpu.CompilerParams(vmem_limit_bytes=LIMIT),
        name="form_near",
    )(parent_two, order_two, own, sibling, ours, theirs, *sum(factors, []))


def level_two(rows_one, parent_two, order_two, inverse, near, upper, pieces, factors):
    nodes, group, tile = pieces[0].shape[0], pieces[0].shape[1], pieces[0].shape[2]
    count = len(pieces)
    per_row = group * count
    flops = 2 * nodes * per_row * (per_row + 3) * tile**3
    choices = [len(f) for f in factors]
    return pl.pallas_call(
        functools.partial(level_two_kernel, nodes, count, choices),
        out_shape=[jax.ShapeDtypeStruct((per_row, tile, tile), BF16)] * nodes
        + [jax.ShapeDtypeStruct((2, tile, tile), BF16)] * nodes,
        in_specs=[SMEM] * 3 + [VMEM] * (3 + count + sum(choices)),
        out_specs=[VMEM] * (2 * nodes),
        compiler_params=pltpu.CompilerParams(vmem_limit_bytes=LIMIT),
        cost_estimate=pl.CostEstimate(flops=flops, bytes_accessed=16 << 20, transcendentals=0),
        name="level_two",
    )(rows_one, parent_two, order_two, inverse, near, upper, *pieces, *sum(factors, []))


def exchange(x, axis, step):
    size = lax.axis_size(axis)
    return lax.ppermute(x, axis, [(i, i ^ step) for i in range(size)])


def spread(x, axis):
    return [x] + [exchange(x, axis, s) for s in range(1, lax.axis_size(axis))]


def after(x, *others):
    return lax.optimization_barrier((x,) + others)[0]


def together(*arrays):
    return lax.optimization_barrier(arrays)


def halves(panel, axis):
    rows = lax.axis_size(axis)
    return panel.reshape((rows, panel.shape[0] // rows) + panel.shape[1:])


def swap(blocks, axis):
    return lax.all_to_all(blocks, axis, 0, 0, tiled=True)


def total(parts):
    return functools.reduce(jnp.add, [part.astype(F32) for part in parts])


def local(
    inverse_top, rows_one, panel_one, base_one, parent_two, order_two, panel_two, link_two, base_two
):
    chip, core = lax.axis_index(CHIP), lax.axis_index(CORE)
    nodes = lax.axis_size(CHIP)
    line = nodes == 4
    payload = jnp.concatenate([panel_two[0], link_two], axis=0)
    near = exchange(payload, CHIP, 1)
    if line:
        inner = lax.ppermute(payload, CHIP, [(1, 2), (2, 1)])
    else:
        inner = [exchange(payload, CHIP, t) for t in range(2, nodes)]
    sibling = exchange(inverse_top, CORE, 1)
    quarters = swap(halves(panel_one[0], ROW), ROW)
    kept, *sends = cut_groups(panel_two[0], lax.axis_size(ROW))
    quarters, near, inner, sends = together(quarters, near, inner, sends)
    blocks_one = swap(quarters, CHIP)
    groups = [kept] + [exchange(send, ROW, s + 1) for s, send in enumerate(sends)]
    blocks_one, groups = together(blocks_one, groups)
    quarters_two = join_groups(groups)
    pieces_one = spread(blocks_one, ROW)
    inverse = pair(inverse_top, after(sibling, blocks_one))
    quarters_two, payload_late, near_late, inner_late = together(
        quarters_two, payload, near, inner, blocks_one
    )[:4]
    blocks_two = swap(quarters_two, CHIP)
    over = out_one = ()
    if line:
        is_end = jnp.logical_or(chip == 0, chip == nodes - 1)
        over = exchange(jnp.where(is_end, payload_late, near_late), CHIP, nodes - 1)
        out_one = lax.ppermute(inner_late, CHIP, [(1, 0), (2, 3)])
    ours = level_one(rows_one, inverse, pieces_one)
    ours, blocks_two, over, out_one = together(ours, blocks_two, over, out_one)
    theirs = exchange(ours, CORE, 1)
    parts_one = swap(ours, CHIP)
    pieces_two = spread(blocks_two, ROW)
    if line:
        factors = [[payload], [near], [over, out_one], [inner, over]]
    else:
        factors = [[f] for f in [payload, near, *inner]]
    near_two, upper_part, inverse = form_near(
        parent_two, order_two, inverse_top, sibling, ours, theirs, factors
    )
    outs = level_two(
        rows_one, parent_two, order_two, inverse, near_two, upper_part, pieces_two, factors
    )
    columns, smalls = outs[:nodes], outs[nodes:]
    parts_small = [smalls[0]] + [exchange(smalls[t], CHIP, t) for t in range(1, nodes)]
    first = [exchange(columns[t], CHIP, t) for t in range(nodes // 2 + 1, nodes)]
    *columns, token = together(*columns, parts_small[1])
    parts_two = [exchange(columns[t], CHIP, t) for t in range(1, nodes // 2 + 1)] + first
    column_one, small = form_column(parts_one, panel_one[0], parts_small)
    diagonal_one, sums = form_diagonal(base_one[0], spread(small, ROW))
    chosen = choose(nodes, parent_two, diagonal_one, exchange(diagonal_one, CORE, 1))
    diagonals = swap(chosen, CHIP)
    upper, diagonal_two = form_last(parent_two, link_two[0], base_two[0], diagonals, sums)
    column_two = form_sum([columns[0], *parts_two])
    return (
        column_one[None],
        diagonal_one[None],
        column_two[None],
        upper[None],
        diagonal_two[None],
    )


def solution(mesh):
    rows, columns = mesh.devices.shape
    fine = Mesh(mesh.devices.reshape(rows, columns // 2, 2), (ROW, CHIP, CORE))
    col = (CHIP, CORE)
    return jax.shard_map(
        local,
        mesh=fine,
        in_specs=(
            P(ROW, col, None, None),
            P(),
            P(col, ROW, None, None),
            P(col, None, None),
            P(),
            P(),
            P(col, ROW, None, None),
            P(col, None, None),
            P(col, None, None),
        ),
        out_specs=(
            P(col, ROW, None, None),
            P(col, None, None),
            P(col, ROW, None, None),
            P(col, None, None),
            P(col, None, None),
        ),
        check_vma=False,
    )
```

time: 131 us -> 124 us (0.947)
  blocking collectives: 15 us -> 0 us
  waiting for transfers between devices: 26.2 us -> 37.6 us
  local copies, waits for them, and re-layouts: 2.8 us -> 11.5 us
  starting transfers between devices: 56.9 us -> 52.1 us
  other arithmetic: 5.59 us -> 1.03 us
  Pallas kernels: 23 us -> 19.5 us
    all_to_all x1 -> x0, blocking collectives: 15 us -> none  [swap(): return lax.all_to_all(blocks, axis, 0, 0, tiled=True)]
    unnamed x42 -> x36, local copies, waits for them, and re-layouts: 1.99 us -> 11.5 us
    pallas_call x2 -> x8, Pallas kernels: 2.04 us -> 11 us  [the longest x1 3.76 us: form_near(): pl.pallas_call(functools.partial(near_kernel, nodes, choices), out_shape=...]
    pallas_call x1, Pallas kernels: 12.3 us -> 3.57 us  [level_two(): pl.pallas_call(functools.partial(level_two_kernel, nodes, count, choices)...]
    all_to_all x3 -> x5, starting transfers between devices: 11.7 us -> 20.2 us  [swap(): return lax.all_to_all(blocks, axis, 0, 0, tiled=True)]
    ppermute x25 -> x23, starting transfers between devices: 37 us -> 29.9 us  [exchange(): return lax.ppermute(x, axis, [(i, i ^ step) for i in range(size)])]
    ppermute x2 -> x0, starting transfers between devices: 6.29 us -> none  [the longest x1 5.62 us: local(): out_two = lax.ppermute(payload_late, CHIP, [(0, 3), (3, 0)])]
    all_to_all x3 -> x5, waiting for transfers between devices: 0.01 us -> 6.24 us  [swap(): return lax.all_to_all(blocks, axis, 0, 0, tiled=True)]
  transfers between devices with their start and end apart: 32 -> 30, of which waited for: 8 -> 14; matrix products, arithmetic and copies ran while one was open for 5% -> 1% of each run, Pallas kernels for 17% -> 14%
where the time goes in v4:
time: 124 us; the launch traced here: 123 us
  starting transfers between devices  52.1 us (42%)
  waiting for transfers between devices  37.6 us (30%)
  Pallas kernels  19.5 us (16%)
  local copies, waits for them, and re-layouts  11.5 us (9%)
    ppermute x23, starting transfers between devices, exchange(): return lax.ppermute(x, axis, [(i, i ^ step) for i in range(size)])  29.9 us
    ppermute x23, waiting for transfers between devices, exchange(): return lax.ppermute(x, axis, [(i, i ^ step) for i in range(size)])  29.9 us
    all_to_all x5, starting transfers between devices, swap(): return lax.all_to_all(blocks, axis, 0, 0, tiled=True)  20.2 us
    unnamed x36, local copies, waits for them, and re-layouts  11.5 us
    all_to_all x5, waiting for transfers between devices, swap(): return lax.all_to_all(blocks, axis, 0, 0, tiled=True)  6.24 us
    pallas_call x1, Pallas kernels, level_one(): pl.pallas_call(functools.partial(level_one_kernel, nodes, count), out_sha...  3.94 us
    pallas_call x1, Pallas kernels, form_near(): pl.pallas_call(functools.partial(near_kernel, nodes, choices), out_shape=...  3.76 us
    pallas_call x1, Pallas kernels, level_two(): pl.pallas_call(functools.partial(level_two_kernel, nodes, count, choices)...  3.57 us
  transfers between devices with their start and end apart: 30, of which 14 were waited for; matrix products, arithmetic and copies ran while one was open for 1% of the time, Pallas kernels for 14%

profile of v4, /device:TPU:0, one launch (start us, length us, event | category | flops | bytes accessed | tf_op | source)
XLA Modules:
  0.0 122.6 jit_solution(6946276499490369203)
XLA Ops:
  2.1 2.7 %collective-permute-start.1 = (bf16[9,128,128]{2,1,0:T(8,128)(2,1)S(1)}, bf16[9,128,128]{2,1,0:T(8,128)(2,1)S(1)}, u32[]{:S(2)}, u32[]{:S(2)}) collective-permute-start(bf16[9,128,128]{2,1,0:T(8,128)(2,1)S(1)} %pad_maximum_fusion.refs_0_.refs_4_), channel_id=1, source_target_pairs={{0,2},{2,0},{4,6},{6,4},{1,3},{3,1},{5,7},{7,5},{8,10},{10,8},{12,... | collective-permute-start | bytes 884744 | tf_op jit(solution)/shard_map/ppermute | solution.py:357
  5.5 4.1 %all-to-all-start = ((bf16[4,2,128,128]{3,2,1,0:T(8,128)(2,1)}), bf16[4,2,128,128]{3,2,1,0:T(8,128)(2,1)}, u32[]{:S(2)}, u32[]{:S(2)}) async-start(bf16[4,2,128,128]{3,2,1,0:T(8,128)(2,1)} %bitcast.13), calls=%async_computation | async-start | bytes 524288 | tf_op jit(solution)/shard_map/all_to_all | solution.py:378
  10.5 5.1 %all-to-all-done = bf16[4,2,128,128]{3,2,1,0:T(8,128)(2,1)} async-done(((bf16[4,2,128,128]{3,2,1,0:T(8,128)(2,1)}), bf16[4,2,128,128]{3,2,1,0:T(8,128)(2,1)}, u32[]{:S(2)}, u32[]{:S(2)}) %all-to-all-start) | async-done | bytes 262176 | tf_op jit(solution)/shard_map/all_to_all | solution.py:378
  15.6 5.4 %all-to-all-start.1 = ((bf16[4,2,128,128]{3,2,1,0:T(8,128)(2,1)}), bf16[4,2,128,128]{3,2,1,0:T(8,128)(2,1)S(1)}, u32[]{:S(2)}, u32[]{:S(2)}) async-start(bf16[4,2,128,128]{3,2,1,0:T(8,128)(2,1)} %all-to-all-done), calls=%async_computation.1 | async-start | bytes 524288 | tf_op jit(solution)/shard_map/all_to_all | solution.py:378
  22.9 1.6 %collective-permute-start.5 = (bf16[2,128,128]{2,1,0:T(8,128)(2,1)S(1)}, bf16[2,128,128]{2,1,0:T(8,128)(2,1)S(1)}, u32[]{:S(2)}, u32[]{:S(2)}) collective-permute-start(bf16[2,128,128]{2,1,0:T(8,128)(2,1)S(1)} %get-tuple-element.56), channel_id=1, source_target_pairs={{0,24},{8,16},{16,8},{24,0},{1,25},{9,17},{17,9},{25,1},{2,26},{10... | collective-permute-start | bytes 196616 | tf_op jit(solution)/shard_map/ppermute | solution.py:357
  26.6 1.5 %collective-permute-done.5.refs_3_ = bf16[2,128,128]{2,1,0:T(8,128)(2,1)S(1)} collective-permute-done((bf16[2,128,128]{2,1,0:T(8,128)(2,1)S(1)}, bf16[2,128,128]{2,1,0:T(8,128)(2,1)S(1)}, u32[]{:S(2)}, u32[]{:S(2)}) %collective-permute-start.5) | collective-permute-done | bytes 65568 | tf_op jit(solution)/shard_map/ppermute | solution.py:357
  31.2 1.4 %collective-permute-start.8 = (bf16[4,2,128,128]{3,2,1,0:T(8,128)(2,1)S(1)}, bf16[4,2,128,128]{3,2,1,0:T(8,128)(2,1)S(1)}, u32[]{:S(2)}, u32[]{:S(2)}) collective-permute-start(bf16[4,2,128,128]{3,2,1,0:T(8,128)(2,1)S(1)} %all-to-all-done.1.refs_0_), channel_id=1, source_target_pairs={{0,24},{8,16},{16,8},{24,0},{1,25},{9,17},{17,9},{25,1},{2,26},{10... | collective-permute-start | bytes 786440 | tf_op jit(solution)/shard_map/ppermute | solution.py:357
  33.4 4.0 %all-to-all-start.2 = ((bf16[4,2,128,128]{3,2,1,0:T(8,128)(2,1)}), bf16[4,2,128,128]{3,2,1,0:T(8,128)(2,1)S(1)}, u32[]{:S(2)}, u32[]{:S(2)}) async-start(bf16[4,2,128,128]{3,2,1,0:T(8,128)(2,1)} %join_groups.1), calls=%async_computation.2 | async-start | bytes 524288 | tf_op jit(solution)/shard_map/all_to_all | solution.py:378
  37.4 3.9 %collective-permute-start.9 = (bf16[9,128,128]{2,1,0:T(8,128)(2,1)S(1)}, bf16[9,128,128]{2,1,0:T(8,128)(2,1)S(1)}, u32[]{:S(2)}, u32[]{:S(2)}) collective-permute-start(bf16[9,128,128]{2,1,0:T(8,128)(2,1)S(1)} %broadcast_select_fusion), channel_id=1, source_target_pairs={{0,6},{2,4},{4,2},{6,0},{1,7},{3,5},{5,3},{7,1},{8,14},{10,12},{12... | collective-permute-start | bytes 884744 | tf_op jit(solution)/shard_map/ppermute | solution.py:357
  42.6 2.2 %copy-done = bf16[16,8,128,128]{3,2,1,0:T(8,128)(2,1)S(1)} copy-done((bf16[16,8,128,128]{3,2,1,0:T(8,128)(2,1)S(1)}, bf16[16,8,128,128]{3,2,1,0:T(8,128)(2,1)}, u32[]{:S(2)}) %copy-start) | copy-done | bytes 4194328
  44.8 2.4 %pair.1.inverse = bf16[2,16,8,128,128]{4,3,2,1,0:T(8,128)(2,1)S(1)} custom-call(bf16[16,8,128,128]{3,2,1,0:T(8,128)(2,1)S(1)} %copy-done, bf16[16,8,128,128]{3,2,1,0:T(8,128)(2,1)} %collective-permute-done.sibling), custom_call_target="tpu_custom_call" | custom-call | tf_op jit(solution)/shard_map/pair/pallas_call | solution.py:51
  50.5 3.9 %level_one.1.ours = bf16[4,8,128,128]{3,2,1,0:T(8,128)(2,1)} custom-call(s32[8,32]{1,0:T(8,128)S(1)} %copy-done.12, bf16[2,16,8,128,128]{4,3,2,1,0:T(8,128)(2,1)S(1)} %pair.1.inverse, bf16[4,2,128,128]{3,2,1,0:T(8,128)(2,1)S(1)} %all-to-all-done.1.refs_0_, bf16[4,2,128,128]{3,2,1,0:T(8,128)(2,1)S(1)} %collective-permute-done.6.refs_1_, ...), custom_call_target="tpu_custom_call" | custom-call | flops 1073741824 | bytes 12582912 | tf_op jit(solution)/shard_map/level_one/pallas_call | solution.py:308
  54.4 1.4 %collective-permute-done.10.refs_3_.refs_7_ = bf16[9,128,128]{2,1,0:T(8,128)(2,1)S(1)} collective-permute-done((bf16[9,128,128]{2,1,0:T(8,128)(2,1)S(1)}, bf16[9,128,128]{2,1,0:T(8,128)(2,1)S(1)}, u32[]{:S(2)}, u32[]{:S(2)}) %collective-permute-start.10) | collective-permute-done | bytes 294944 | tf_op jit(solution)/shard_map/ppermute | solution.py:415
  55.9 3.5 %all-to-all-start.3 = ((bf16[4,8,128,128]{3,2,1,0:T(8,128)(2,1)}), bf16[4,8,128,128]{3,2,1,0:T(8,128)(2,1)S(1)}, u32[]{:S(2)}, u32[]{:S(2)}) async-start(bf16[4,8,128,128]{3,2,1,0:T(8,128)(2,1)} %level_one.1.ours), calls=%async_computation.3 | async-start | bytes 2097152 | tf_op jit(solution)/shard_map/all_to_all | solution.py:378
  61.7 1.3 %collective-permute-start.14 = (bf16[4,2,128,128]{3,2,1,0:T(8,128)(2,1)S(1)}, bf16[4,2,128,128]{3,2,1,0:T(8,128)(2,1)S(1)}, u32[]{:S(2)}, u32[]{:S(2)}) collective-permute-start(bf16[4,2,128,128]{3,2,1,0:T(8,128)(2,1)S(1)} %all-to-all-done.2.refs_0_), channel_id=1, source_target_pairs={{0,24},{8,16},{16,8},{24,0},{1,25},{9,17},{17,9},{25,1},{2,26},{10... | collective-permute-start | bytes 786440 | tf_op jit(solution)/shard_map/ppermute | solution.py:357
  63.0 2.2 %copy-done.1 = bf16[16,8,128,128]{3,2,1,0:T(8,128)(2,1)S(1)} copy-done((bf16[16,8,128,128]{3,2,1,0:T(8,128)(2,1)S(1)}, bf16[16,8,128,128]{3,2,1,0:T(8,128)(2,1)}, u32[]{:S(2)}) %copy-start.1) | copy-done | bytes 4194328
  65.2 3.8 %form_near.1 = (bf16[4,8,128,128]{3,2,1,0:T(8,128)(2,1)S(1)}, bf16[4,128,128]{2,1,0:T(8,128)(2,1)S(1)}, bf16[2,16,8,128,128]{4,3,2,1,0:T(8,128)(2,1)S(1)}) custom-call(s32[8]{0:T(128)S(1)} %copy-done.14, s32[8,32]{1,0:T(8,128)S(1)} %copy-done.13, bf16[16,8,128,128]{3,2,1,0:T(8,128)(2,1)S(1)} %copy-done.1, ...), custom_call_target="tpu_custom_call" | custom-call | tf_op jit(solution)/shard_map/form_near/pallas_call | solution.py:322
  69.0 4.2 %collective-permute-done.13.refs_2_ = bf16[4,2,128,128]{3,2,1,0:T(8,128)(2,1)S(1)} collective-permute-done((bf16[4,2,128,128]{3,2,1,0:T(8,128)(2,1)S(1)}, bf16[4,2,128,128]{3,2,1,0:T(8,128)(2,1)S(1)}, u32[]{:S(2)}, u32[]{:S(2)}) %collective-permute-start.13) | collective-permute-done | bytes 262176 | tf_op jit(solution)/shard_map/ppermute | solution.py:357
  73.3 1.4 %collective-permute-done.14.refs_3_ = bf16[4,2,128,128]{3,2,1,0:T(8,128)(2,1)S(1)} collective-permute-done((bf16[4,2,128,128]{3,2,1,0:T(8,128)(2,1)S(1)}, bf16[4,2,128,128]{3,2,1,0:T(8,128)(2,1)S(1)}, u32[]{:S(2)}, u32[]{:S(2)}) %collective-permute-start.14) | collective-permute-done | bytes 262176 | tf_op jit(solution)/shard_map/ppermute | solution.py:357
  74.7 3.6 %level_two.1 = (bf16[8,128,128]{2,1,0:T(8,128)(2,1)S(1)}, bf16[8,128,128]{2,1,0:T(8,128)(2,1)S(1)}, bf16[8,128,128]{2,1,0:T(8,128)(2,1)S(1)}, bf16[8,128,128]{2,...) custom-call(s32[8,32]{1,0:T(8,128)S(1)} %copy-done.12, ...), custom_call_target="tpu_custom_call" | custom-call | flops 1476395008 | bytes 16777216 | tf_op jit(solution)/shard_map/level_two/pallas_call | solution.py:343
  80.4 1.9 %collective-permute-start.15 = (bf16[2,128,128]{2,1,0:T(8,128)(2,1)S(1)}, bf16[2,128,128]{2,1,0:T(8,128)(2,1)S(1)}, u32[]{:S(2)}, u32[]{:S(2)}) collective-permute-start(bf16[2,128,128]{2,1,0:T(8,128)(2,1)S(1)} %get-tuple-element.77), channel_id=1, source_target_pairs={{0,2},{2,0},{4,6},{6,4},{1,3},{3,1},{5,7},{7,5},{8,10},{10,8},{12,... | collective-permute-start | bytes 196616 | tf_op jit(solution)/shard_map/ppermute | solution.py:357
  82.3 2.4 %collective-permute-start.16 = (bf16[2,128,128]{2,1,0:T(8,128)(2,1)S(1)}, bf16[2,128,128]{2,1,0:T(8,128)(2,1)S(1)}, u32[]{:S(2)}, u32[]{:S(2)}) collective-permute-start(bf16[2,128,128]{2,1,0:T(8,128)(2,1)S(1)} %get-tuple-element.78), channel_id=1, source_target_pairs={{0,4},{2,6},{4,0},{6,2},{1,5},{3,7},{5,1},{7,3},{8,12},{10,14},{12... | collective-permute-start | bytes 196616 | tf_op jit(solution)/shard_map/ppermute | solution.py:357
  84.7 1.7 %collective-permute-done.15.refs_1_ = bf16[2,128,128]{2,1,0:T(8,128)(2,1)S(1)} collective-permute-done((bf16[2,128,128]{2,1,0:T(8,128)(2,1)S(1)}, bf16[2,128,128]{2,1,0:T(8,128)(2,1)S(1)}, u32[]{:S(2)}, u32[]{:S(2)}) %collective-permute-start.15) | collective-permute-done | bytes 65568 | tf_op jit(solution)/shard_map/ppermute | solution.py:357
  86.5 2.9 %collective-permute-done.16.refs_2_ = bf16[2,128,128]{2,1,0:T(8,128)(2,1)S(1)} collective-permute-done((bf16[2,128,128]{2,1,0:T(8,128)(2,1)S(1)}, bf16[2,128,128]{2,1,0:T(8,128)(2,1)S(1)}, u32[]{:S(2)}, u32[]{:S(2)}) %collective-permute-start.16) | collective-permute-done | bytes 65568 | tf_op jit(solution)/shard_map/ppermute | solution.py:357
  89.4 1.4 %collective-permute-done.17.refs_3_ = bf16[2,128,128]{2,1,0:T(8,128)(2,1)S(1)} collective-permute-done((bf16[2,128,128]{2,1,0:T(8,128)(2,1)S(1)}, bf16[2,128,128]{2,1,0:T(8,128)(2,1)S(1)}, u32[]{:S(2)}, u32[]{:S(2)}) %collective-permute-start.17) | collective-permute-done | bytes 65568 | tf_op jit(solution)/shard_map/ppermute | solution.py:357
  92.6 1.4 %collective-permute-start.19 = (bf16[3,128,128]{2,1,0:T(8,128)(2,1)S(1)}, bf16[3,128,128]{2,1,0:T(8,128)(2,1)S(1)}, u32[]{:S(2)}, u32[]{:S(2)}) collective-permute-start(bf16[3,128,128]{2,1,0:T(8,128)(2,1)S(1)} %get-tuple-element.81.refs_0_), channel_id=1, source_target_pairs={{0,16},{8,24},{16,0},{24,8},{1,17},{9,25},{17,1},{25,9},{2,18},{10... | collective-permute-start | bytes 294920 | tf_op jit(solution)/shard_map/ppermute | solution.py:357
  95.3 1.7 %collective-permute-start.23 = (bf16[8,128,128]{2,1,0:T(8,128)(2,1)}, bf16[8,128,128]{2,1,0:T(8,128)(2,1)S(1)}, u32[]{:S(2)}, u32[]{:S(2)}) collective-permute-start(bf16[8,128,128]{2,1,0:T(8,128)(2,1)} %copy-done.17), channel_id=1, source_target_pairs={{0,6},{2,4},{4,2},{6,0},{1,7},{3,5},{5,3},{7,1},{8,14},{10,12},{12... | collective-permute-start | bytes 786440 | tf_op jit(solution)/shard_map/ppermute | solution.py:357
  97.3 2.3 %collective-permute-start.22 = (bf16[8,128,128]{2,1,0:T(8,128)(2,1)}, bf16[8,128,128]{2,1,0:T(8,128)(2,1)S(1)}, u32[]{:S(2)}, u32[]{:S(2)}) collective-permute-start(bf16[8,128,128]{2,1,0:T(8,128)(2,1)} %copy-done.15), channel_id=1, source_target_pairs={{0,4},{2,6},{4,0},{6,2},{1,5},{3,7},{5,1},{7,3},{8,12},{10,14},{12... | collective-permute-start | bytes 786440 | tf_op jit(solution)/shard_map/ppermute | solution.py:357
  100.3 1.4 %collective-permute-done.24.theirs = bf16[128,128]{1,0:T(8,128)(2,1)S(1)} collective-permute-done((bf16[128,128]{1,0:T(8,128)(2,1)}, bf16[128,128]{1,0:T(8,128)(2,1)S(1)}, u32[]{:S(2)}, u32[]{:S(2)}) %collective-permute-start.24) | collective-permute-done | bytes 32800 | tf_op jit(solution)/shard_map/ppermute | solution.py:357
  103.7 3.3 %all-to-all-start.4 = ((bf16[4,128,128]{2,1,0:T(8,128)(2,1)}), bf16[4,128,128]{2,1,0:T(8,128)(2,1)S(1)}, u32[]{:S(2)}, u32[]{:S(2)}) async-start(bf16[4,128,128]{2,1,0:T(8,128)(2,1)} %choose.1), calls=%async_computation.4 | async-start | bytes 262144 | tf_op jit(solution)/shard_map/all_to_all | solution.py:378
  108.0 12.3 %collective-permute-done.22.refs_2_ = bf16[8,128,128]{2,1,0:T(8,128)(2,1)S(1)} collective-permute-done((bf16[8,128,128]{2,1,0:T(8,128)(2,1)}, bf16[8,128,128]{2,1,0:T(8,128)(2,1)S(1)}, u32[]{:S(2)}, u32[]{:S(2)}) %collective-permute-start.22) | collective-permute-done | bytes 262176 | tf_op jit(solution)/shard_map/ppermute | solution.py:357
  121.2 1.5 %form_last.1 = (bf16[128,128]{1,0:T(8,128)(2,1)}, bf16[128,128]{1,0:T(8,128)(2,1)}) custom-call(s32[8]{0:T(128)S(1)} %copy-done.14, bf16[128,128]{1,0:T(8,128)(2,1)S(1)} %bitcast.15, f32[128,128]{1,0:T(8,128)S(1)} %bitcast.17, bf16[4,128,128]{2,1,0:T(8,128)(2,1)S(1)} %all-to-all-done.4.diagonals, f32[2,128,128]{2,1,0:T(8,128)S(1)} %get-tuple-element.90.sums), custom_call_target="tpu_custom_call" | custom-call | tf_op jit(solution)/shard_map/form_last/pallas_call | solution.py:293
  (77 shorter events, 28.1 us)
Async XLA Ops:
  0.6 40.6 %collective-permute-start = (bf16[16,8,128,128]{3,2,1,0:T(8,128)(2,1)}, bf16[16,8,128,128]{3,2,1,0:T(8,128)(2,1)}, u32[]{:S(2)}, u32[]{:S(2)}) collective-permute-start(bf16[16,8,128,128]{3,2,1,0:T(8,128)(2,1)} %own.3), channel_id=1, source_target_pairs={{0,1},{1,0},{2,3},{3,2},{4,5},{5,4},{6,7},{7,6},{8,9},{9,8},{10,11... | collective-permute-start | bytes 12582920 | tf_op jit(solution)/shard_map/ppermute | solution.py:357
  2.1 13.5 %collective-permute-start.1 = (bf16[9,128,128]{2,1,0:T(8,128)(2,1)S(1)}, bf16[9,128,128]{2,1,0:T(8,128)(2,1)S(1)}, u32[]{:S(2)}, u32[]{:S(2)}) collective-permute-start(bf16[9,128,128]{2,1,0:T(8,128)(2,1)S(1)} %pad_maximum_fusion.refs_0_.refs_4_), channel_id=1, source_target_pairs={{0,2},{2,0},{4,6},{6,4},{1,3},{3,1},{5,7},{7,5},{8,10},{10,8},{12,... | collective-permute-start | bytes 884744 | tf_op jit(solution)/shard_map/ppermute | solution.py:357
  4.8 10.8 %collective-permute-start.2 = (bf16[9,128,128]{2,1,0:T(8,128)(2,1)S(1)}, bf16[9,128,128]{2,1,0:T(8,128)(2,1)S(1)}, u32[]{:S(2)}, u32[]{:S(2)}) collective-permute-start(bf16[9,128,128]{2,1,0:T(8,128)(2,1)S(1)} %pad_maximum_fusion.refs_0_.refs_4_), channel_id=1, source_target_pairs={{2,4},{4,2},{3,5},{5,3},{10,12},{12,10},{11,13},{13,11},{18,20},{2... | collective-permute-start | bytes 884744 | tf_op jit(solution)/shard_map/ppermute | solution.py:394
  5.5 10.2 %all-to-all-start = ((bf16[4,2,128,128]{3,2,1,0:T(8,128)(2,1)}), bf16[4,2,128,128]{3,2,1,0:T(8,128)(2,1)}, u32[]{:S(2)}, u32[]{:S(2)}) async-start(bf16[4,2,128,128]{3,2,1,0:T(8,128)(2,1)} %bitcast.13), calls=%async_computation | async-start | bytes 524288 | tf_op jit(solution)/shard_map/all_to_all | solution.py:378
  15.6 13.5 %all-to-all-start.1 = ((bf16[4,2,128,128]{3,2,1,0:T(8,128)(2,1)}), bf16[4,2,128,128]{3,2,1,0:T(8,128)(2,1)S(1)}, u32[]{:S(2)}, u32[]{:S(2)}) async-start(bf16[4,2,128,128]{3,2,1,0:T(8,128)(2,1)} %all-to-all-done), calls=%async_computation.1 | async-start | bytes 524288 | tf_op jit(solution)/shard_map/all_to_all | solution.py:378
  21.0 4.7 %collective-permute-start.3 = (bf16[2,128,128]{2,1,0:T(8,128)(2,1)S(1)}, bf16[2,128,128]{2,1,0:T(8,128)(2,1)S(1)}, u32[]{:S(2)}, u32[]{:S(2)}) collective-permute-start(bf16[2,128,128]{2,1,0:T(8,128)(2,1)S(1)} %get-tuple-element.54), channel_id=1, source_target_pairs={{0,8},{8,0},{16,24},{24,16},{1,9},{9,1},{17,25},{25,17},{2,10},{10... | collective-permute-start | bytes 196616 | tf_op jit(solution)/shard_map/ppermute | solution.py:357
  22.3 4.3 %collective-permute-start.4 = (bf16[2,128,128]{2,1,0:T(8,128)(2,1)S(1)}, bf16[2,128,128]{2,1,0:T(8,128)(2,1)S(1)}, u32[]{:S(2)}, u32[]{:S(2)}) collective-permute-start(bf16[2,128,128]{2,1,0:T(8,128)(2,1)S(1)} %get-tuple-element.55), channel_id=1, source_target_pairs={{0,16},{8,24},{16,0},{24,8},{1,17},{9,25},{17,1},{25,9},{2,18},{10... | collective-permute-start | bytes 196616 | tf_op jit(solution)/shard_map/ppermute | solution.py:357
  22.9 5.2 %collective-permute-start.5 = (bf16[2,128,128]{2,1,0:T(8,128)(2,1)S(1)}, bf16[2,128,128]{2,1,0:T(8,128)(2,1)S(1)}, u32[]{:S(2)}, u32[]{:S(2)}) collective-permute-start(bf16[2,128,128]{2,1,0:T(8,128)(2,1)S(1)} %get-tuple-element.56), channel_id=1, source_target_pairs={{0,24},{8,16},{16,8},{24,0},{1,25},{9,17},{17,9},{25,1},{2,26},{10... | collective-permute-start | bytes 196616 | tf_op jit(solution)/shard_map/ppermute | solution.py:357
  29.2 18.0 %collective-permute-start.6 = (bf16[4,2,128,128]{3,2,1,0:T(8,128)(2,1)S(1)}, bf16[4,2,128,128]{3,2,1,0:T(8,128)(2,1)S(1)}, u32[]{:S(2)}, u32[]{:S(2)}) collective-permute-start(bf16[4,2,128,128]{3,2,1,0:T(8,128)(2,1)S(1)} %all-to-all-done.1.refs_0_), channel_id=1, source_target_pairs={{0,8},{8,0},{16,24},{24,16},{1,9},{9,1},{17,25},{25,17},{2,10},{10... | collective-permute-start | bytes 786440 | tf_op jit(solution)/shard_map/ppermute | solution.py:357
  30.3 16.8 %collective-permute-start.7 = (bf16[4,2,128,128]{3,2,1,0:T(8,128)(2,1)S(1)}, bf16[4,2,128,128]{3,2,1,0:T(8,128)(2,1)S(1)}, u32[]{:S(2)}, u32[]{:S(2)}) collective-permute-start(bf16[4,2,128,128]{3,2,1,0:T(8,128)(2,1)S(1)} %all-to-all-done.1.refs_0_), channel_id=1, source_target_pairs={{0,16},{8,24},{16,0},{24,8},{1,17},{9,25},{17,1},{25,9},{2,18},{10... | collective-permute-start | bytes 786440 | tf_op jit(solution)/shard_map/ppermute | solution.py:357
  31.2 16.6 %collective-permute-start.8 = (bf16[4,2,128,128]{3,2,1,0:T(8,128)(2,1)S(1)}, bf16[4,2,128,128]{3,2,1,0:T(8,128)(2,1)S(1)}, u32[]{:S(2)}, u32[]{:S(2)}) collective-permute-start(bf16[4,2,128,128]{3,2,1,0:T(8,128)(2,1)S(1)} %all-to-all-done.1.refs_0_), channel_id=1, source_target_pairs={{0,24},{8,16},{16,8},{24,0},{1,25},{9,17},{17,9},{25,1},{2,26},{10... | collective-permute-start | bytes 786440 | tf_op jit(solution)/shard_map/ppermute | solution.py:357
  33.4 22.5 %all-to-all-start.2 = ((bf16[4,2,128,128]{3,2,1,0:T(8,128)(2,1)}), bf16[4,2,128,128]{3,2,1,0:T(8,128)(2,1)S(1)}, u32[]{:S(2)}, u32[]{:S(2)}) async-start(bf16[4,2,128,128]{3,2,1,0:T(8,128)(2,1)} %join_groups.1), calls=%async_computation.2 | async-start | bytes 524288 | tf_op jit(solution)/shard_map/all_to_all | solution.py:378
  37.4 17.0 %collective-permute-start.9 = (bf16[9,128,128]{2,1,0:T(8,128)(2,1)S(1)}, bf16[9,128,128]{2,1,0:T(8,128)(2,1)S(1)}, u32[]{:S(2)}, u32[]{:S(2)}) collective-permute-start(bf16[9,128,128]{2,1,0:T(8,128)(2,1)S(1)} %broadcast_select_fusion), channel_id=1, source_target_pairs={{0,6},{2,4},{4,2},{6,0},{1,7},{3,5},{5,3},{7,1},{8,14},{10,12},{12... | collective-permute-start | bytes 884744 | tf_op jit(solution)/shard_map/ppermute | solution.py:357
  41.3 14.6 %collective-permute-start.10 = (bf16[9,128,128]{2,1,0:T(8,128)(2,1)S(1)}, bf16[9,128,128]{2,1,0:T(8,128)(2,1)S(1)}, u32[]{:S(2)}, u32[]{:S(2)}) collective-permute-start(bf16[9,128,128]{2,1,0:T(8,128)(2,1)S(1)} %collective-permute-done.2.refs_4_.refs_8_), channel_id=1, source_target_pairs={{2,0},{4,6},{3,1},{5,7},{10,8},{12,14},{11,9},{13,15},{18,16},{20,... | collective-permute-start | bytes 884744 | tf_op jit(solution)/shard_map/ppermute | solution.py:415
  55.9 35.0 %all-to-all-start.3 = ((bf16[4,8,128,128]{3,2,1,0:T(8,128)(2,1)}), bf16[4,8,128,128]{3,2,1,0:T(8,128)(2,1)S(1)}, u32[]{:S(2)}, u32[]{:S(2)}) async-start(bf16[4,8,128,128]{3,2,1,0:T(8,128)(2,1)} %level_one.1.ours), calls=%async_computation.3 | async-start | bytes 2097152 | tf_op jit(solution)/shard_map/all_to_all | solution.py:378
  59.4 3.6 %collective-permute-start.11 = (bf16[4,8,128,128]{3,2,1,0:T(8,128)(2,1)}, bf16[4,8,128,128]{3,2,1,0:T(8,128)(2,1)S(1)}, u32[]{:S(2)}, u32[]{:S(2)}) collective-permute-start(bf16[4,8,128,128]{3,2,1,0:T(8,128)(2,1)} %level_one.1.ours), channel_id=1, source_target_pairs={{0,1},{1,0},{2,3},{3,2},{4,5},{5,4},{6,7},{7,6},{8,9},{9,8},{10,11... | collective-permute-start | bytes 3145736 | tf_op jit(solution)/shard_map/ppermute | solution.py:357
  59.5 9.6 %collective-permute-start.12 = (bf16[4,2,128,128]{3,2,1,0:T(8,128)(2,1)S(1)}, bf16[4,2,128,128]{3,2,1,0:T(8,128)(2,1)S(1)}, u32[]{:S(2)}, u32[]{:S(2)}) collective-permute-start(bf16[4,2,128,128]{3,2,1,0:T(8,128)(2,1)S(1)} %all-to-all-done.2.refs_0_), channel_id=1, source_target_pairs={{0,8},{8,0},{16,24},{24,16},{1,9},{9,1},{17,25},{25,17},{2,10},{10... | collective-permute-start | bytes 786440 | tf_op jit(solution)/shard_map/ppermute | solution.py:357
  60.7 12.6 %collective-permute-start.13 = (bf16[4,2,128,128]{3,2,1,0:T(8,128)(2,1)S(1)}, bf16[4,2,128,128]{3,2,1,0:T(8,128)(2,1)S(1)}, u32[]{:S(2)}, u32[]{:S(2)}) collective-permute-start(bf16[4,2,128,128]{3,2,1,0:T(8,128)(2,1)S(1)} %all-to-all-done.2.refs_0_), channel_id=1, source_target_pairs={{0,16},{8,24},{16,0},{24,8},{1,17},{9,25},{17,1},{25,9},{2,18},{10... | collective-permute-start | bytes 786440 | tf_op jit(solution)/shard_map/ppermute | solution.py:357
  61.7 13.0 %collective-permute-start.14 = (bf16[4,2,128,128]{3,2,1,0:T(8,128)(2,1)S(1)}, bf16[4,2,128,128]{3,2,1,0:T(8,128)(2,1)S(1)}, u32[]{:S(2)}, u32[]{:S(2)}) collective-permute-start(bf16[4,2,128,128]{3,2,1,0:T(8,128)(2,1)S(1)} %all-to-all-done.2.refs_0_), channel_id=1, source_target_pairs={{0,24},{8,16},{16,8},{24,0},{1,25},{9,17},{17,9},{25,1},{2,26},{10... | collective-permute-start | bytes 786440 | tf_op jit(solution)/shard_map/ppermute | solution.py:357
  69.0 52.2 %copy-start.8 = (bf16[1,128,128]{2,1,0:T(8,128)(2,1)S(1)}, bf16[1,128,128]{2,1,0:T(8,128)(2,1)}, u32[]{:S(2)}) copy-start(bf16[1,128,128]{2,1,0:T(8,128)(2,1)} %param.16) | copy-start | bytes 98308
  69.0 52.2 %copy-start.10 = (f32[1,128,128]{2,1,0:T(8,128)S(1)}, f32[1,128,128]{2,1,0:T(8,128)}, u32[]{:S(2)}) copy-start(f32[1,128,128]{2,1,0:T(8,128)} %param.17) | copy-start | bytes 196612
  80.4 6.1 %collective-permute-start.15 = (bf16[2,128,128]{2,1,0:T(8,128)(2,1)S(1)}, bf16[2,128,128]{2,1,0:T(8,128)(2,1)S(1)}, u32[]{:S(2)}, u32[]{:S(2)}) collective-permute-start(bf16[2,128,128]{2,1,0:T(8,128)(2,1)S(1)} %get-tuple-element.77), channel_id=1, source_target_pairs={{0,2},{2,0},{4,6},{6,4},{1,3},{3,1},{5,7},{7,5},{8,10},{10,8},{12,... | collective-permute-start | bytes 196616 | tf_op jit(solution)/shard_map/ppermute | solution.py:357
  82.3 7.2 %collective-permute-start.16 = (bf16[2,128,128]{2,1,0:T(8,128)(2,1)S(1)}, bf16[2,128,128]{2,1,0:T(8,128)(2,1)S(1)}, u32[]{:S(2)}, u32[]{:S(2)}) collective-permute-start(bf16[2,128,128]{2,1,0:T(8,128)(2,1)S(1)} %get-tuple-element.78), channel_id=1, source_target_pairs={{0,4},{2,6},{4,0},{6,2},{1,5},{3,7},{5,1},{7,3},{8,12},{10,14},{12... | collective-permute-start | bytes 196616 | tf_op jit(solution)/shard_map/ppermute | solution.py:357
  84.6 6.2 %collective-permute-start.17 = (bf16[2,128,128]{2,1,0:T(8,128)(2,1)S(1)}, bf16[2,128,128]{2,1,0:T(8,128)(2,1)S(1)}, u32[]{:S(2)}, u32[]{:S(2)}) collective-permute-start(bf16[2,128,128]{2,1,0:T(8,128)(2,1)S(1)} %get-tuple-element.79), channel_id=1, source_target_pairs={{0,6},{2,4},{4,2},{6,0},{1,7},{3,5},{5,3},{7,1},{8,14},{10,12},{12... | collective-permute-start | bytes 196616 | tf_op jit(solution)/shard_map/ppermute | solution.py:357
  91.8 5.5 %collective-permute-start.18 = (bf16[3,128,128]{2,1,0:T(8,128)(2,1)S(1)}, bf16[3,128,128]{2,1,0:T(8,128)(2,1)S(1)}, u32[]{:S(2)}, u32[]{:S(2)}) collective-permute-start(bf16[3,128,128]{2,1,0:T(8,128)(2,1)S(1)} %get-tuple-element.81.refs_0_), channel_id=1, source_target_pairs={{0,8},{8,0},{16,24},{24,16},{1,9},{9,1},{17,25},{25,17},{2,10},{10... | collective-permute-start | bytes 294920 | tf_op jit(solution)/shard_map/ppermute | solution.py:357
  92.6 7.1 %collective-permute-start.19 = (bf16[3,128,128]{2,1,0:T(8,128)(2,1)S(1)}, bf16[3,128,128]{2,1,0:T(8,128)(2,1)S(1)}, u32[]{:S(2)}, u32[]{:S(2)}) collective-permute-start(bf16[3,128,128]{2,1,0:T(8,128)(2,1)S(1)} %get-tuple-element.81.refs_0_), channel_id=1, source_target_pairs={{0,16},{8,24},{16,0},{24,8},{1,17},{9,25},{17,1},{25,9},{2,18},{10... | collective-permute-start | bytes 294920 | tf_op jit(solution)/shard_map/ppermute | solution.py:357
  94.0 5.7 %collective-permute-start.20 = (bf16[3,128,128]{2,1,0:T(8,128)(2,1)S(1)}, bf16[3,128,128]{2,1,0:T(8,128)(2,1)S(1)}, u32[]{:S(2)}, u32[]{:S(2)}) collective-permute-start(bf16[3,128,128]{2,1,0:T(8,128)(2,1)S(1)} %get-tuple-element.81.refs_0_), channel_id=1, source_target_pairs={{0,24},{8,16},{16,8},{24,0},{1,25},{9,17},{17,9},{25,1},{2,26},{10... | collective-permute-start | bytes 294920 | tf_op jit(solution)/shard_map/ppermute | solution.py:357
  95.3 11.8 %collective-permute-start.23 = (bf16[8,128,128]{2,1,0:T(8,128)(2,1)}, bf16[8,128,128]{2,1,0:T(8,128)(2,1)S(1)}, u32[]{:S(2)}, u32[]{:S(2)}) collective-permute-start(bf16[8,128,128]{2,1,0:T(8,128)(2,1)} %copy-done.17), channel_id=1, source_target_pairs={{0,6},{2,4},{4,2},{6,0},{1,7},{3,5},{5,3},{7,1},{8,14},{10,12},{12... | collective-permute-start | bytes 786440 | tf_op jit(solution)/shard_map/ppermute | solution.py:357
  97.0 11.1 %collective-permute-start.21 = (bf16[8,128,128]{2,1,0:T(8,128)(2,1)}, bf16[8,128,128]{2,1,0:T(8,128)(2,1)S(1)}, u32[]{:S(2)}, u32[]{:S(2)}) collective-permute-start(bf16[8,128,128]{2,1,0:T(8,128)(2,1)} %copy-done.16), channel_id=1, source_target_pairs={{0,2},{2,0},{4,6},{6,4},{1,3},{3,1},{5,7},{7,5},{8,10},{10,8},{12,... | collective-permute-start | bytes 786440 | tf_op jit(solution)/shard_map/ppermute | solution.py:357
  97.3 23.0 %collective-permute-start.22 = (bf16[8,128,128]{2,1,0:T(8,128)(2,1)}, bf16[8,128,128]{2,1,0:T(8,128)(2,1)S(1)}, u32[]{:S(2)}, u32[]{:S(2)}) collective-permute-start(bf16[8,128,128]{2,1,0:T(8,128)(2,1)} %copy-done.15), channel_id=1, source_target_pairs={{0,4},{2,6},{4,0},{6,2},{1,5},{3,7},{5,1},{7,3},{8,12},{10,14},{12... | collective-permute-start | bytes 786440 | tf_op jit(solution)/shard_map/ppermute | solution.py:357
  100.3 1.4 %collective-permute-start.24 = (bf16[128,128]{1,0:T(8,128)(2,1)}, bf16[128,128]{1,0:T(8,128)(2,1)S(1)}, u32[]{:S(2)}, u32[]{:S(2)}) collective-permute-start(bf16[128,128]{1,0:T(8,128)(2,1)} %get-tuple-element.82.ours), channel_id=1, source_target_pairs={{0,1},{1,0},{2,3},{3,2},{4,5},{5,4},{6,7},{7,6},{8,9},{9,8},{10,11... | collective-permute-start | bytes 98312 | tf_op jit(solution)/shard_map/ppermute | solution.py:357
  103.7 17.4 %all-to-all-start.4 = ((bf16[4,128,128]{2,1,0:T(8,128)(2,1)}), bf16[4,128,128]{2,1,0:T(8,128)(2,1)S(1)}, u32[]{:S(2)}, u32[]{:S(2)}) async-start(bf16[4,128,128]{2,1,0:T(8,128)(2,1)} %choose.1), calls=%async_computation.4 | async-start | bytes 262144 | tf_op jit(solution)/shard_map/all_to_all | solution.py:378
  (16 other events, 111.8 us)

commit v5 on v4

--- a/solution.py
+++ b/solution.py
@@ -199,51 +199,29 @@
     )(*groups)
 
 
-def column_kernel(parts, panel, *refs):
-    smalls, (column, small) = refs[:-2], refs[-2:]
+def column_kernel(parts, panel, column, part):
     column[...] = (-jnp.sum(parts[...].astype(F32), axis=0)).astype(BF16)
     shape = (panel.shape[0] * panel.shape[1], panel.shape[2])
-    small[0] = lax.dot_general(
+    part[...] = lax.dot_general(
         panel[...].reshape(shape),
         column[...].reshape(shape),
         (((0,), (0,)), ((), ())),
         preferred_element_type=F32,
     ).astype(BF16)
-    small[1:] = total([ref[...] for ref in smalls]).astype(BF16)
-
-
-def form_column(parts, panel, smalls):
+
+
+def form_column(parts, panel):
     return pl.pallas_call(
         column_kernel,
         out_shape=[
             jax.ShapeDtypeStruct(panel.shape, BF16),
-            jax.ShapeDtypeStruct((3,) + panel.shape[1:], BF16),
+            jax.ShapeDtypeStruct(panel.shape[1:], BF16),
         ],
-        in_specs=[VMEM] * (2 + len(smalls)),
+        in_specs=[VMEM] * 2,
         out_specs=[VMEM] * 2,
         compiler_params=pltpu.CompilerParams(vmem_limit_bytes=LIMIT),
         name="form_column",
-    )(parts, panel, *smalls)
-
-
-def diagonal_kernel(base, *refs):
-    parts, (diagonal, sums) = refs[:-2], refs[-2:]
-    sums[...] = total([part[1:] for part in parts])
-    diagonal[...] = (base[...] - total([part[0] for part in parts])).astype(BF16)
-
-
-def form_diagonal(base, parts):
-    return pl.pallas_call(
-        diagonal_kernel,
-        out_shape=[
-            jax.ShapeDtypeStruct(base.shape, BF16),
-            jax.ShapeDtypeStruct((2,) + base.shape, F32),
-        ],
-        in_specs=[VMEM] * (1 + len(parts)),
-        out_specs=[VMEM] * 2,
-        compiler_params=pltpu.CompilerParams(vmem_limit_bytes=LIMIT),
-        name="form_diagonal",
-    )(base, *parts)
+    )(parts, panel)
 
 
 def sum_kernel(*refs):
@@ -261,26 +239,32 @@
     )(*parts)
 
 
-def choose_kernel(parent_two, ours, theirs, out):
-    core = lax.axis_index(CORE)
-    for at in range(out.shape[0]):
-        out[at] = jnp.where(parent_two[2 * at + core] % 2 == core, ours[...], theirs[...])
+def choose_kernel(nodes, parent_two, ours, theirs, *outs):
+    chip, core = lax.axis_index(CHIP), lax.axis_index(CORE)
+    for t in range(nodes):
+        parent = parent_two[2 * (chip ^ t) + core]
+        outs[t][...] = jnp.where(parent % 2 == core, ours[...], theirs[...])
 
 
 def choose(nodes, parent_two, ours, theirs):
     return pl.pallas_call(
-        choose_kernel,
-        out_shape=jax.ShapeDtypeStruct((nodes,) + ours.shape, BF16),
+        functools.partial(choose_kernel, nodes),
+        out_shape=[jax.ShapeDtypeStruct(ours.shape, BF16)] * nodes,
         in_specs=[SMEM] + [VMEM] * 2,
-        out_specs=VMEM,
+        out_specs=[VMEM] * nodes,
         compiler_params=pltpu.CompilerParams(vmem_limit_bytes=LIMIT),
         name="choose",
     )(parent_two, ours, theirs)
 
 
-def last_kernel(parent_two, link, base, diagonals, sums, upper, diagonal_two):
+def last_kernel(nodes, parent_two, link, base, *refs):
+    diagonals, parts, (upper, diagonal_two) = refs[:nodes], refs[nodes:-2], refs[-2:]
     chip, core = lax.axis_index(CHIP), lax.axis_index(CORE)
-    near = diagonals[parent_two[2 * chip + core] // 2]
+    step = (parent_two[2 * chip + core] // 2) ^ chip
+    near = diagonals[0][...]
+    for t in range(1, nodes):
+        near = jnp.where(step == t, diagonals[t][...], near)
+    sums = total([part[...] for part in parts])
     parent_term = jnp.dot(near, link[...], preferred_element_type=F32)
     upper[...] = (sums[0] - parent_term).astype(BF16)
     term = lax.dot_general(
@@ -289,15 +273,15 @@
     diagonal_two[...] = (base[...] - term + sums[1]).astype(BF16)
 
 
-def form_last(parent_two, link, base, diagonals, sums):
-    return pl.pallas_call(
-        last_kernel,
+def form_last(parent_two, link, base, diagonals, parts):
+    return pl.pallas_call(
+        functools.partial(last_kernel, len(diagonals)),
         out_shape=[jax.ShapeDtypeStruct(link.shape, BF16)] * 2,
-        in_specs=[SMEM] + [VMEM] * 4,
+        in_specs=[SMEM] + [VMEM] * (2 + len(diagonals) + len(parts)),
         out_specs=[VMEM] * 2,
         compiler_params=pltpu.CompilerParams(vmem_limit_bytes=LIMIT),
         name="form_last",
-    )(parent_two, link, base, diagonals, sums)
+    )(parent_two, link, base, *diagonals, *parts)
 
 
 def level_one(rows_one, inverse, pieces):
@@ -431,13 +415,14 @@
     columns, smalls = outs[:nodes], outs[nodes:]
     parts_small = [smalls[0]] + [exchange(smalls[t], CHIP, t) for t in range(1, nodes)]
     first = [exchange(columns[t], CHIP, t) for t in range(nodes // 2 + 1, nodes)]
-    *columns, token = together(*columns, parts_small[1])
+    column_one, part = form_column(parts_one, panel_one[0])
+    columns, parts_small, parts_diagonal = together(columns, parts_small, spread(part, ROW))
     parts_two = [exchange(columns[t], CHIP, t) for t in range(1, nodes // 2 + 1)] + first
-    column_one, small = form_column(parts_one, panel_one[0], parts_small)
-    diagonal_one, sums = form_diagonal(base_one[0], spread(small, ROW))
+    diagonal_one = (base_one[0] - total(parts_diagonal)).astype(BF16)
     chosen = choose(nodes, parent_two, diagonal_one, exchange(diagonal_one, CORE, 1))
-    diagonals = swap(chosen, CHIP)
-    upper, diagonal_two = form_last(parent_two, link_two[0], base_two[0], diagonals, sums)
+    diagonals = [chosen[0]] + [exchange(chosen[t], CHIP, t) for t in range(1, nodes)]
+    parts_last = spread(total(parts_small).astype(BF16), ROW)
+    upper, diagonal_two = form_last(parent_two, link_two[0], base_two[0], diagonals, parts_last)
     column_two = form_sum([columns[0], *parts_two])
     return (
         column_one[None],

time: 124 us -> 120 us (0.968)
  local copies, waits for them, and re-layouts: 11.5 us -> 7.45 us
  starting transfers between devices: 52.1 us -> 56.1 us
  waiting for transfers between devices: 37.6 us -> 33.7 us
    ppermute x23 -> x29, starting transfers between devices: 29.9 us -> 37.2 us  [exchange(): return lax.ppermute(x, axis, [(i, i ^ step) for i in range(size)])]
    ppermute x23 -> x29, waiting for transfers between devices: 29.9 us -> 22.7 us  [exchange(): return lax.ppermute(x, axis, [(i, i ^ step) for i in range(size)])]
    unnamed x36 -> x26, local copies, waits for them, and re-layouts: 11.5 us -> 7.45 us
    all_to_all x5 -> x4, starting transfers between devices: 20.2 us -> 16.9 us  [swap(): return lax.all_to_all(blocks, axis, 0, 0, tiled=True)]
    ppermute x1, waiting for transfers between devices: 1.45 us -> 4.72 us  [local(): out_one = lax.ppermute(inner_late, CHIP, [(1, 0), (2, 3)])]
    pallas_call x3 -> x2, Pallas kernels: 3.31 us -> 2.04 us  [the longest x1 1.46 us: form_last(): pl.pallas_call(functools.partial(last_kernel, len(diagonals)), out_shape=...]
    all_to_all x5 -> x4, waiting for transfers between devices: 6.24 us -> 6.24 us  [swap(): return lax.all_to_all(blocks, axis, 0, 0, tiled=True)]
  transfers between devices with their start and end apart: 30 -> 35, of which waited for: 14 -> 14; matrix products, arithmetic and copies ran while one was open for 1% -> 2% of each run, Pallas kernels for 14% -> 15%
where the time goes in v5:
time: 120 us; the launch traced here: 119 us
  starting transfers between devices  56.1 us (47%)
  waiting for transfers between devices  33.7 us (28%)
  Pallas kernels  18.9 us (16%)
  local copies, waits for them, and re-layouts  7.45 us (6%)
  other arithmetic  1.93 us (2%)
    ppermute x29, starting transfers between devices, exchange(): return lax.ppermute(x, axis, [(i, i ^ step) for i in range(size)])  37.2 us
    ppermute x29, waiting for transfers between devices, exchange(): return lax.ppermute(x, axis, [(i, i ^ step) for i in range(size)])  22.7 us
    all_to_all x4, starting transfers between devices, swap(): return lax.all_to_all(blocks, axis, 0, 0, tiled=True)  16.9 us
    unnamed x26, local copies, waits for them, and re-layouts  7.45 us
    all_to_all x4, waiting for transfers between devices, swap(): return lax.all_to_all(blocks, axis, 0, 0, tiled=True)  6.24 us
    ppermute x1, waiting for transfers between devices, local(): out_one = lax.ppermute(inner_late, CHIP, [(1, 0), (2, 3)])  4.72 us
    pallas_call x1, Pallas kernels, level_two(): pl.pallas_call(functools.partial(level_two_kernel, nodes, count, choices)...  4.21 us
    pallas_call x1, Pallas kernels, level_one(): pl.pallas_call(functools.partial(level_one_kernel, nodes, count), out_sha...  3.95 us
  transfers between devices with their start and end apart: 35, of which 14 were waited for; matrix products, arithmetic and copies ran while one was open for 2% of the time, Pallas kernels for 15%

profile of v5, /device:TPU:0, one launch (start us, length us, event | category | flops | bytes accessed | tf_op | source)
XLA Modules:
  0.0 118.9 jit_solution(6303793918909253044)
XLA Ops:
  2.1 2.7 %collective-permute-start.1 = (bf16[9,128,128]{2,1,0:T(8,128)(2,1)S(1)}, bf16[9,128,128]{2,1,0:T(8,128)(2,1)S(1)}, u32[]{:S(2)}, u32[]{:S(2)}) collective-permute-start(bf16[9,128,128]{2,1,0:T(8,128)(2,1)S(1)} %pad_maximum_fusion.refs_0_.refs_4_), channel_id=1, source_target_pairs={{0,2},{2,0},{4,6},{6,4},{1,3},{3,1},{5,7},{7,5},{8,10},{10,8},{12,... | collective-permute-start | bytes 884744 | tf_op jit(solution)/shard_map/ppermute | solution.py:341
  5.5 4.1 %all-to-all-start = ((bf16[4,2,128,128]{3,2,1,0:T(8,128)(2,1)}), bf16[4,2,128,128]{3,2,1,0:T(8,128)(2,1)}, u32[]{:S(2)}, u32[]{:S(2)}) async-start(bf16[4,2,128,128]{3,2,1,0:T(8,128)(2,1)} %bitcast.14), calls=%async_computation | async-start | bytes 524288 | tf_op jit(solution)/shard_map/all_to_all | solution.py:362
  10.5 5.1 %all-to-all-done = bf16[4,2,128,128]{3,2,1,0:T(8,128)(2,1)} async-done(((bf16[4,2,128,128]{3,2,1,0:T(8,128)(2,1)}), bf16[4,2,128,128]{3,2,1,0:T(8,128)(2,1)}, u32[]{:S(2)}, u32[]{:S(2)}) %all-to-all-start) | async-done | bytes 262176 | tf_op jit(solution)/shard_map/all_to_all | solution.py:362
  15.6 5.4 %all-to-all-start.1 = ((bf16[4,2,128,128]{3,2,1,0:T(8,128)(2,1)}), bf16[4,2,128,128]{3,2,1,0:T(8,128)(2,1)S(1)}, u32[]{:S(2)}, u32[]{:S(2)}) async-start(bf16[4,2,128,128]{3,2,1,0:T(8,128)(2,1)} %all-to-all-done), calls=%async_computation.1 | async-start | bytes 524288 | tf_op jit(solution)/shard_map/all_to_all | solution.py:362
  21.0 1.3 %collective-permute-start.3 = (bf16[2,128,128]{2,1,0:T(8,128)(2,1)S(1)}, bf16[2,128,128]{2,1,0:T(8,128)(2,1)S(1)}, u32[]{:S(2)}, u32[]{:S(2)}) collective-permute-start(bf16[2,128,128]{2,1,0:T(8,128)(2,1)S(1)} %get-tuple-element.64), channel_id=1, source_target_pairs={{0,8},{8,0},{16,24},{24,16},{1,9},{9,1},{17,25},{25,17},{2,10},{10... | collective-permute-start | bytes 196616 | tf_op jit(solution)/shard_map/ppermute | solution.py:341
  22.9 1.6 %collective-permute-start.5 = (bf16[2,128,128]{2,1,0:T(8,128)(2,1)S(1)}, bf16[2,128,128]{2,1,0:T(8,128)(2,1)S(1)}, u32[]{:S(2)}, u32[]{:S(2)}) collective-permute-start(bf16[2,128,128]{2,1,0:T(8,128)(2,1)S(1)} %get-tuple-element.66), channel_id=1, source_target_pairs={{0,24},{8,16},{16,8},{24,0},{1,25},{9,17},{17,9},{25,1},{2,26},{10... | collective-permute-start | bytes 196616 | tf_op jit(solution)/shard_map/ppermute | solution.py:341
  26.6 1.5 %collective-permute-done.5.refs_3_ = bf16[2,128,128]{2,1,0:T(8,128)(2,1)S(1)} collective-permute-done((bf16[2,128,128]{2,1,0:T(8,128)(2,1)S(1)}, bf16[2,128,128]{2,1,0:T(8,128)(2,1)S(1)}, u32[]{:S(2)}, u32[]{:S(2)}) %collective-permute-start.5) | collective-permute-done | bytes 65568 | tf_op jit(solution)/shard_map/ppermute | solution.py:341
  31.2 1.4 %collective-permute-start.8 = (bf16[4,2,128,128]{3,2,1,0:T(8,128)(2,1)S(1)}, bf16[4,2,128,128]{3,2,1,0:T(8,128)(2,1)S(1)}, u32[]{:S(2)}, u32[]{:S(2)}) collective-permute-start(bf16[4,2,128,128]{3,2,1,0:T(8,128)(2,1)S(1)} %all-to-all-done.1.refs_0_), channel_id=1, source_target_pairs={{0,24},{8,16},{16,8},{24,0},{1,25},{9,17},{17,9},{25,1},{2,26},{10... | collective-permute-start | bytes 786440 | tf_op jit(solution)/shard_map/ppermute | solution.py:341
  33.4 4.0 %all-to-all-start.2 = ((bf16[4,2,128,128]{3,2,1,0:T(8,128)(2,1)}), bf16[4,2,128,128]{3,2,1,0:T(8,128)(2,1)S(1)}, u32[]{:S(2)}, u32[]{:S(2)}) async-start(bf16[4,2,128,128]{3,2,1,0:T(8,128)(2,1)} %join_groups.1), calls=%async_computation.2 | async-start | bytes 524288 | tf_op jit(solution)/shard_map/all_to_all | solution.py:362
  37.4 3.9 %collective-permute-start.9 = (bf16[9,128,128]{2,1,0:T(8,128)(2,1)S(1)}, bf16[9,128,128]{2,1,0:T(8,128)(2,1)S(1)}, u32[]{:S(2)}, u32[]{:S(2)}) collective-permute-start(bf16[9,128,128]{2,1,0:T(8,128)(2,1)S(1)} %broadcast_select_fusion), channel_id=1, source_target_pairs={{0,6},{2,4},{4,2},{6,0},{1,7},{3,5},{5,3},{7,1},{8,14},{10,12},{12... | collective-permute-start | bytes 884744 | tf_op jit(solution)/shard_map/ppermute | solution.py:341
  41.3 1.3 %collective-permute-start.10 = (bf16[9,128,128]{2,1,0:T(8,128)(2,1)S(1)}, bf16[9,128,128]{2,1,0:T(8,128)(2,1)S(1)}, u32[]{:S(2)}, u32[]{:S(2)}) collective-permute-start(bf16[9,128,128]{2,1,0:T(8,128)(2,1)S(1)} %collective-permute-done.2.refs_4_.refs_8_), channel_id=1, source_target_pairs={{2,0},{4,6},{3,1},{5,7},{10,8},{12,14},{11,9},{13,15},{18,16},{20,... | collective-permute-start | bytes 884744 | tf_op jit(solution)/shard_map/ppermute | solution.py:399
  42.6 2.2 %copy-done = bf16[16,8,128,128]{3,2,1,0:T(8,128)(2,1)S(1)} copy-done((bf16[16,8,128,128]{3,2,1,0:T(8,128)(2,1)S(1)}, bf16[16,8,128,128]{3,2,1,0:T(8,128)(2,1)}, u32[]{:S(2)}) %copy-start) | copy-done | bytes 4194328
  44.7 2.4 %pair.1.inverse = bf16[2,16,8,128,128]{4,3,2,1,0:T(8,128)(2,1)S(1)} custom-call(bf16[16,8,128,128]{3,2,1,0:T(8,128)(2,1)S(1)} %copy-done, bf16[16,8,128,128]{3,2,1,0:T(8,128)(2,1)} %collective-permute-done.sibling), custom_call_target="tpu_custom_call" | custom-call | tf_op jit(solution)/shard_map/pair/pallas_call | solution.py:51
  47.2 3.9 %level_one.1.ours = bf16[4,8,128,128]{3,2,1,0:T(8,128)(2,1)} custom-call(s32[8,32]{1,0:T(8,128)S(1)} %copy-done.7, bf16[2,16,8,128,128]{4,3,2,1,0:T(8,128)(2,1)S(1)} %pair.1.inverse, bf16[4,2,128,128]{3,2,1,0:T(8,128)(2,1)S(1)} %all-to-all-done.1.refs_0_, bf16[4,2,128,128]{3,2,1,0:T(8,128)(2,1)S(1)} %collective-permute-done.6.refs_1_, ...), custom_call_target="tpu_custom_call" | custom-call | flops 1073741824 | bytes 12582912 | tf_op jit(solution)/shard_map/level_one/pallas_call | solution.py:292
  51.1 4.7 %collective-permute-done.10.refs_3_.refs_7_ = bf16[9,128,128]{2,1,0:T(8,128)(2,1)S(1)} collective-permute-done((bf16[9,128,128]{2,1,0:T(8,128)(2,1)S(1)}, bf16[9,128,128]{2,1,0:T(8,128)(2,1)S(1)}, u32[]{:S(2)}, u32[]{:S(2)}) %collective-permute-start.10) | collective-permute-done | bytes 294944 | tf_op jit(solution)/shard_map/ppermute | solution.py:399
  55.9 3.5 %all-to-all-start.3 = ((bf16[4,8,128,128]{3,2,1,0:T(8,128)(2,1)}), bf16[4,8,128,128]{3,2,1,0:T(8,128)(2,1)S(1)}, u32[]{:S(2)}, u32[]{:S(2)}) async-start(bf16[4,8,128,128]{3,2,1,0:T(8,128)(2,1)} %level_one.1.ours), calls=%async_computation.3 | async-start | bytes 2097152 | tf_op jit(solution)/shard_map/all_to_all | solution.py:362
  61.7 1.3 %collective-permute-start.14 = (bf16[4,2,128,128]{3,2,1,0:T(8,128)(2,1)S(1)}, bf16[4,2,128,128]{3,2,1,0:T(8,128)(2,1)S(1)}, u32[]{:S(2)}, u32[]{:S(2)}) collective-permute-start(bf16[4,2,128,128]{3,2,1,0:T(8,128)(2,1)S(1)} %all-to-all-done.2.refs_0_), channel_id=1, source_target_pairs={{0,24},{8,16},{16,8},{24,0},{1,25},{9,17},{17,9},{25,1},{2,26},{10... | collective-permute-start | bytes 786440 | tf_op jit(solution)/shard_map/ppermute | solution.py:341
  63.0 2.2 %copy-done.1 = bf16[16,8,128,128]{3,2,1,0:T(8,128)(2,1)S(1)} copy-done((bf16[16,8,128,128]{3,2,1,0:T(8,128)(2,1)S(1)}, bf16[16,8,128,128]{3,2,1,0:T(8,128)(2,1)}, u32[]{:S(2)}) %copy-start.1) | copy-done | bytes 4194328
  65.2 3.8 %form_near.1 = (bf16[4,8,128,128]{3,2,1,0:T(8,128)(2,1)S(1)}, bf16[4,128,128]{2,1,0:T(8,128)(2,1)S(1)}, bf16[2,16,8,128,128]{4,3,2,1,0:T(8,128)(2,1)S(1)}) custom-call(s32[8]{0:T(128)S(1)} %copy-done.9, s32[8,32]{1,0:T(8,128)S(1)} %copy-done.8, bf16[16,8,128,128]{3,2,1,0:T(8,128)(2,1)S(1)} %copy-done.1, ...), custom_call_target="tpu_custom_call" | custom-call | tf_op jit(solution)/shard_map/form_near/pallas_call | solution.py:306
  69.0 4.2 %collective-permute-done.13.refs_2_ = bf16[4,2,128,128]{3,2,1,0:T(8,128)(2,1)S(1)} collective-permute-done((bf16[4,2,128,128]{3,2,1,0:T(8,128)(2,1)S(1)}, bf16[4,2,128,128]{3,2,1,0:T(8,128)(2,1)S(1)}, u32[]{:S(2)}, u32[]{:S(2)}) %collective-permute-start.13) | collective-permute-done | bytes 262176 | tf_op jit(solution)/shard_map/ppermute | solution.py:341
  73.3 1.4 %collective-permute-done.14.refs_3_ = bf16[4,2,128,128]{3,2,1,0:T(8,128)(2,1)S(1)} collective-permute-done((bf16[4,2,128,128]{3,2,1,0:T(8,128)(2,1)S(1)}, bf16[4,2,128,128]{3,2,1,0:T(8,128)(2,1)S(1)}, u32[]{:S(2)}, u32[]{:S(2)}) %collective-permute-start.14) | collective-permute-done | bytes 262176 | tf_op jit(solution)/shard_map/ppermute | solution.py:341
  74.7 4.2 %level_two.1 = (bf16[8,128,128]{2,1,0:T(8,128)(2,1)S(1)}, bf16[8,128,128]{2,1,0:T(8,128)(2,1)S(1)}, bf16[8,128,128]{2,1,0:T(8,128)(2,1)S(1)}, bf16[8,128,128]{2,...) custom-call(s32[8,32]{1,0:T(8,128)S(1)} %copy-done.7, ...), custom_call_target="tpu_custom_call" | custom-call | flops 1476395008 | bytes 16777216 | tf_op jit(solution)/shard_map/level_two/pallas_call | solution.py:327
  81.0 1.9 %collective-permute-start.15 = (bf16[2,128,128]{2,1,0:T(8,128)(2,1)}, bf16[2,128,128]{2,1,0:T(8,128)(2,1)S(1)}, u32[]{:S(2)}, u32[]{:S(2)}) collective-permute-start(bf16[2,128,128]{2,1,0:T(8,128)(2,1)} %get-tuple-element.92), channel_id=1, source_target_pairs={{0,2},{2,0},{4,6},{6,4},{1,3},{3,1},{5,7},{7,5},{8,10},{10,8},{12,... | collective-permute-start | bytes 196616 | tf_op jit(solution)/shard_map/ppermute | solution.py:341
  82.9 2.4 %collective-permute-start.16 = (bf16[2,128,128]{2,1,0:T(8,128)(2,1)}, bf16[2,128,128]{2,1,0:T(8,128)(2,1)S(1)}, u32[]{:S(2)}, u32[]{:S(2)}) collective-permute-start(bf16[2,128,128]{2,1,0:T(8,128)(2,1)} %get-tuple-element.93), channel_id=1, source_target_pairs={{0,4},{2,6},{4,0},{6,2},{1,5},{3,7},{5,1},{7,3},{8,12},{10,14},{12... | collective-permute-start | bytes 196616 | tf_op jit(solution)/shard_map/ppermute | solution.py:341
  87.2 1.4 %collective-permute-start.19 = (bf16[128,128]{1,0:T(8,128)(2,1)S(1)}, bf16[128,128]{1,0:T(8,128)(2,1)S(1)}, u32[]{:S(2)}, u32[]{:S(2)}) collective-permute-start(bf16[128,128]{1,0:T(8,128)(2,1)S(1)} %get-tuple-element.96), channel_id=1, source_target_pairs={{0,16},{8,24},{16,0},{24,8},{1,17},{9,25},{17,1},{25,9},{2,18},{10... | collective-permute-start | bytes 98312 | tf_op jit(solution)/shard_map/ppermute | solution.py:341
  90.3 3.3 %collective-permute-start.23 = (bf16[8,128,128]{2,1,0:T(8,128)(2,1)}, bf16[8,128,128]{2,1,0:T(8,128)(2,1)S(1)}, u32[]{:S(2)}, u32[]{:S(2)}) collective-permute-start(bf16[8,128,128]{2,1,0:T(8,128)(2,1)} %copy-done.12), channel_id=1, source_target_pairs={{0,6},{2,4},{4,2},{6,0},{1,7},{3,5},{5,3},{7,1},{8,14},{10,12},{12... | collective-permute-start | bytes 786440 | tf_op jit(solution)/shard_map/ppermute | solution.py:341
  95.3 3.3 %collective-permute-start.22 = (bf16[8,128,128]{2,1,0:T(8,128)(2,1)}, bf16[8,128,128]{2,1,0:T(8,128)(2,1)S(1)}, u32[]{:S(2)}, u32[]{:S(2)}) collective-permute-start(bf16[8,128,128]{2,1,0:T(8,128)(2,1)} %copy-done.10), channel_id=1, source_target_pairs={{0,4},{2,6},{4,0},{6,2},{1,5},{3,7},{5,1},{7,3},{8,12},{10,14},{12... | collective-permute-start | bytes 786440 | tf_op jit(solution)/shard_map/ppermute | solution.py:341
  101.8 1.9 %collective-permute-start.30 = (bf16[2,128,128]{2,1,0:T(8,128)(2,1)S(1)}, bf16[2,128,128]{2,1,0:T(8,128)(2,1)S(1)}, u32[]{:S(2)}, u32[]{:S(2)}) collective-permute-start(bf16[2,128,128]{2,1,0:T(8,128)(2,1)S(1)} %add_convert_fusion.refs_4_), channel_id=1, source_target_pairs={{0,24},{8,16},{16,8},{24,0},{1,25},{9,17},{17,9},{25,1},{2,26},{10... | collective-permute-start | bytes 196616 | tf_op jit(solution)/shard_map/ppermute | solution.py:341
  105.0 1.9 %collective-permute-done.30.refs_7_ = bf16[2,128,128]{2,1,0:T(8,128)(2,1)S(1)} collective-permute-done((bf16[2,128,128]{2,1,0:T(8,128)(2,1)S(1)}, bf16[2,128,128]{2,1,0:T(8,128)(2,1)S(1)}, u32[]{:S(2)}, u32[]{:S(2)}) %collective-permute-start.30) | collective-permute-done | bytes 65568 | tf_op jit(solution)/shard_map/ppermute | solution.py:341
  106.9 3.2 %collective-permute-done.25.refs_1_ = bf16[128,128]{1,0:T(8,128)(2,1)S(1)} collective-permute-done((bf16[128,128]{1,0:T(8,128)(2,1)S(1)}, bf16[128,128]{1,0:T(8,128)(2,1)S(1)}, u32[]{:S(2)}, u32[]{:S(2)}) %collective-permute-start.25) | collective-permute-done | bytes 32800 | tf_op jit(solution)/shard_map/ppermute | solution.py:341
  110.7 5.9 %collective-permute-done.26.refs_2_ = bf16[128,128]{1,0:T(8,128)(2,1)S(1)} collective-permute-done((bf16[128,128]{1,0:T(8,128)(2,1)S(1)}, bf16[128,128]{1,0:T(8,128)(2,1)S(1)}, u32[]{:S(2)}, u32[]{:S(2)}) %collective-permute-start.26) | collective-permute-done | bytes 32800 | tf_op jit(solution)/shard_map/ppermute | solution.py:341
  116.6 1.5 %form_last.1 = (bf16[128,128]{1,0:T(8,128)(2,1)}, bf16[128,128]{1,0:T(8,128)(2,1)}) custom-call(s32[8]{0:T(128)S(1)} %copy-done.9, bf16[128,128]{1,0:T(8,128)(2,1)S(1)} %bitcast.18, f32[128,128]{1,0:T(8,128)S(1)} %bitcast.20, bf16[128,128]{1,0:T(8,128)(2,1)S(1)} %get-tuple-element.103.refs_0_, bf16[128,128]{1,0:T(8,128)(2,1)S(1)} %collective-permute-done.25.refs_1_, ...), custom_call_target="tpu_custom_call" | custom-call | tf_op jit(solution)/shard_map/form_last/pallas_call | solution.py:277
  (78 shorter events, 25.5 us)
Async XLA Ops:
  0.6 40.6 %collective-permute-start = (bf16[16,8,128,128]{3,2,1,0:T(8,128)(2,1)}, bf16[16,8,128,128]{3,2,1,0:T(8,128)(2,1)}, u32[]{:S(2)}, u32[]{:S(2)}) collective-permute-start(bf16[16,8,128,128]{3,2,1,0:T(8,128)(2,1)} %own.3), channel_id=1, source_target_pairs={{0,1},{1,0},{2,3},{3,2},{4,5},{5,4},{6,7},{7,6},{8,9},{9,8},{10,11... | collective-permute-start | bytes 12582920 | tf_op jit(solution)/shard_map/ppermute | solution.py:341
  2.1 13.5 %collective-permute-start.1 = (bf16[9,128,128]{2,1,0:T(8,128)(2,1)S(1)}, bf16[9,128,128]{2,1,0:T(8,128)(2,1)S(1)}, u32[]{:S(2)}, u32[]{:S(2)}) collective-permute-start(bf16[9,128,128]{2,1,0:T(8,128)(2,1)S(1)} %pad_maximum_fusion.refs_0_.refs_4_), channel_id=1, source_target_pairs={{0,2},{2,0},{4,6},{6,4},{1,3},{3,1},{5,7},{7,5},{8,10},{10,8},{12,... | collective-permute-start | bytes 884744 | tf_op jit(solution)/shard_map/ppermute | solution.py:341
  4.8 10.8 %collective-permute-start.2 = (bf16[9,128,128]{2,1,0:T(8,128)(2,1)S(1)}, bf16[9,128,128]{2,1,0:T(8,128)(2,1)S(1)}, u32[]{:S(2)}, u32[]{:S(2)}) collective-permute-start(bf16[9,128,128]{2,1,0:T(8,128)(2,1)S(1)} %pad_maximum_fusion.refs_0_.refs_4_), channel_id=1, source_target_pairs={{2,4},{4,2},{3,5},{5,3},{10,12},{12,10},{11,13},{13,11},{18,20},{2... | collective-permute-start | bytes 884744 | tf_op jit(solution)/shard_map/ppermute | solution.py:378
  5.5 10.1 %all-to-all-start = ((bf16[4,2,128,128]{3,2,1,0:T(8,128)(2,1)}), bf16[4,2,128,128]{3,2,1,0:T(8,128)(2,1)}, u32[]{:S(2)}, u32[]{:S(2)}) async-start(bf16[4,2,128,128]{3,2,1,0:T(8,128)(2,1)} %bitcast.14), calls=%async_computation | async-start | bytes 524288 | tf_op jit(solution)/shard_map/all_to_all | solution.py:362
  15.6 13.5 %all-to-all-start.1 = ((bf16[4,2,128,128]{3,2,1,0:T(8,128)(2,1)}), bf16[4,2,128,128]{3,2,1,0:T(8,128)(2,1)S(1)}, u32[]{:S(2)}, u32[]{:S(2)}) async-start(bf16[4,2,128,128]{3,2,1,0:T(8,128)(2,1)} %all-to-all-done), calls=%async_computation.1 | async-start | bytes 524288 | tf_op jit(solution)/shard_map/all_to_all | solution.py:362
  21.0 4.7 %collective-permute-start.3 = (bf16[2,128,128]{2,1,0:T(8,128)(2,1)S(1)}, bf16[2,128,128]{2,1,0:T(8,128)(2,1)S(1)}, u32[]{:S(2)}, u32[]{:S(2)}) collective-permute-start(bf16[2,128,128]{2,1,0:T(8,128)(2,1)S(1)} %get-tuple-element.64), channel_id=1, source_target_pairs={{0,8},{8,0},{16,24},{24,16},{1,9},{9,1},{17,25},{25,17},{2,10},{10... | collective-permute-start | bytes 196616 | tf_op jit(solution)/shard_map/ppermute | solution.py:341
  22.3 4.3 %collective-permute-start.4 = (bf16[2,128,128]{2,1,0:T(8,128)(2,1)S(1)}, bf16[2,128,128]{2,1,0:T(8,128)(2,1)S(1)}, u32[]{:S(2)}, u32[]{:S(2)}) collective-permute-start(bf16[2,128,128]{2,1,0:T(8,128)(2,1)S(1)} %get-tuple-element.65), channel_id=1, source_target_pairs={{0,16},{8,24},{16,0},{24,8},{1,17},{9,25},{17,1},{25,9},{2,18},{10... | collective-permute-start | bytes 196616 | tf_op jit(solution)/shard_map/ppermute | solution.py:341
  22.9 5.2 %collective-permute-start.5 = (bf16[2,128,128]{2,1,0:T(8,128)(2,1)S(1)}, bf16[2,128,128]{2,1,0:T(8,128)(2,1)S(1)}, u32[]{:S(2)}, u32[]{:S(2)}) collective-permute-start(bf16[2,128,128]{2,1,0:T(8,128)(2,1)S(1)} %get-tuple-element.66), channel_id=1, source_target_pairs={{0,24},{8,16},{16,8},{24,0},{1,25},{9,17},{17,9},{25,1},{2,26},{10... | collective-permute-start | bytes 196616 | tf_op jit(solution)/shard_map/ppermute | solution.py:341
  29.1 18.0 %collective-permute-start.6 = (bf16[4,2,128,128]{3,2,1,0:T(8,128)(2,1)S(1)}, bf16[4,2,128,128]{3,2,1,0:T(8,128)(2,1)S(1)}, u32[]{:S(2)}, u32[]{:S(2)}) collective-permute-start(bf16[4,2,128,128]{3,2,1,0:T(8,128)(2,1)S(1)} %all-to-all-done.1.refs_0_), channel_id=1, source_target_pairs={{0,8},{8,0},{16,24},{24,16},{1,9},{9,1},{17,25},{25,17},{2,10},{10... | collective-permute-start | bytes 786440 | tf_op jit(solution)/shard_map/ppermute | solution.py:341
  30.3 16.8 %collective-permute-start.7 = (bf16[4,2,128,128]{3,2,1,0:T(8,128)(2,1)S(1)}, bf16[4,2,128,128]{3,2,1,0:T(8,128)(2,1)S(1)}, u32[]{:S(2)}, u32[]{:S(2)}) collective-permute-start(bf16[4,2,128,128]{3,2,1,0:T(8,128)(2,1)S(1)} %all-to-all-done.1.refs_0_), channel_id=1, source_target_pairs={{0,16},{8,24},{16,0},{24,8},{1,17},{9,25},{17,1},{25,9},{2,18},{10... | collective-permute-start | bytes 786440 | tf_op jit(solution)/shard_map/ppermute | solution.py:341
  31.2 15.9 %collective-permute-start.8 = (bf16[4,2,128,128]{3,2,1,0:T(8,128)(2,1)S(1)}, bf16[4,2,128,128]{3,2,1,0:T(8,128)(2,1)S(1)}, u32[]{:S(2)}, u32[]{:S(2)}) collective-permute-start(bf16[4,2,128,128]{3,2,1,0:T(8,128)(2,1)S(1)} %all-to-all-done.1.refs_0_), channel_id=1, source_target_pairs={{0,24},{8,16},{16,8},{24,0},{1,25},{9,17},{17,9},{25,1},{2,26},{10... | collective-permute-start | bytes 786440 | tf_op jit(solution)/shard_map/ppermute | solution.py:341
  33.4 22.5 %all-to-all-start.2 = ((bf16[4,2,128,128]{3,2,1,0:T(8,128)(2,1)}), bf16[4,2,128,128]{3,2,1,0:T(8,128)(2,1)S(1)}, u32[]{:S(2)}, u32[]{:S(2)}) async-start(bf16[4,2,128,128]{3,2,1,0:T(8,128)(2,1)} %join_groups.1), calls=%async_computation.2 | async-start | bytes 524288 | tf_op jit(solution)/shard_map/all_to_all | solution.py:362
  37.4 13.8 %collective-permute-start.9 = (bf16[9,128,128]{2,1,0:T(8,128)(2,1)S(1)}, bf16[9,128,128]{2,1,0:T(8,128)(2,1)S(1)}, u32[]{:S(2)}, u32[]{:S(2)}) collective-permute-start(bf16[9,128,128]{2,1,0:T(8,128)(2,1)S(1)} %broadcast_select_fusion), channel_id=1, source_target_pairs={{0,6},{2,4},{4,2},{6,0},{1,7},{3,5},{5,3},{7,1},{8,14},{10,12},{12... | collective-permute-start | bytes 884744 | tf_op jit(solution)/shard_map/ppermute | solution.py:341
  41.3 14.6 %collective-permute-start.10 = (bf16[9,128,128]{2,1,0:T(8,128)(2,1)S(1)}, bf16[9,128,128]{2,1,0:T(8,128)(2,1)S(1)}, u32[]{:S(2)}, u32[]{:S(2)}) collective-permute-start(bf16[9,128,128]{2,1,0:T(8,128)(2,1)S(1)} %collective-permute-done.2.refs_4_.refs_8_), channel_id=1, source_target_pairs={{2,0},{4,6},{3,1},{5,7},{10,8},{12,14},{11,9},{13,15},{18,16},{20,... | collective-permute-start | bytes 884744 | tf_op jit(solution)/shard_map/ppermute | solution.py:399
  55.9 29.5 %all-to-all-start.3 = ((bf16[4,8,128,128]{3,2,1,0:T(8,128)(2,1)}), bf16[4,8,128,128]{3,2,1,0:T(8,128)(2,1)S(1)}, u32[]{:S(2)}, u32[]{:S(2)}) async-start(bf16[4,8,128,128]{3,2,1,0:T(8,128)(2,1)} %level_one.1.ours), calls=%async_computation.3 | async-start | bytes 2097152 | tf_op jit(solution)/shard_map/all_to_all | solution.py:362
  59.5 9.6 %collective-permute-start.12 = (bf16[4,2,128,128]{3,2,1,0:T(8,128)(2,1)S(1)}, bf16[4,2,128,128]{3,2,1,0:T(8,128)(2,1)S(1)}, u32[]{:S(2)}, u32[]{:S(2)}) collective-permute-start(bf16[4,2,128,128]{3,2,1,0:T(8,128)(2,1)S(1)} %all-to-all-done.2.refs_0_), channel_id=1, source_target_pairs={{0,8},{8,0},{16,24},{24,16},{1,9},{9,1},{17,25},{25,17},{2,10},{10... | collective-permute-start | bytes 786440 | tf_op jit(solution)/shard_map/ppermute | solution.py:341
  60.7 12.6 %collective-permute-start.13 = (bf16[4,2,128,128]{3,2,1,0:T(8,128)(2,1)S(1)}, bf16[4,2,128,128]{3,2,1,0:T(8,128)(2,1)S(1)}, u32[]{:S(2)}, u32[]{:S(2)}) collective-permute-start(bf16[4,2,128,128]{3,2,1,0:T(8,128)(2,1)S(1)} %all-to-all-done.2.refs_0_), channel_id=1, source_target_pairs={{0,16},{8,24},{16,0},{24,8},{1,17},{9,25},{17,1},{25,9},{2,18},{10... | collective-permute-start | bytes 786440 | tf_op jit(solution)/shard_map/ppermute | solution.py:341
  61.7 13.0 %collective-permute-start.14 = (bf16[4,2,128,128]{3,2,1,0:T(8,128)(2,1)S(1)}, bf16[4,2,128,128]{3,2,1,0:T(8,128)(2,1)S(1)}, u32[]{:S(2)}, u32[]{:S(2)}) collective-permute-start(bf16[4,2,128,128]{3,2,1,0:T(8,128)(2,1)S(1)} %all-to-all-done.2.refs_0_), channel_id=1, source_target_pairs={{0,24},{8,16},{16,8},{24,0},{1,25},{9,17},{17,9},{25,1},{2,26},{10... | collective-permute-start | bytes 786440 | tf_op jit(solution)/shard_map/ppermute | solution.py:341
  81.0 7.6 %collective-permute-start.15 = (bf16[2,128,128]{2,1,0:T(8,128)(2,1)}, bf16[2,128,128]{2,1,0:T(8,128)(2,1)S(1)}, u32[]{:S(2)}, u32[]{:S(2)}) collective-permute-start(bf16[2,128,128]{2,1,0:T(8,128)(2,1)} %get-tuple-element.92), channel_id=1, source_target_pairs={{0,2},{2,0},{4,6},{6,4},{1,3},{3,1},{5,7},{7,5},{8,10},{10,8},{12,... | collective-permute-start | bytes 196616 | tf_op jit(solution)/shard_map/ppermute | solution.py:341
  82.9 7.4 %collective-permute-start.16 = (bf16[2,128,128]{2,1,0:T(8,128)(2,1)}, bf16[2,128,128]{2,1,0:T(8,128)(2,1)S(1)}, u32[]{:S(2)}, u32[]{:S(2)}) collective-permute-start(bf16[2,128,128]{2,1,0:T(8,128)(2,1)} %get-tuple-element.93), channel_id=1, source_target_pairs={{0,4},{2,6},{4,0},{6,2},{1,5},{3,7},{5,1},{7,3},{8,12},{10,14},{12... | collective-permute-start | bytes 196616 | tf_op jit(solution)/shard_map/ppermute | solution.py:341
  85.3 8.3 %collective-permute-start.17 = (bf16[2,128,128]{2,1,0:T(8,128)(2,1)S(1)}, bf16[2,128,128]{2,1,0:T(8,128)(2,1)S(1)}, u32[]{:S(2)}, u32[]{:S(2)}) collective-permute-start(bf16[2,128,128]{2,1,0:T(8,128)(2,1)S(1)} %get-tuple-element.94), channel_id=1, source_target_pairs={{0,6},{2,4},{4,2},{6,0},{1,7},{3,5},{5,3},{7,1},{8,14},{10,12},{12... | collective-permute-start | bytes 196616 | tf_op jit(solution)/shard_map/ppermute | solution.py:341
  86.3 7.2 %collective-permute-start.18 = (bf16[128,128]{1,0:T(8,128)(2,1)S(1)}, bf16[128,128]{1,0:T(8,128)(2,1)S(1)}, u32[]{:S(2)}, u32[]{:S(2)}) collective-permute-start(bf16[128,128]{1,0:T(8,128)(2,1)S(1)} %get-tuple-element.96), channel_id=1, source_target_pairs={{0,8},{8,0},{16,24},{24,16},{1,9},{9,1},{17,25},{25,17},{2,10},{10... | collective-permute-start | bytes 98312 | tf_op jit(solution)/shard_map/ppermute | solution.py:341
  87.2 6.3 %collective-permute-start.19 = (bf16[128,128]{1,0:T(8,128)(2,1)S(1)}, bf16[128,128]{1,0:T(8,128)(2,1)S(1)}, u32[]{:S(2)}, u32[]{:S(2)}) collective-permute-start(bf16[128,128]{1,0:T(8,128)(2,1)S(1)} %get-tuple-element.96), channel_id=1, source_target_pairs={{0,16},{8,24},{16,0},{24,8},{1,17},{9,25},{17,1},{25,9},{2,18},{10... | collective-permute-start | bytes 98312 | tf_op jit(solution)/shard_map/ppermute | solution.py:341
  88.6 4.9 %collective-permute-start.20 = (bf16[128,128]{1,0:T(8,128)(2,1)S(1)}, bf16[128,128]{1,0:T(8,128)(2,1)S(1)}, u32[]{:S(2)}, u32[]{:S(2)}) collective-permute-start(bf16[128,128]{1,0:T(8,128)(2,1)S(1)} %get-tuple-element.96), channel_id=1, source_target_pairs={{0,24},{8,16},{16,8},{24,0},{1,25},{9,17},{17,9},{25,1},{2,26},{10... | collective-permute-start | bytes 98312 | tf_op jit(solution)/shard_map/ppermute | solution.py:341
  90.3 27.8 %collective-permute-start.23 = (bf16[8,128,128]{2,1,0:T(8,128)(2,1)}, bf16[8,128,128]{2,1,0:T(8,128)(2,1)S(1)}, u32[]{:S(2)}, u32[]{:S(2)}) collective-permute-start(bf16[8,128,128]{2,1,0:T(8,128)(2,1)} %copy-done.12), channel_id=1, source_target_pairs={{0,6},{2,4},{4,2},{6,0},{1,7},{3,5},{5,3},{7,1},{8,14},{10,12},{12... | collective-permute-start | bytes 786440 | tf_op jit(solution)/shard_map/ppermute | solution.py:341
  93.6 8.2 %collective-permute-start.28 = (bf16[2,128,128]{2,1,0:T(8,128)(2,1)S(1)}, bf16[2,128,128]{2,1,0:T(8,128)(2,1)S(1)}, u32[]{:S(2)}, u32[]{:S(2)}) collective-permute-start(bf16[2,128,128]{2,1,0:T(8,128)(2,1)S(1)} %add_convert_fusion.refs_4_), channel_id=1, source_target_pairs={{0,8},{8,0},{16,24},{24,16},{1,9},{9,1},{17,25},{25,17},{2,10},{10... | collective-permute-start | bytes 196616 | tf_op jit(solution)/shard_map/ppermute | solution.py:341
  94.5 23.5 %collective-permute-start.21 = (bf16[8,128,128]{2,1,0:T(8,128)(2,1)}, bf16[8,128,128]{2,1,0:T(8,128)(2,1)S(1)}, u32[]{:S(2)}, u32[]{:S(2)}) collective-permute-start(bf16[8,128,128]{2,1,0:T(8,128)(2,1)} %copy-done.11), channel_id=1, source_target_pairs={{0,2},{2,0},{4,6},{6,4},{1,3},{3,1},{5,7},{7,5},{8,10},{10,8},{12,... | collective-permute-start | bytes 786440 | tf_op jit(solution)/shard_map/ppermute | solution.py:341
  95.3 22.7 %collective-permute-start.22 = (bf16[8,128,128]{2,1,0:T(8,128)(2,1)}, bf16[8,128,128]{2,1,0:T(8,128)(2,1)S(1)}, u32[]{:S(2)}, u32[]{:S(2)}) collective-permute-start(bf16[8,128,128]{2,1,0:T(8,128)(2,1)} %copy-done.10), channel_id=1, source_target_pairs={{0,4},{2,6},{4,0},{6,2},{1,5},{3,7},{5,1},{7,3},{8,12},{10,14},{12... | collective-permute-start | bytes 786440 | tf_op jit(solution)/shard_map/ppermute | solution.py:341
  101.8 5.2 %collective-permute-start.30 = (bf16[2,128,128]{2,1,0:T(8,128)(2,1)S(1)}, bf16[2,128,128]{2,1,0:T(8,128)(2,1)S(1)}, u32[]{:S(2)}, u32[]{:S(2)}) collective-permute-start(bf16[2,128,128]{2,1,0:T(8,128)(2,1)S(1)} %add_convert_fusion.refs_4_), channel_id=1, source_target_pairs={{0,24},{8,16},{16,8},{24,0},{1,25},{9,17},{17,9},{25,1},{2,26},{10... | collective-permute-start | bytes 196616 | tf_op jit(solution)/shard_map/ppermute | solution.py:341
  105.0 5.2 %collective-permute-start.25 = (bf16[128,128]{1,0:T(8,128)(2,1)S(1)}, bf16[128,128]{1,0:T(8,128)(2,1)S(1)}, u32[]{:S(2)}, u32[]{:S(2)}) collective-permute-start(bf16[128,128]{1,0:T(8,128)(2,1)S(1)} %get-tuple-element.104), channel_id=1, source_target_pairs={{0,2},{2,0},{4,6},{6,4},{1,3},{3,1},{5,7},{7,5},{8,10},{10,8},{12,... | collective-permute-start | bytes 98312 | tf_op jit(solution)/shard_map/ppermute | solution.py:341
  106.9 9.6 %collective-permute-start.26 = (bf16[128,128]{1,0:T(8,128)(2,1)S(1)}, bf16[128,128]{1,0:T(8,128)(2,1)S(1)}, u32[]{:S(2)}, u32[]{:S(2)}) collective-permute-start(bf16[128,128]{1,0:T(8,128)(2,1)S(1)} %get-tuple-element.105), channel_id=1, source_target_pairs={{0,4},{2,6},{4,0},{6,2},{1,5},{3,7},{5,1},{7,3},{8,12},{10,14},{12... | collective-permute-start | bytes 98312 | tf_op jit(solution)/shard_map/ppermute | solution.py:341
  110.2 6.4 %collective-permute-start.27 = (bf16[128,128]{1,0:T(8,128)(2,1)S(1)}, bf16[128,128]{1,0:T(8,128)(2,1)S(1)}, u32[]{:S(2)}, u32[]{:S(2)}) collective-permute-start(bf16[128,128]{1,0:T(8,128)(2,1)S(1)} %get-tuple-element.106), channel_id=1, source_target_pairs={{0,6},{2,4},{4,2},{6,0},{1,7},{3,5},{5,3},{7,1},{8,14},{10,12},{12... | collective-permute-start | bytes 98312 | tf_op jit(solution)/shard_map/ppermute | solution.py:341
  (16 other events, 189.3 us)

commit v6 on v5

--- a/solution.py
+++ b/solution.py
@@ -384,7 +384,6 @@
     quarters, near, inner, sends = together(quarters, near, inner, sends)
     blocks_one = swap(quarters, CHIP)
     groups = [kept] + [exchange(send, ROW, s + 1) for s, send in enumerate(sends)]
-    blocks_one, groups = together(blocks_one, groups)
     quarters_two = join_groups(groups)
     pieces_one = spread(blocks_one, ROW)
     inverse = pair(inverse_top, after(sibling, blocks_one))
@@ -414,10 +413,10 @@
     )
     columns, smalls = outs[:nodes], outs[nodes:]
     parts_small = [smalls[0]] + [exchange(smalls[t], CHIP, t) for t in range(1, nodes)]
-    first = [exchange(columns[t], CHIP, t) for t in range(nodes // 2 + 1, nodes)]
+    first = [exchange(columns[t], CHIP, t) for t in range(nodes // 2, nodes)]
     column_one, part = form_column(parts_one, panel_one[0])
     columns, parts_small, parts_diagonal = together(columns, parts_small, spread(part, ROW))
-    parts_two = [exchange(columns[t], CHIP, t) for t in range(1, nodes // 2 + 1)] + first
+    parts_two = [exchange(columns[t], CHIP, t) for t in range(1, nodes // 2)] + first
     diagonal_one = (base_one[0] - total(parts_diagonal)).astype(BF16)
     chosen = choose(nodes, parent_two, diagonal_one, exchange(diagonal_one, CORE, 1))
     diagonals = [chosen[0]] + [exchange(chosen[t], CHIP, t) for t in range(1, nodes)]

time: 120 us -> 117 us (0.975)
  waiting for transfers between devices: 33.7 us -> 26 us
  starting transfers between devices: 56.1 us -> 61.7 us
    ppermute x29, starting transfers between devices: 37.2 us -> 41.9 us  [exchange(): return lax.ppermute(x, axis, [(i, i ^ step) for i in range(size)])]
    ppermute x29, waiting for transfers between devices: 22.7 us -> 18.6 us  [exchange(): return lax.ppermute(x, axis, [(i, i ^ step) for i in range(size)])]
    ppermute x1, waiting for transfers between devices: 4.72 us -> 1.82 us  [local(): out_one = lax.ppermute(inner_late, CHIP, [(1, 0), (2, 3)])]
  transfers between devices with their start and end apart: 35 -> 35, of which waited for: 14 -> 15; matrix products, arithmetic and copies ran while one was open for 2% -> 2% of each run, Pallas kernels for 15% -> 15%
where the time goes in v6:
time: 117 us
  starting transfers between devices  61.7 us (53%)
  waiting for transfers between devices  26 us (22%)
  Pallas kernels  18.8 us (16%)
  local copies, waits for them, and re-layouts  7.45 us (6%)
  other arithmetic  1.93 us (2%)
    ppermute x29, starting transfers between devices, exchange(): return lax.ppermute(x, axis, [(i, i ^ step) for i in range(size)])  41.9 us
    ppermute x29, waiting for transfers between devices, exchange(): return lax.ppermute(x, axis, [(i, i ^ step) for i in range(size)])  18.6 us
    all_to_all x4, starting transfers between devices, swap(): return lax.all_to_all(blocks, axis, 0, 0, tiled=True)  17.8 us
    unnamed x26, local copies, waits for them, and re-layouts  7.45 us
    all_to_all x4, waiting for transfers between devices, swap(): return lax.all_to_all(blocks, axis, 0, 0, tiled=True)  5.51 us
    pallas_call x1, Pallas kernels, level_two(): pl.pallas_call(functools.partial(level_two_kernel, nodes, count, choices)...  4.21 us
    pallas_call x1, Pallas kernels, level_one(): pl.pallas_call(functools.partial(level_one_kernel, nodes, count), out_sha...  3.95 us
    pallas_call x1, Pallas kernels, form_near(): pl.pallas_call(functools.partial(near_kernel, nodes, choices), out_shape=...  3.76 us
  transfers between devices with their start and end apart: 35, of which 15 were waited for; matrix products, arithmetic and copies ran while one was open for 2% of the time, Pallas kernels for 15%

profile of v6, /device:TPU:0, one launch (start us, length us, event | category | flops | bytes accessed | tf_op | source)
XLA Modules:
  0.0 116.7 jit_solution(13919868776698662690)
XLA Ops:
  2.1 2.7 %collective-permute-start.1 = (bf16[9,128,128]{2,1,0:T(8,128)(2,1)S(1)}, bf16[9,128,128]{2,1,0:T(8,128)(2,1)S(1)}, u32[]{:S(2)}, u32[]{:S(2)}) collective-permute-start(bf16[9,128,128]{2,1,0:T(8,128)(2,1)S(1)} %pad_maximum_fusion.refs_0_.refs_4_), channel_id=1, source_target_pairs={{0,2},{2,0},{4,6},{6,4},{1,3},{3,1},{5,7},{7,5},{8,10},{10,8},{12,... | collective-permute-start | bytes 884744 | tf_op jit(solution)/shard_map/ppermute | solution.py:341
  5.5 4.1 %all-to-all-start = ((bf16[4,2,128,128]{3,2,1,0:T(8,128)(2,1)}), bf16[4,2,128,128]{3,2,1,0:T(8,128)(2,1)}, u32[]{:S(2)}, u32[]{:S(2)}) async-start(bf16[4,2,128,128]{3,2,1,0:T(8,128)(2,1)} %bitcast.14), calls=%async_computation | async-start | bytes 524288 | tf_op jit(solution)/shard_map/all_to_all | solution.py:362
  10.5 5.1 %all-to-all-done = bf16[4,2,128,128]{3,2,1,0:T(8,128)(2,1)} async-done(((bf16[4,2,128,128]{3,2,1,0:T(8,128)(2,1)}), bf16[4,2,128,128]{3,2,1,0:T(8,128)(2,1)}, u32[]{:S(2)}, u32[]{:S(2)}) %all-to-all-start) | async-done | bytes 262176 | tf_op jit(solution)/shard_map/all_to_all | solution.py:362
  15.6 5.4 %all-to-all-start.1 = ((bf16[4,2,128,128]{3,2,1,0:T(8,128)(2,1)}), bf16[4,2,128,128]{3,2,1,0:T(8,128)(2,1)S(1)}, u32[]{:S(2)}, u32[]{:S(2)}) async-start(bf16[4,2,128,128]{3,2,1,0:T(8,128)(2,1)} %all-to-all-done), calls=%async_computation.1 | async-start | bytes 524288 | tf_op jit(solution)/shard_map/all_to_all | solution.py:362
  22.9 1.6 %collective-permute-start.8 = (bf16[2,128,128]{2,1,0:T(8,128)(2,1)S(1)}, bf16[2,128,128]{2,1,0:T(8,128)(2,1)S(1)}, u32[]{:S(2)}, u32[]{:S(2)}) collective-permute-start(bf16[2,128,128]{2,1,0:T(8,128)(2,1)S(1)} %get-tuple-element.61), channel_id=1, source_target_pairs={{0,24},{8,16},{16,8},{24,0},{1,25},{9,17},{17,9},{25,1},{2,26},{10... | collective-permute-start | bytes 196616 | tf_op jit(solution)/shard_map/ppermute | solution.py:341
  26.6 1.5 %collective-permute-done.8.refs_3_ = bf16[2,128,128]{2,1,0:T(8,128)(2,1)S(1)} collective-permute-done((bf16[2,128,128]{2,1,0:T(8,128)(2,1)S(1)}, bf16[2,128,128]{2,1,0:T(8,128)(2,1)S(1)}, u32[]{:S(2)}, u32[]{:S(2)}) %collective-permute-start.8) | collective-permute-done | bytes 65568 | tf_op jit(solution)/shard_map/ppermute | solution.py:341
  29.1 4.7 %all-to-all-start.2 = ((bf16[4,2,128,128]{3,2,1,0:T(8,128)(2,1)}), bf16[4,2,128,128]{3,2,1,0:T(8,128)(2,1)S(1)}, u32[]{:S(2)}, u32[]{:S(2)}) async-start(bf16[4,2,128,128]{3,2,1,0:T(8,128)(2,1)} %join_groups.1), calls=%async_computation.2 | async-start | bytes 524288 | tf_op jit(solution)/shard_map/all_to_all | solution.py:362
  37.4 3.9 %collective-permute-start.9 = (bf16[9,128,128]{2,1,0:T(8,128)(2,1)S(1)}, bf16[9,128,128]{2,1,0:T(8,128)(2,1)S(1)}, u32[]{:S(2)}, u32[]{:S(2)}) collective-permute-start(bf16[9,128,128]{2,1,0:T(8,128)(2,1)S(1)} %broadcast_select_fusion), channel_id=1, source_target_pairs={{0,6},{2,4},{4,2},{6,0},{1,7},{3,5},{5,3},{7,1},{8,14},{10,12},{12... | collective-permute-start | bytes 884744 | tf_op jit(solution)/shard_map/ppermute | solution.py:341
  42.6 2.2 %copy-done = bf16[16,8,128,128]{3,2,1,0:T(8,128)(2,1)S(1)} copy-done((bf16[16,8,128,128]{3,2,1,0:T(8,128)(2,1)S(1)}, bf16[16,8,128,128]{3,2,1,0:T(8,128)(2,1)}, u32[]{:S(2)}) %copy-start) | copy-done | bytes 4194328
  44.7 2.4 %pair.1.inverse = bf16[2,16,8,128,128]{4,3,2,1,0:T(8,128)(2,1)S(1)} custom-call(bf16[16,8,128,128]{3,2,1,0:T(8,128)(2,1)S(1)} %copy-done, bf16[16,8,128,128]{3,2,1,0:T(8,128)(2,1)} %collective-permute-done.sibling), custom_call_target="tpu_custom_call" | custom-call | tf_op jit(solution)/shard_map/pair/pallas_call | solution.py:51
  47.2 3.9 %level_one.1.ours = bf16[4,8,128,128]{3,2,1,0:T(8,128)(2,1)} custom-call(s32[8,32]{1,0:T(8,128)S(1)} %copy-done.7, bf16[2,16,8,128,128]{4,3,2,1,0:T(8,128)(2,1)S(1)} %pair.1.inverse, bf16[4,2,128,128]{3,2,1,0:T(8,128)(2,1)S(1)} %all-to-all-done.1.refs_0_, bf16[4,2,128,128]{3,2,1,0:T(8,128)(2,1)S(1)} %collective-permute-done.3.refs_1_, ...), custom_call_target="tpu_custom_call" | custom-call | flops 1073741824 | bytes 12582912 | tf_op jit(solution)/shard_map/level_one/pallas_call | solution.py:292
  51.1 1.8 %collective-permute-done.10.refs_3_.refs_7_ = bf16[9,128,128]{2,1,0:T(8,128)(2,1)S(1)} collective-permute-done((bf16[9,128,128]{2,1,0:T(8,128)(2,1)S(1)}, bf16[9,128,128]{2,1,0:T(8,128)(2,1)S(1)}, u32[]{:S(2)}, u32[]{:S(2)}) %collective-permute-start.10) | collective-permute-done | bytes 294944 | tf_op jit(solution)/shard_map/ppermute | solution.py:398
  53.0 3.6 %all-to-all-start.3 = ((bf16[4,8,128,128]{3,2,1,0:T(8,128)(2,1)}), bf16[4,8,128,128]{3,2,1,0:T(8,128)(2,1)S(1)}, u32[]{:S(2)}, u32[]{:S(2)}) async-start(bf16[4,8,128,128]{3,2,1,0:T(8,128)(2,1)} %level_one.1.ours), calls=%async_computation.3 | async-start | bytes 2097152 | tf_op jit(solution)/shard_map/all_to_all | solution.py:362
  58.5 1.6 %collective-permute-start.14 = (bf16[4,2,128,128]{3,2,1,0:T(8,128)(2,1)S(1)}, bf16[4,2,128,128]{3,2,1,0:T(8,128)(2,1)S(1)}, u32[]{:S(2)}, u32[]{:S(2)}) collective-permute-start(bf16[4,2,128,128]{3,2,1,0:T(8,128)(2,1)S(1)} %all-to-all-done.2.refs_0_), channel_id=1, source_target_pairs={{0,24},{8,16},{16,8},{24,0},{1,25},{9,17},{17,9},{25,1},{2,26},{10... | collective-permute-start | bytes 786440 | tf_op jit(solution)/shard_map/ppermute | solution.py:341
  60.1 2.2 %copy-done.1 = bf16[16,8,128,128]{3,2,1,0:T(8,128)(2,1)S(1)} copy-done((bf16[16,8,128,128]{3,2,1,0:T(8,128)(2,1)S(1)}, bf16[16,8,128,128]{3,2,1,0:T(8,128)(2,1)}, u32[]{:S(2)}) %copy-start.1) | copy-done | bytes 4194328
  62.3 3.8 %form_near.1 = (bf16[4,8,128,128]{3,2,1,0:T(8,128)(2,1)S(1)}, bf16[4,128,128]{2,1,0:T(8,128)(2,1)S(1)}, bf16[2,16,8,128,128]{4,3,2,1,0:T(8,128)(2,1)S(1)}) custom-call(s32[8]{0:T(128)S(1)} %copy-done.9, s32[8,32]{1,0:T(8,128)S(1)} %copy-done.8, bf16[16,8,128,128]{3,2,1,0:T(8,128)(2,1)S(1)} %copy-done.1, ...), custom_call_target="tpu_custom_call" | custom-call | tf_op jit(solution)/shard_map/form_near/pallas_call | solution.py:306
  66.1 4.1 %collective-permute-done.13.refs_2_ = bf16[4,2,128,128]{3,2,1,0:T(8,128)(2,1)S(1)} collective-permute-done((bf16[4,2,128,128]{3,2,1,0:T(8,128)(2,1)S(1)}, bf16[4,2,128,128]{3,2,1,0:T(8,128)(2,1)S(1)}, u32[]{:S(2)}, u32[]{:S(2)}) %collective-permute-start.13) | collective-permute-done | bytes 262176 | tf_op jit(solution)/shard_map/ppermute | solution.py:341
  70.3 1.9 %collective-permute-done.14.refs_3_ = bf16[4,2,128,128]{3,2,1,0:T(8,128)(2,1)S(1)} collective-permute-done((bf16[4,2,128,128]{3,2,1,0:T(8,128)(2,1)S(1)}, bf16[4,2,128,128]{3,2,1,0:T(8,128)(2,1)S(1)}, u32[]{:S(2)}, u32[]{:S(2)}) %collective-permute-start.14) | collective-permute-done | bytes 262176 | tf_op jit(solution)/shard_map/ppermute | solution.py:341
  72.1 4.2 %level_two.1 = (bf16[8,128,128]{2,1,0:T(8,128)(2,1)S(1)}, bf16[8,128,128]{2,1,0:T(8,128)(2,1)S(1)}, bf16[8,128,128]{2,1,0:T(8,128)(2,1)S(1)}, bf16[8,128,128]{2,...) custom-call(s32[8,32]{1,0:T(8,128)S(1)} %copy-done.7, ...), custom_call_target="tpu_custom_call" | custom-call | flops 1476395008 | bytes 16777216 | tf_op jit(solution)/shard_map/level_two/pallas_call | solution.py:327
  78.5 2.0 %collective-permute-start.15 = (bf16[2,128,128]{2,1,0:T(8,128)(2,1)}, bf16[2,128,128]{2,1,0:T(8,128)(2,1)S(1)}, u32[]{:S(2)}, u32[]{:S(2)}) collective-permute-start(bf16[2,128,128]{2,1,0:T(8,128)(2,1)} %get-tuple-element.81), channel_id=1, source_target_pairs={{0,2},{2,0},{4,6},{6,4},{1,3},{3,1},{5,7},{7,5},{8,10},{10,8},{12,... | collective-permute-start | bytes 196616 | tf_op jit(solution)/shard_map/ppermute | solution.py:341
  80.5 2.4 %collective-permute-start.16 = (bf16[2,128,128]{2,1,0:T(8,128)(2,1)}, bf16[2,128,128]{2,1,0:T(8,128)(2,1)S(1)}, u32[]{:S(2)}, u32[]{:S(2)}) collective-permute-start(bf16[2,128,128]{2,1,0:T(8,128)(2,1)} %get-tuple-element.82), channel_id=1, source_target_pairs={{0,4},{2,6},{4,0},{6,2},{1,5},{3,7},{5,1},{7,3},{8,12},{10,14},{12... | collective-permute-start | bytes 196616 | tf_op jit(solution)/shard_map/ppermute | solution.py:341
  84.4 1.7 %collective-permute-start.19 = (bf16[128,128]{1,0:T(8,128)(2,1)S(1)}, bf16[128,128]{1,0:T(8,128)(2,1)S(1)}, u32[]{:S(2)}, u32[]{:S(2)}) collective-permute-start(bf16[128,128]{1,0:T(8,128)(2,1)S(1)} %get-tuple-element.85), channel_id=1, source_target_pairs={{0,16},{8,24},{16,0},{24,8},{1,17},{9,25},{17,1},{25,9},{2,18},{10... | collective-permute-start | bytes 98312 | tf_op jit(solution)/shard_map/ppermute | solution.py:341
  87.8 1.5 %collective-permute-start.22 = (bf16[8,128,128]{2,1,0:T(8,128)(2,1)}, bf16[8,128,128]{2,1,0:T(8,128)(2,1)S(1)}, u32[]{:S(2)}, u32[]{:S(2)}) collective-permute-start(bf16[8,128,128]{2,1,0:T(8,128)(2,1)} %copy-done.12), channel_id=1, source_target_pairs={{0,4},{2,6},{4,0},{6,2},{1,5},{3,7},{5,1},{7,3},{8,12},{10,14},{12... | collective-permute-start | bytes 786440 | tf_op jit(solution)/shard_map/ppermute | solution.py:341
  89.3 1.9 %collective-permute-start.23 = (bf16[8,128,128]{2,1,0:T(8,128)(2,1)}, bf16[8,128,128]{2,1,0:T(8,128)(2,1)S(1)}, u32[]{:S(2)}, u32[]{:S(2)}) collective-permute-start(bf16[8,128,128]{2,1,0:T(8,128)(2,1)} %copy-done.11), channel_id=1, source_target_pairs={{0,6},{2,4},{4,2},{6,0},{1,7},{3,5},{5,3},{7,1},{8,14},{10,12},{12... | collective-permute-start | bytes 786440 | tf_op jit(solution)/shard_map/ppermute | solution.py:341
  94.6 1.7 %collective-permute-start.29 = (bf16[2,128,128]{2,1,0:T(8,128)(2,1)S(1)}, bf16[2,128,128]{2,1,0:T(8,128)(2,1)S(1)}, u32[]{:S(2)}, u32[]{:S(2)}) collective-permute-start(bf16[2,128,128]{2,1,0:T(8,128)(2,1)S(1)} %add_convert_fusion.refs_4_), channel_id=1, source_target_pairs={{0,16},{8,24},{16,0},{24,8},{1,17},{9,25},{17,1},{25,9},{2,18},{10... | collective-permute-start | bytes 196616 | tf_op jit(solution)/shard_map/ppermute | solution.py:341
  96.3 1.5 %collective-permute-start.30 = (bf16[2,128,128]{2,1,0:T(8,128)(2,1)S(1)}, bf16[2,128,128]{2,1,0:T(8,128)(2,1)S(1)}, u32[]{:S(2)}, u32[]{:S(2)}) collective-permute-start(bf16[2,128,128]{2,1,0:T(8,128)(2,1)S(1)} %add_convert_fusion.refs_4_), channel_id=1, source_target_pairs={{0,24},{8,16},{16,8},{24,0},{1,25},{9,17},{17,9},{25,1},{2,26},{10... | collective-permute-start | bytes 196616 | tf_op jit(solution)/shard_map/ppermute | solution.py:341
  98.8 1.8 %collective-permute-start.25 = (bf16[128,128]{1,0:T(8,128)(2,1)S(1)}, bf16[128,128]{1,0:T(8,128)(2,1)S(1)}, u32[]{:S(2)}, u32[]{:S(2)}) collective-permute-start(bf16[128,128]{1,0:T(8,128)(2,1)S(1)} %get-tuple-element.92), channel_id=1, source_target_pairs={{0,2},{2,0},{4,6},{6,4},{1,3},{3,1},{5,7},{7,5},{8,10},{10,8},{12,... | collective-permute-start | bytes 98312 | tf_op jit(solution)/shard_map/ppermute | solution.py:341
  101.4 3.3 %collective-permute-start.26 = (bf16[128,128]{1,0:T(8,128)(2,1)S(1)}, bf16[128,128]{1,0:T(8,128)(2,1)S(1)}, u32[]{:S(2)}, u32[]{:S(2)}) collective-permute-start(bf16[128,128]{1,0:T(8,128)(2,1)S(1)} %get-tuple-element.93), channel_id=1, source_target_pairs={{0,4},{2,6},{4,0},{6,2},{1,5},{3,7},{5,1},{7,3},{8,12},{10,14},{12... | collective-permute-start | bytes 98312 | tf_op jit(solution)/shard_map/ppermute | solution.py:341
  104.8 3.8 %collective-permute-done.25.refs_1_ = bf16[128,128]{1,0:T(8,128)(2,1)S(1)} collective-permute-done((bf16[128,128]{1,0:T(8,128)(2,1)S(1)}, bf16[128,128]{1,0:T(8,128)(2,1)S(1)}, u32[]{:S(2)}, u32[]{:S(2)}) %collective-permute-start.25) | collective-permute-done | bytes 32800 | tf_op jit(solution)/shard_map/ppermute | solution.py:341
  108.6 3.6 %collective-permute-start.27 = (bf16[128,128]{1,0:T(8,128)(2,1)S(1)}, bf16[128,128]{1,0:T(8,128)(2,1)S(1)}, u32[]{:S(2)}, u32[]{:S(2)}) collective-permute-start(bf16[128,128]{1,0:T(8,128)(2,1)S(1)} %get-tuple-element.94), channel_id=1, source_target_pairs={{0,6},{2,4},{4,2},{6,0},{1,7},{3,5},{5,3},{7,1},{8,14},{10,12},{12... | collective-permute-start | bytes 98312 | tf_op jit(solution)/shard_map/ppermute | solution.py:341
  112.1 1.8 %collective-permute-done.26.refs_2_ = bf16[128,128]{1,0:T(8,128)(2,1)S(1)} collective-permute-done((bf16[128,128]{1,0:T(8,128)(2,1)S(1)}, bf16[128,128]{1,0:T(8,128)(2,1)S(1)}, u32[]{:S(2)}, u32[]{:S(2)}) %collective-permute-start.26) | collective-permute-done | bytes 32800 | tf_op jit(solution)/shard_map/ppermute | solution.py:341
  114.4 1.5 %form_last.1 = (bf16[128,128]{1,0:T(8,128)(2,1)}, bf16[128,128]{1,0:T(8,128)(2,1)}) custom-call(s32[8]{0:T(128)S(1)} %copy-done.9, bf16[128,128]{1,0:T(8,128)(2,1)S(1)} %bitcast.18, f32[128,128]{1,0:T(8,128)S(1)} %bitcast.20, bf16[128,128]{1,0:T(8,128)(2,1)S(1)} %get-tuple-element.91.refs_0_, bf16[128,128]{1,0:T(8,128)(2,1)S(1)} %collective-permute-done.25.refs_1_, ...), custom_call_target="tpu_custom_call" | custom-call | tf_op jit(solution)/shard_map/form_last/pallas_call | solution.py:277
  (78 shorter events, 26.9 us)
Async XLA Ops:
  0.6 40.6 %collective-permute-start = (bf16[16,8,128,128]{3,2,1,0:T(8,128)(2,1)}, bf16[16,8,128,128]{3,2,1,0:T(8,128)(2,1)}, u32[]{:S(2)}, u32[]{:S(2)}) collective-permute-start(bf16[16,8,128,128]{3,2,1,0:T(8,128)(2,1)} %own.3), channel_id=1, source_target_pairs={{0,1},{1,0},{2,3},{3,2},{4,5},{5,4},{6,7},{7,6},{8,9},{9,8},{10,11... | collective-permute-start | bytes 12582920 | tf_op jit(solution)/shard_map/ppermute | solution.py:341
  2.1 13.5 %collective-permute-start.1 = (bf16[9,128,128]{2,1,0:T(8,128)(2,1)S(1)}, bf16[9,128,128]{2,1,0:T(8,128)(2,1)S(1)}, u32[]{:S(2)}, u32[]{:S(2)}) collective-permute-start(bf16[9,128,128]{2,1,0:T(8,128)(2,1)S(1)} %pad_maximum_fusion.refs_0_.refs_4_), channel_id=1, source_target_pairs={{0,2},{2,0},{4,6},{6,4},{1,3},{3,1},{5,7},{7,5},{8,10},{10,8},{12,... | collective-permute-start | bytes 884744 | tf_op jit(solution)/shard_map/ppermute | solution.py:341
  4.8 10.8 %collective-permute-start.2 = (bf16[9,128,128]{2,1,0:T(8,128)(2,1)S(1)}, bf16[9,128,128]{2,1,0:T(8,128)(2,1)S(1)}, u32[]{:S(2)}, u32[]{:S(2)}) collective-permute-start(bf16[9,128,128]{2,1,0:T(8,128)(2,1)S(1)} %pad_maximum_fusion.refs_0_.refs_4_), channel_id=1, source_target_pairs={{2,4},{4,2},{3,5},{5,3},{10,12},{12,10},{11,13},{13,11},{18,20},{2... | collective-permute-start | bytes 884744 | tf_op jit(solution)/shard_map/ppermute | solution.py:378
  5.5 10.1 %all-to-all-start = ((bf16[4,2,128,128]{3,2,1,0:T(8,128)(2,1)}), bf16[4,2,128,128]{3,2,1,0:T(8,128)(2,1)}, u32[]{:S(2)}, u32[]{:S(2)}) async-start(bf16[4,2,128,128]{3,2,1,0:T(8,128)(2,1)} %bitcast.14), calls=%async_computation | async-start | bytes 524288 | tf_op jit(solution)/shard_map/all_to_all | solution.py:362
  15.6 13.5 %all-to-all-start.1 = ((bf16[4,2,128,128]{3,2,1,0:T(8,128)(2,1)}), bf16[4,2,128,128]{3,2,1,0:T(8,128)(2,1)S(1)}, u32[]{:S(2)}, u32[]{:S(2)}) async-start(bf16[4,2,128,128]{3,2,1,0:T(8,128)(2,1)} %all-to-all-done), calls=%async_computation.1 | async-start | bytes 524288 | tf_op jit(solution)/shard_map/all_to_all | solution.py:362
  21.0 4.7 %collective-permute-start.6 = (bf16[2,128,128]{2,1,0:T(8,128)(2,1)S(1)}, bf16[2,128,128]{2,1,0:T(8,128)(2,1)S(1)}, u32[]{:S(2)}, u32[]{:S(2)}) collective-permute-start(bf16[2,128,128]{2,1,0:T(8,128)(2,1)S(1)} %get-tuple-element.59), channel_id=1, source_target_pairs={{0,8},{8,0},{16,24},{24,16},{1,9},{9,1},{17,25},{25,17},{2,10},{10... | collective-permute-start | bytes 196616 | tf_op jit(solution)/shard_map/ppermute | solution.py:341
  22.3 4.3 %collective-permute-start.7 = (bf16[2,128,128]{2,1,0:T(8,128)(2,1)S(1)}, bf16[2,128,128]{2,1,0:T(8,128)(2,1)S(1)}, u32[]{:S(2)}, u32[]{:S(2)}) collective-permute-start(bf16[2,128,128]{2,1,0:T(8,128)(2,1)S(1)} %get-tuple-element.60), channel_id=1, source_target_pairs={{0,16},{8,24},{16,0},{24,8},{1,17},{9,25},{17,1},{25,9},{2,18},{10... | collective-permute-start | bytes 196616 | tf_op jit(solution)/shard_map/ppermute | solution.py:341
  22.9 5.2 %collective-permute-start.8 = (bf16[2,128,128]{2,1,0:T(8,128)(2,1)S(1)}, bf16[2,128,128]{2,1,0:T(8,128)(2,1)S(1)}, u32[]{:S(2)}, u32[]{:S(2)}) collective-permute-start(bf16[2,128,128]{2,1,0:T(8,128)(2,1)S(1)} %get-tuple-element.61), channel_id=1, source_target_pairs={{0,24},{8,16},{16,8},{24,0},{1,25},{9,17},{17,9},{25,1},{2,26},{10... | collective-permute-start | bytes 196616 | tf_op jit(solution)/shard_map/ppermute | solution.py:341
  29.1 23.8 %all-to-all-start.2 = ((bf16[4,2,128,128]{3,2,1,0:T(8,128)(2,1)}), bf16[4,2,128,128]{3,2,1,0:T(8,128)(2,1)S(1)}, u32[]{:S(2)}, u32[]{:S(2)}) async-start(bf16[4,2,128,128]{3,2,1,0:T(8,128)(2,1)} %join_groups.1), calls=%async_computation.2 | async-start | bytes 524288 | tf_op jit(solution)/shard_map/all_to_all | solution.py:362
  33.8 13.3 %collective-permute-start.3 = (bf16[4,2,128,128]{3,2,1,0:T(8,128)(2,1)S(1)}, bf16[4,2,128,128]{3,2,1,0:T(8,128)(2,1)S(1)}, u32[]{:S(2)}, u32[]{:S(2)}) collective-permute-start(bf16[4,2,128,128]{3,2,1,0:T(8,128)(2,1)S(1)} %all-to-all-done.1.refs_0_), channel_id=1, source_target_pairs={{0,8},{8,0},{16,24},{24,16},{1,9},{9,1},{17,25},{25,17},{2,10},{10... | collective-permute-start | bytes 786440 | tf_op jit(solution)/shard_map/ppermute | solution.py:341
  35.3 11.9 %collective-permute-start.4 = (bf16[4,2,128,128]{3,2,1,0:T(8,128)(2,1)S(1)}, bf16[4,2,128,128]{3,2,1,0:T(8,128)(2,1)S(1)}, u32[]{:S(2)}, u32[]{:S(2)}) collective-permute-start(bf16[4,2,128,128]{3,2,1,0:T(8,128)(2,1)S(1)} %all-to-all-done.1.refs_0_), channel_id=1, source_target_pairs={{0,16},{8,24},{16,0},{24,8},{1,17},{9,25},{17,1},{25,9},{2,18},{10... | collective-permute-start | bytes 786440 | tf_op jit(solution)/shard_map/ppermute | solution.py:341
  36.0 11.1 %collective-permute-start.5 = (bf16[4,2,128,128]{3,2,1,0:T(8,128)(2,1)S(1)}, bf16[4,2,128,128]{3,2,1,0:T(8,128)(2,1)S(1)}, u32[]{:S(2)}, u32[]{:S(2)}) collective-permute-start(bf16[4,2,128,128]{3,2,1,0:T(8,128)(2,1)S(1)} %all-to-all-done.1.refs_0_), channel_id=1, source_target_pairs={{0,24},{8,16},{16,8},{24,0},{1,25},{9,17},{17,9},{25,1},{2,26},{10... | collective-permute-start | bytes 786440 | tf_op jit(solution)/shard_map/ppermute | solution.py:341
  37.4 13.8 %collective-permute-start.9 = (bf16[9,128,128]{2,1,0:T(8,128)(2,1)S(1)}, bf16[9,128,128]{2,1,0:T(8,128)(2,1)S(1)}, u32[]{:S(2)}, u32[]{:S(2)}) collective-permute-start(bf16[9,128,128]{2,1,0:T(8,128)(2,1)S(1)} %broadcast_select_fusion), channel_id=1, source_target_pairs={{0,6},{2,4},{4,2},{6,0},{1,7},{3,5},{5,3},{7,1},{8,14},{10,12},{12... | collective-permute-start | bytes 884744 | tf_op jit(solution)/shard_map/ppermute | solution.py:341
  41.3 11.7 %collective-permute-start.10 = (bf16[9,128,128]{2,1,0:T(8,128)(2,1)S(1)}, bf16[9,128,128]{2,1,0:T(8,128)(2,1)S(1)}, u32[]{:S(2)}, u32[]{:S(2)}) collective-permute-start(bf16[9,128,128]{2,1,0:T(8,128)(2,1)S(1)} %collective-permute-done.2.refs_4_.refs_8_), channel_id=1, source_target_pairs={{2,0},{4,6},{3,1},{5,7},{10,8},{12,14},{11,9},{13,15},{18,16},{20,... | collective-permute-start | bytes 884744 | tf_op jit(solution)/shard_map/ppermute | solution.py:398
  53.0 29.9 %all-to-all-start.3 = ((bf16[4,8,128,128]{3,2,1,0:T(8,128)(2,1)}), bf16[4,8,128,128]{3,2,1,0:T(8,128)(2,1)S(1)}, u32[]{:S(2)}, u32[]{:S(2)}) async-start(bf16[4,8,128,128]{3,2,1,0:T(8,128)(2,1)} %level_one.1.ours), calls=%async_computation.3 | async-start | bytes 2097152 | tf_op jit(solution)/shard_map/all_to_all | solution.py:362
  56.6 9.5 %collective-permute-start.12 = (bf16[4,2,128,128]{3,2,1,0:T(8,128)(2,1)S(1)}, bf16[4,2,128,128]{3,2,1,0:T(8,128)(2,1)S(1)}, u32[]{:S(2)}, u32[]{:S(2)}) collective-permute-start(bf16[4,2,128,128]{3,2,1,0:T(8,128)(2,1)S(1)} %all-to-all-done.2.refs_0_), channel_id=1, source_target_pairs={{0,8},{8,0},{16,24},{24,16},{1,9},{9,1},{17,25},{25,17},{2,10},{10... | collective-permute-start | bytes 786440 | tf_op jit(solution)/shard_map/ppermute | solution.py:341
  57.8 12.5 %collective-permute-start.13 = (bf16[4,2,128,128]{3,2,1,0:T(8,128)(2,1)S(1)}, bf16[4,2,128,128]{3,2,1,0:T(8,128)(2,1)S(1)}, u32[]{:S(2)}, u32[]{:S(2)}) collective-permute-start(bf16[4,2,128,128]{3,2,1,0:T(8,128)(2,1)S(1)} %all-to-all-done.2.refs_0_), channel_id=1, source_target_pairs={{0,16},{8,24},{16,0},{24,8},{1,17},{9,25},{17,1},{25,9},{2,18},{10... | collective-permute-start | bytes 786440 | tf_op jit(solution)/shard_map/ppermute | solution.py:341
  58.5 13.6 %collective-permute-start.14 = (bf16[4,2,128,128]{3,2,1,0:T(8,128)(2,1)S(1)}, bf16[4,2,128,128]{3,2,1,0:T(8,128)(2,1)S(1)}, u32[]{:S(2)}, u32[]{:S(2)}) collective-permute-start(bf16[4,2,128,128]{3,2,1,0:T(8,128)(2,1)S(1)} %all-to-all-done.2.refs_0_), channel_id=1, source_target_pairs={{0,24},{8,16},{16,8},{24,0},{1,25},{9,17},{17,9},{25,1},{2,26},{10... | collective-permute-start | bytes 786440 | tf_op jit(solution)/shard_map/ppermute | solution.py:341
  78.5 7.6 %collective-permute-start.15 = (bf16[2,128,128]{2,1,0:T(8,128)(2,1)}, bf16[2,128,128]{2,1,0:T(8,128)(2,1)S(1)}, u32[]{:S(2)}, u32[]{:S(2)}) collective-permute-start(bf16[2,128,128]{2,1,0:T(8,128)(2,1)} %get-tuple-element.81), channel_id=1, source_target_pairs={{0,2},{2,0},{4,6},{6,4},{1,3},{3,1},{5,7},{7,5},{8,10},{10,8},{12,... | collective-permute-start | bytes 196616 | tf_op jit(solution)/shard_map/ppermute | solution.py:341
  80.5 7.4 %collective-permute-start.16 = (bf16[2,128,128]{2,1,0:T(8,128)(2,1)}, bf16[2,128,128]{2,1,0:T(8,128)(2,1)S(1)}, u32[]{:S(2)}, u32[]{:S(2)}) collective-permute-start(bf16[2,128,128]{2,1,0:T(8,128)(2,1)} %get-tuple-element.82), channel_id=1, source_target_pairs={{0,4},{2,6},{4,0},{6,2},{1,5},{3,7},{5,1},{7,3},{8,12},{10,14},{12... | collective-permute-start | bytes 196616 | tf_op jit(solution)/shard_map/ppermute | solution.py:341
  82.8 6.5 %collective-permute-start.17 = (bf16[2,128,128]{2,1,0:T(8,128)(2,1)S(1)}, bf16[2,128,128]{2,1,0:T(8,128)(2,1)S(1)}, u32[]{:S(2)}, u32[]{:S(2)}) collective-permute-start(bf16[2,128,128]{2,1,0:T(8,128)(2,1)S(1)} %get-tuple-element.83), channel_id=1, source_target_pairs={{0,6},{2,4},{4,2},{6,0},{1,7},{3,5},{5,3},{7,1},{8,14},{10,12},{12... | collective-permute-start | bytes 196616 | tf_op jit(solution)/shard_map/ppermute | solution.py:341
  83.8 7.4 %collective-permute-start.18 = (bf16[128,128]{1,0:T(8,128)(2,1)S(1)}, bf16[128,128]{1,0:T(8,128)(2,1)S(1)}, u32[]{:S(2)}, u32[]{:S(2)}) collective-permute-start(bf16[128,128]{1,0:T(8,128)(2,1)S(1)} %get-tuple-element.85), channel_id=1, source_target_pairs={{0,8},{8,0},{16,24},{24,16},{1,9},{9,1},{17,25},{25,17},{2,10},{10... | collective-permute-start | bytes 98312 | tf_op jit(solution)/shard_map/ppermute | solution.py:341
  84.4 6.8 %collective-permute-start.19 = (bf16[128,128]{1,0:T(8,128)(2,1)S(1)}, bf16[128,128]{1,0:T(8,128)(2,1)S(1)}, u32[]{:S(2)}, u32[]{:S(2)}) collective-permute-start(bf16[128,128]{1,0:T(8,128)(2,1)S(1)} %get-tuple-element.85), channel_id=1, source_target_pairs={{0,16},{8,24},{16,0},{24,8},{1,17},{9,25},{17,1},{25,9},{2,18},{10... | collective-permute-start | bytes 98312 | tf_op jit(solution)/shard_map/ppermute | solution.py:341
  86.1 5.1 %collective-permute-start.20 = (bf16[128,128]{1,0:T(8,128)(2,1)S(1)}, bf16[128,128]{1,0:T(8,128)(2,1)S(1)}, u32[]{:S(2)}, u32[]{:S(2)}) collective-permute-start(bf16[128,128]{1,0:T(8,128)(2,1)S(1)} %get-tuple-element.85), channel_id=1, source_target_pairs={{0,24},{8,16},{16,8},{24,0},{1,25},{9,17},{17,9},{25,1},{2,26},{10... | collective-permute-start | bytes 98312 | tf_op jit(solution)/shard_map/ppermute | solution.py:341
  87.8 28.0 %collective-permute-start.22 = (bf16[8,128,128]{2,1,0:T(8,128)(2,1)}, bf16[8,128,128]{2,1,0:T(8,128)(2,1)S(1)}, u32[]{:S(2)}, u32[]{:S(2)}) collective-permute-start(bf16[8,128,128]{2,1,0:T(8,128)(2,1)} %copy-done.12), channel_id=1, source_target_pairs={{0,4},{2,6},{4,0},{6,2},{1,5},{3,7},{5,1},{7,3},{8,12},{10,14},{12... | collective-permute-start | bytes 786440 | tf_op jit(solution)/shard_map/ppermute | solution.py:341
  89.3 26.6 %collective-permute-start.23 = (bf16[8,128,128]{2,1,0:T(8,128)(2,1)}, bf16[8,128,128]{2,1,0:T(8,128)(2,1)S(1)}, u32[]{:S(2)}, u32[]{:S(2)}) collective-permute-start(bf16[8,128,128]{2,1,0:T(8,128)(2,1)} %copy-done.11), channel_id=1, source_target_pairs={{0,6},{2,4},{4,2},{6,0},{1,7},{3,5},{5,3},{7,1},{8,14},{10,12},{12... | collective-permute-start | bytes 786440 | tf_op jit(solution)/shard_map/ppermute | solution.py:341
  91.2 5.0 %collective-permute-start.28 = (bf16[2,128,128]{2,1,0:T(8,128)(2,1)S(1)}, bf16[2,128,128]{2,1,0:T(8,128)(2,1)S(1)}, u32[]{:S(2)}, u32[]{:S(2)}) collective-permute-start(bf16[2,128,128]{2,1,0:T(8,128)(2,1)S(1)} %add_convert_fusion.refs_4_), channel_id=1, source_target_pairs={{0,8},{8,0},{16,24},{24,16},{1,9},{9,1},{17,25},{25,17},{2,10},{10... | collective-permute-start | bytes 196616 | tf_op jit(solution)/shard_map/ppermute | solution.py:341
  91.9 24.0 %collective-permute-start.21 = (bf16[8,128,128]{2,1,0:T(8,128)(2,1)}, bf16[8,128,128]{2,1,0:T(8,128)(2,1)S(1)}, u32[]{:S(2)}, u32[]{:S(2)}) collective-permute-start(bf16[8,128,128]{2,1,0:T(8,128)(2,1)} %copy-done.10), channel_id=1, source_target_pairs={{0,2},{2,0},{4,6},{6,4},{1,3},{3,1},{5,7},{7,5},{8,10},{10,8},{12,... | collective-permute-start | bytes 786440 | tf_op jit(solution)/shard_map/ppermute | solution.py:341
  96.3 5.2 %collective-permute-start.30 = (bf16[2,128,128]{2,1,0:T(8,128)(2,1)S(1)}, bf16[2,128,128]{2,1,0:T(8,128)(2,1)S(1)}, u32[]{:S(2)}, u32[]{:S(2)}) collective-permute-start(bf16[2,128,128]{2,1,0:T(8,128)(2,1)S(1)} %add_convert_fusion.refs_4_), channel_id=1, source_target_pairs={{0,24},{8,16},{16,8},{24,0},{1,25},{9,17},{17,9},{25,1},{2,26},{10... | collective-permute-start | bytes 196616 | tf_op jit(solution)/shard_map/ppermute | solution.py:341
  98.8 9.7 %collective-permute-start.25 = (bf16[128,128]{1,0:T(8,128)(2,1)S(1)}, bf16[128,128]{1,0:T(8,128)(2,1)S(1)}, u32[]{:S(2)}, u32[]{:S(2)}) collective-permute-start(bf16[128,128]{1,0:T(8,128)(2,1)S(1)} %get-tuple-element.92), channel_id=1, source_target_pairs={{0,2},{2,0},{4,6},{6,4},{1,3},{3,1},{5,7},{7,5},{8,10},{10,8},{12,... | collective-permute-start | bytes 98312 | tf_op jit(solution)/shard_map/ppermute | solution.py:341
  101.4 12.5 %collective-permute-start.26 = (bf16[128,128]{1,0:T(8,128)(2,1)S(1)}, bf16[128,128]{1,0:T(8,128)(2,1)S(1)}, u32[]{:S(2)}, u32[]{:S(2)}) collective-permute-start(bf16[128,128]{1,0:T(8,128)(2,1)S(1)} %get-tuple-element.93), channel_id=1, source_target_pairs={{0,4},{2,6},{4,0},{6,2},{1,5},{3,7},{5,1},{7,3},{8,12},{10,14},{12... | collective-permute-start | bytes 98312 | tf_op jit(solution)/shard_map/ppermute | solution.py:341
  108.6 5.8 %collective-permute-start.27 = (bf16[128,128]{1,0:T(8,128)(2,1)S(1)}, bf16[128,128]{1,0:T(8,128)(2,1)S(1)}, u32[]{:S(2)}, u32[]{:S(2)}) collective-permute-start(bf16[128,128]{1,0:T(8,128)(2,1)S(1)} %get-tuple-element.94), channel_id=1, source_target_pairs={{0,6},{2,4},{4,2},{6,0},{1,7},{3,5},{5,3},{7,1},{8,14},{10,12},{12... | collective-permute-start | bytes 98312 | tf_op jit(solution)/shard_map/ppermute | solution.py:341
  (16 other events, 189.1 us)

commit v7 on v6

--- a/solution.py
+++ b/solution.py
@@ -413,10 +413,10 @@
     )
     columns, smalls = outs[:nodes], outs[nodes:]
     parts_small = [smalls[0]] + [exchange(smalls[t], CHIP, t) for t in range(1, nodes)]
-    first = [exchange(columns[t], CHIP, t) for t in range(nodes // 2, nodes)]
+    first = [exchange(columns[2], CHIP, 2)]
     column_one, part = form_column(parts_one, panel_one[0])
     columns, parts_small, parts_diagonal = together(columns, parts_small, spread(part, ROW))
-    parts_two = [exchange(columns[t], CHIP, t) for t in range(1, nodes // 2)] + first
+    parts_two = [exchange(columns[t], CHIP, t) for t in range(1, nodes) if t != 2] + first
     diagonal_one = (base_one[0] - total(parts_diagonal)).astype(BF16)
     chosen = choose(nodes, parent_two, diagonal_one, exchange(diagonal_one, CORE, 1))
     diagonals = [chosen[0]] + [exchange(chosen[t], CHIP, t) for t in range(1, nodes)]

time: 117 us -> 117 us (level)
  starting transfers between devices: 61.7 us -> 60 us
  waiting for transfers between devices: 26 us -> 27.5 us
    ppermute x29, starting transfers between devices: 41.9 us -> 40.3 us  [exchange(): return lax.ppermute(x, axis, [(i, i ^ step) for i in range(size)])]
    ppermute x29, waiting for transfers between devices: 18.6 us -> 20.2 us  [exchange(): return lax.ppermute(x, axis, [(i, i ^ step) for i in range(size)])]
where the time goes in v7:
time: 117 us
  starting transfers between devices  60 us (51%)
  waiting for transfers between devices  27.5 us (24%)
  Pallas kernels  18.8 us (16%)
  local copies, waits for them, and re-layouts  7.45 us (6%)
  other arithmetic  1.93 us (2%)
    ppermute x29, starting transfers between devices, exchange(): return lax.ppermute(x, axis, [(i, i ^ step) for i in range(size)])  40.3 us
    ppermute x29, waiting for transfers between devices, exchange(): return lax.ppermute(x, axis, [(i, i ^ step) for i in range(size)])  20.2 us
    all_to_all x4, starting transfers between devices, swap(): return lax.all_to_all(blocks, axis, 0, 0, tiled=True)  17.8 us
    unnamed x26, local copies, waits for them, and re-layouts  7.45 us
    all_to_all x4, waiting for transfers between devices, swap(): return lax.all_to_all(blocks, axis, 0, 0, tiled=True)  5.51 us
    pallas_call x1, Pallas kernels, level_two(): pl.pallas_call(functools.partial(level_two_kernel, nodes, count, choices)...  4.21 us
    pallas_call x1, Pallas kernels, level_one(): pl.pallas_call(functools.partial(level_one_kernel, nodes, count), out_sha...  3.95 us
    pallas_call x1, Pallas kernels, form_near(): pl.pallas_call(functools.partial(near_kernel, nodes, choices), out_shape=...  3.76 us
  transfers between devices with their start and end apart: 35, of which 15 were waited for; matrix products, arithmetic and copies ran while one was open for 2% of the time, Pallas kernels for 15%

profile of v7, /device:TPU:0, one launch (start us, length us, event | category | flops | bytes accessed | tf_op | source)
XLA Modules:
  0.0 116.6 jit_solution(14708410193309324902)
XLA Ops:
  2.1 2.7 %collective-permute-start.1 = (bf16[9,128,128]{2,1,0:T(8,128)(2,1)S(1)}, bf16[9,128,128]{2,1,0:T(8,128)(2,1)S(1)}, u32[]{:S(2)}, u32[]{:S(2)}) collective-permute-start(bf16[9,128,128]{2,1,0:T(8,128)(2,1)S(1)} %pad_maximum_fusion.refs_0_.refs_4_), channel_id=1, source_target_pairs={{0,2},{2,0},{4,6},{6,4},{1,3},{3,1},{5,7},{7,5},{8,10},{10,8},{12,... | collective-permute-start | bytes 884744 | tf_op jit(solution)/shard_map/ppermute | solution.py:341
  5.5 4.1 %all-to-all-start = ((bf16[4,2,128,128]{3,2,1,0:T(8,128)(2,1)}), bf16[4,2,128,128]{3,2,1,0:T(8,128)(2,1)}, u32[]{:S(2)}, u32[]{:S(2)}) async-start(bf16[4,2,128,128]{3,2,1,0:T(8,128)(2,1)} %bitcast.14), calls=%async_computation | async-start | bytes 524288 | tf_op jit(solution)/shard_map/all_to_all | solution.py:362
  10.5 5.1 %all-to-all-done = bf16[4,2,128,128]{3,2,1,0:T(8,128)(2,1)} async-done(((bf16[4,2,128,128]{3,2,1,0:T(8,128)(2,1)}), bf16[4,2,128,128]{3,2,1,0:T(8,128)(2,1)}, u32[]{:S(2)}, u32[]{:S(2)}) %all-to-all-start) | async-done | bytes 262176 | tf_op jit(solution)/shard_map/all_to_all | solution.py:362
  15.6 5.4 %all-to-all-start.1 = ((bf16[4,2,128,128]{3,2,1,0:T(8,128)(2,1)}), bf16[4,2,128,128]{3,2,1,0:T(8,128)(2,1)S(1)}, u32[]{:S(2)}, u32[]{:S(2)}) async-start(bf16[4,2,128,128]{3,2,1,0:T(8,128)(2,1)} %all-to-all-done), calls=%async_computation.1 | async-start | bytes 524288 | tf_op jit(solution)/shard_map/all_to_all | solution.py:362
  22.9 1.6 %collective-permute-start.8 = (bf16[2,128,128]{2,1,0:T(8,128)(2,1)S(1)}, bf16[2,128,128]{2,1,0:T(8,128)(2,1)S(1)}, u32[]{:S(2)}, u32[]{:S(2)}) collective-permute-start(bf16[2,128,128]{2,1,0:T(8,128)(2,1)S(1)} %get-tuple-element.62), channel_id=1, source_target_pairs={{0,24},{8,16},{16,8},{24,0},{1,25},{9,17},{17,9},{25,1},{2,26},{10... | collective-permute-start | bytes 196616 | tf_op jit(solution)/shard_map/ppermute | solution.py:341
  26.6 1.5 %collective-permute-done.8.refs_3_ = bf16[2,128,128]{2,1,0:T(8,128)(2,1)S(1)} collective-permute-done((bf16[2,128,128]{2,1,0:T(8,128)(2,1)S(1)}, bf16[2,128,128]{2,1,0:T(8,128)(2,1)S(1)}, u32[]{:S(2)}, u32[]{:S(2)}) %collective-permute-start.8) | collective-permute-done | bytes 65568 | tf_op jit(solution)/shard_map/ppermute | solution.py:341
  29.1 4.7 %all-to-all-start.2 = ((bf16[4,2,128,128]{3,2,1,0:T(8,128)(2,1)}), bf16[4,2,128,128]{3,2,1,0:T(8,128)(2,1)S(1)}, u32[]{:S(2)}, u32[]{:S(2)}) async-start(bf16[4,2,128,128]{3,2,1,0:T(8,128)(2,1)} %join_groups.1), calls=%async_computation.2 | async-start | bytes 524288 | tf_op jit(solution)/shard_map/all_to_all | solution.py:362
  33.8 1.4 %collective-permute-start.3 = (bf16[4,2,128,128]{3,2,1,0:T(8,128)(2,1)S(1)}, bf16[4,2,128,128]{3,2,1,0:T(8,128)(2,1)S(1)}, u32[]{:S(2)}, u32[]{:S(2)}) collective-permute-start(bf16[4,2,128,128]{3,2,1,0:T(8,128)(2,1)S(1)} %all-to-all-done.1.refs_0_), channel_id=1, source_target_pairs={{0,8},{8,0},{16,24},{24,16},{1,9},{9,1},{17,25},{25,17},{2,10},{10... | collective-permute-start | bytes 786440 | tf_op jit(solution)/shard_map/ppermute | solution.py:341
  37.4 3.9 %collective-permute-start.9 = (bf16[9,128,128]{2,1,0:T(8,128)(2,1)S(1)}, bf16[9,128,128]{2,1,0:T(8,128)(2,1)S(1)}, u32[]{:S(2)}, u32[]{:S(2)}) collective-permute-start(bf16[9,128,128]{2,1,0:T(8,128)(2,1)S(1)} %broadcast_select_fusion), channel_id=1, source_target_pairs={{0,6},{2,4},{4,2},{6,0},{1,7},{3,5},{5,3},{7,1},{8,14},{10,12},{12... | collective-permute-start | bytes 884744 | tf_op jit(solution)/shard_map/ppermute | solution.py:341
  42.6 2.2 %copy-done = bf16[16,8,128,128]{3,2,1,0:T(8,128)(2,1)S(1)} copy-done((bf16[16,8,128,128]{3,2,1,0:T(8,128)(2,1)S(1)}, bf16[16,8,128,128]{3,2,1,0:T(8,128)(2,1)}, u32[]{:S(2)}) %copy-start) | copy-done | bytes 4194328
  44.7 2.4 %pair.1.inverse = bf16[2,16,8,128,128]{4,3,2,1,0:T(8,128)(2,1)S(1)} custom-call(bf16[16,8,128,128]{3,2,1,0:T(8,128)(2,1)S(1)} %copy-done, bf16[16,8,128,128]{3,2,1,0:T(8,128)(2,1)} %collective-permute-done.sibling), custom_call_target="tpu_custom_call" | custom-call | tf_op jit(solution)/shard_map/pair/pallas_call | solution.py:51
  47.2 3.9 %level_one.1.ours = bf16[4,8,128,128]{3,2,1,0:T(8,128)(2,1)} custom-call(s32[8,32]{1,0:T(8,128)S(1)} %copy-done.7, bf16[2,16,8,128,128]{4,3,2,1,0:T(8,128)(2,1)S(1)} %pair.1.inverse, bf16[4,2,128,128]{3,2,1,0:T(8,128)(2,1)S(1)} %all-to-all-done.1.refs_0_, bf16[4,2,128,128]{3,2,1,0:T(8,128)(2,1)S(1)} %collective-permute-done.3.refs_1_, ...), custom_call_target="tpu_custom_call" | custom-call | flops 1073741824 | bytes 12582912 | tf_op jit(solution)/shard_map/level_one/pallas_call | solution.py:292
  51.1 1.8 %collective-permute-done.10.refs_3_.refs_7_ = bf16[9,128,128]{2,1,0:T(8,128)(2,1)S(1)} collective-permute-done((bf16[9,128,128]{2,1,0:T(8,128)(2,1)S(1)}, bf16[9,128,128]{2,1,0:T(8,128)(2,1)S(1)}, u32[]{:S(2)}, u32[]{:S(2)}) %collective-permute-start.10) | collective-permute-done | bytes 294944 | tf_op jit(solution)/shard_map/ppermute | solution.py:398
  53.0 3.6 %all-to-all-start.3 = ((bf16[4,8,128,128]{3,2,1,0:T(8,128)(2,1)}), bf16[4,8,128,128]{3,2,1,0:T(8,128)(2,1)S(1)}, u32[]{:S(2)}, u32[]{:S(2)}) async-start(bf16[4,8,128,128]{3,2,1,0:T(8,128)(2,1)} %level_one.1.ours), calls=%async_computation.3 | async-start | bytes 2097152 | tf_op jit(solution)/shard_map/all_to_all | solution.py:362
  58.5 1.6 %collective-permute-start.14 = (bf16[4,2,128,128]{3,2,1,0:T(8,128)(2,1)S(1)}, bf16[4,2,128,128]{3,2,1,0:T(8,128)(2,1)S(1)}, u32[]{:S(2)}, u32[]{:S(2)}) collective-permute-start(bf16[4,2,128,128]{3,2,1,0:T(8,128)(2,1)S(1)} %all-to-all-done.2.refs_0_), channel_id=1, source_target_pairs={{0,24},{8,16},{16,8},{24,0},{1,25},{9,17},{17,9},{25,1},{2,26},{10... | collective-permute-start | bytes 786440 | tf_op jit(solution)/shard_map/ppermute | solution.py:341
  60.1 2.2 %copy-done.1 = bf16[16,8,128,128]{3,2,1,0:T(8,128)(2,1)S(1)} copy-done((bf16[16,8,128,128]{3,2,1,0:T(8,128)(2,1)S(1)}, bf16[16,8,128,128]{3,2,1,0:T(8,128)(2,1)}, u32[]{:S(2)}) %copy-start.1) | copy-done | bytes 4194328
  62.3 3.8 %form_near.1 = (bf16[4,8,128,128]{3,2,1,0:T(8,128)(2,1)S(1)}, bf16[4,128,128]{2,1,0:T(8,128)(2,1)S(1)}, bf16[2,16,8,128,128]{4,3,2,1,0:T(8,128)(2,1)S(1)}) custom-call(s32[8]{0:T(128)S(1)} %copy-done.9, s32[8,32]{1,0:T(8,128)S(1)} %copy-done.8, bf16[16,8,128,128]{3,2,1,0:T(8,128)(2,1)S(1)} %copy-done.1, ...), custom_call_target="tpu_custom_call" | custom-call | tf_op jit(solution)/shard_map/form_near/pallas_call | solution.py:306
  66.1 4.1 %collective-permute-done.13.refs_2_ = bf16[4,2,128,128]{3,2,1,0:T(8,128)(2,1)S(1)} collective-permute-done((bf16[4,2,128,128]{3,2,1,0:T(8,128)(2,1)S(1)}, bf16[4,2,128,128]{3,2,1,0:T(8,128)(2,1)S(1)}, u32[]{:S(2)}, u32[]{:S(2)}) %collective-permute-start.13) | collective-permute-done | bytes 262176 | tf_op jit(solution)/shard_map/ppermute | solution.py:341
  70.3 1.9 %collective-permute-done.14.refs_3_ = bf16[4,2,128,128]{3,2,1,0:T(8,128)(2,1)S(1)} collective-permute-done((bf16[4,2,128,128]{3,2,1,0:T(8,128)(2,1)S(1)}, bf16[4,2,128,128]{3,2,1,0:T(8,128)(2,1)S(1)}, u32[]{:S(2)}, u32[]{:S(2)}) %collective-permute-start.14) | collective-permute-done | bytes 262176 | tf_op jit(solution)/shard_map/ppermute | solution.py:341
  72.1 4.2 %level_two.1 = (bf16[8,128,128]{2,1,0:T(8,128)(2,1)S(1)}, bf16[8,128,128]{2,1,0:T(8,128)(2,1)S(1)}, bf16[8,128,128]{2,1,0:T(8,128)(2,1)S(1)}, bf16[8,128,128]{2,...) custom-call(s32[8,32]{1,0:T(8,128)S(1)} %copy-done.7, ...), custom_call_target="tpu_custom_call" | custom-call | flops 1476395008 | bytes 16777216 | tf_op jit(solution)/shard_map/level_two/pallas_call | solution.py:327
  78.5 2.0 %collective-permute-start.15 = (bf16[2,128,128]{2,1,0:T(8,128)(2,1)}, bf16[2,128,128]{2,1,0:T(8,128)(2,1)S(1)}, u32[]{:S(2)}, u32[]{:S(2)}) collective-permute-start(bf16[2,128,128]{2,1,0:T(8,128)(2,1)} %get-tuple-element.82), channel_id=1, source_target_pairs={{0,2},{2,0},{4,6},{6,4},{1,3},{3,1},{5,7},{7,5},{8,10},{10,8},{12,... | collective-permute-start | bytes 196616 | tf_op jit(solution)/shard_map/ppermute | solution.py:341
  80.5 2.4 %collective-permute-start.16 = (bf16[2,128,128]{2,1,0:T(8,128)(2,1)}, bf16[2,128,128]{2,1,0:T(8,128)(2,1)S(1)}, u32[]{:S(2)}, u32[]{:S(2)}) collective-permute-start(bf16[2,128,128]{2,1,0:T(8,128)(2,1)} %get-tuple-element.83), channel_id=1, source_target_pairs={{0,4},{2,6},{4,0},{6,2},{1,5},{3,7},{5,1},{7,3},{8,12},{10,14},{12... | collective-permute-start | bytes 196616 | tf_op jit(solution)/shard_map/ppermute | solution.py:341
  84.4 1.7 %collective-permute-start.19 = (bf16[128,128]{1,0:T(8,128)(2,1)S(1)}, bf16[128,128]{1,0:T(8,128)(2,1)S(1)}, u32[]{:S(2)}, u32[]{:S(2)}) collective-permute-start(bf16[128,128]{1,0:T(8,128)(2,1)S(1)} %get-tuple-element.86), channel_id=1, source_target_pairs={{0,16},{8,24},{16,0},{24,8},{1,17},{9,25},{17,1},{25,9},{2,18},{10... | collective-permute-start | bytes 98312 | tf_op jit(solution)/shard_map/ppermute | solution.py:341
  87.8 1.5 %collective-permute-start.23 = (bf16[8,128,128]{2,1,0:T(8,128)(2,1)}, bf16[8,128,128]{2,1,0:T(8,128)(2,1)S(1)}, u32[]{:S(2)}, u32[]{:S(2)}) collective-permute-start(bf16[8,128,128]{2,1,0:T(8,128)(2,1)} %copy-done.12), channel_id=1, source_target_pairs={{0,4},{2,6},{4,0},{6,2},{1,5},{3,7},{5,1},{7,3},{8,12},{10,14},{12... | collective-permute-start | bytes 786440 | tf_op jit(solution)/shard_map/ppermute | solution.py:341
  89.3 1.6 %collective-permute-done.20 = bf16[128,128]{1,0:T(8,128)(2,1)S(1)} collective-permute-done((bf16[128,128]{1,0:T(8,128)(2,1)S(1)}, bf16[128,128]{1,0:T(8,128)(2,1)S(1)}, u32[]{:S(2)}, u32[]{:S(2)}) %collective-permute-start.20) | collective-permute-done | bytes 32800 | tf_op jit(solution)/shard_map/ppermute | solution.py:341
  92.4 2.9 %collective-permute-start.22 = (bf16[8,128,128]{2,1,0:T(8,128)(2,1)}, bf16[8,128,128]{2,1,0:T(8,128)(2,1)S(1)}, u32[]{:S(2)}, u32[]{:S(2)}) collective-permute-start(bf16[8,128,128]{2,1,0:T(8,128)(2,1)} %copy-done.10), channel_id=1, source_target_pairs={{0,6},{2,4},{4,2},{6,0},{1,7},{3,5},{5,3},{7,1},{8,14},{10,12},{12... | collective-permute-start | bytes 786440 | tf_op jit(solution)/shard_map/ppermute | solution.py:341
  97.5 1.5 %collective-permute-start.29 = (bf16[2,128,128]{2,1,0:T(8,128)(2,1)S(1)}, bf16[2,128,128]{2,1,0:T(8,128)(2,1)S(1)}, u32[]{:S(2)}, u32[]{:S(2)}) collective-permute-start(bf16[2,128,128]{2,1,0:T(8,128)(2,1)S(1)} %add_convert_fusion.refs_4_), channel_id=1, source_target_pairs={{0,16},{8,24},{16,0},{24,8},{1,17},{9,25},{17,1},{25,9},{2,18},{10... | collective-permute-start | bytes 196616 | tf_op jit(solution)/shard_map/ppermute | solution.py:341
  99.0 1.8 %collective-permute-start.30 = (bf16[2,128,128]{2,1,0:T(8,128)(2,1)S(1)}, bf16[2,128,128]{2,1,0:T(8,128)(2,1)S(1)}, u32[]{:S(2)}, u32[]{:S(2)}) collective-permute-start(bf16[2,128,128]{2,1,0:T(8,128)(2,1)S(1)} %add_convert_fusion.refs_4_), channel_id=1, source_target_pairs={{0,24},{8,16},{16,8},{24,0},{1,25},{9,17},{17,9},{25,1},{2,26},{10... | collective-permute-start | bytes 196616 | tf_op jit(solution)/shard_map/ppermute | solution.py:341
  104.8 3.4 %collective-permute-done.25.refs_1_ = bf16[128,128]{1,0:T(8,128)(2,1)S(1)} collective-permute-done((bf16[128,128]{1,0:T(8,128)(2,1)S(1)}, bf16[128,128]{1,0:T(8,128)(2,1)S(1)}, u32[]{:S(2)}, u32[]{:S(2)}) %collective-permute-start.25) | collective-permute-done | bytes 32800 | tf_op jit(solution)/shard_map/ppermute | solution.py:341
  108.1 4.0 %collective-permute-start.27 = (bf16[128,128]{1,0:T(8,128)(2,1)S(1)}, bf16[128,128]{1,0:T(8,128)(2,1)S(1)}, u32[]{:S(2)}, u32[]{:S(2)}) collective-permute-start(bf16[128,128]{1,0:T(8,128)(2,1)S(1)} %get-tuple-element.96), channel_id=1, source_target_pairs={{0,6},{2,4},{4,2},{6,0},{1,7},{3,5},{5,3},{7,1},{8,14},{10,12},{12... | collective-permute-start | bytes 98312 | tf_op jit(solution)/shard_map/ppermute | solution.py:341
  112.1 2.1 %collective-permute-done.26.refs_2_ = bf16[128,128]{1,0:T(8,128)(2,1)S(1)} collective-permute-done((bf16[128,128]{1,0:T(8,128)(2,1)S(1)}, bf16[128,128]{1,0:T(8,128)(2,1)S(1)}, u32[]{:S(2)}, u32[]{:S(2)}) %collective-permute-start.26) | collective-permute-done | bytes 32800 | tf_op jit(solution)/shard_map/ppermute | solution.py:341
  114.3 1.5 %form_last.1 = (bf16[128,128]{1,0:T(8,128)(2,1)}, bf16[128,128]{1,0:T(8,128)(2,1)}) custom-call(s32[8]{0:T(128)S(1)} %copy-done.9, bf16[128,128]{1,0:T(8,128)(2,1)S(1)} %bitcast.18, f32[128,128]{1,0:T(8,128)S(1)} %bitcast.20, bf16[128,128]{1,0:T(8,128)(2,1)S(1)} %get-tuple-element.93.refs_0_, bf16[128,128]{1,0:T(8,128)(2,1)S(1)} %collective-permute-done.25.refs_1_, ...), custom_call_target="tpu_custom_call" | custom-call | tf_op jit(solution)/shard_map/form_last/pallas_call | solution.py:277
  (78 shorter events, 27.4 us)
Async XLA Ops:
  0.6 40.6 %collective-permute-start = (bf16[16,8,128,128]{3,2,1,0:T(8,128)(2,1)}, bf16[16,8,128,128]{3,2,1,0:T(8,128)(2,1)}, u32[]{:S(2)}, u32[]{:S(2)}) collective-permute-start(bf16[16,8,128,128]{3,2,1,0:T(8,128)(2,1)} %own.3), channel_id=1, source_target_pairs={{0,1},{1,0},{2,3},{3,2},{4,5},{5,4},{6,7},{7,6},{8,9},{9,8},{10,11... | collective-permute-start | bytes 12582920 | tf_op jit(solution)/shard_map/ppermute | solution.py:341
  2.1 13.5 %collective-permute-start.1 = (bf16[9,128,128]{2,1,0:T(8,128)(2,1)S(1)}, bf16[9,128,128]{2,1,0:T(8,128)(2,1)S(1)}, u32[]{:S(2)}, u32[]{:S(2)}) collective-permute-start(bf16[9,128,128]{2,1,0:T(8,128)(2,1)S(1)} %pad_maximum_fusion.refs_0_.refs_4_), channel_id=1, source_target_pairs={{0,2},{2,0},{4,6},{6,4},{1,3},{3,1},{5,7},{7,5},{8,10},{10,8},{12,... | collective-permute-start | bytes 884744 | tf_op jit(solution)/shard_map/ppermute | solution.py:341
  4.8 10.8 %collective-permute-start.2 = (bf16[9,128,128]{2,1,0:T(8,128)(2,1)S(1)}, bf16[9,128,128]{2,1,0:T(8,128)(2,1)S(1)}, u32[]{:S(2)}, u32[]{:S(2)}) collective-permute-start(bf16[9,128,128]{2,1,0:T(8,128)(2,1)S(1)} %pad_maximum_fusion.refs_0_.refs_4_), channel_id=1, source_target_pairs={{2,4},{4,2},{3,5},{5,3},{10,12},{12,10},{11,13},{13,11},{18,20},{2... | collective-permute-start | bytes 884744 | tf_op jit(solution)/shard_map/ppermute | solution.py:378
  5.5 10.1 %all-to-all-start = ((bf16[4,2,128,128]{3,2,1,0:T(8,128)(2,1)}), bf16[4,2,128,128]{3,2,1,0:T(8,128)(2,1)}, u32[]{:S(2)}, u32[]{:S(2)}) async-start(bf16[4,2,128,128]{3,2,1,0:T(8,128)(2,1)} %bitcast.14), calls=%async_computation | async-start | bytes 524288 | tf_op jit(solution)/shard_map/all_to_all | solution.py:362
  15.6 13.5 %all-to-all-start.1 = ((bf16[4,2,128,128]{3,2,1,0:T(8,128)(2,1)}), bf16[4,2,128,128]{3,2,1,0:T(8,128)(2,1)S(1)}, u32[]{:S(2)}, u32[]{:S(2)}) async-start(bf16[4,2,128,128]{3,2,1,0:T(8,128)(2,1)} %all-to-all-done), calls=%async_computation.1 | async-start | bytes 524288 | tf_op jit(solution)/shard_map/all_to_all | solution.py:362
  21.0 4.7 %collective-permute-start.6 = (bf16[2,128,128]{2,1,0:T(8,128)(2,1)S(1)}, bf16[2,128,128]{2,1,0:T(8,128)(2,1)S(1)}, u32[]{:S(2)}, u32[]{:S(2)}) collective-permute-start(bf16[2,128,128]{2,1,0:T(8,128)(2,1)S(1)} %get-tuple-element.60), channel_id=1, source_target_pairs={{0,8},{8,0},{16,24},{24,16},{1,9},{9,1},{17,25},{25,17},{2,10},{10... | collective-permute-start | bytes 196616 | tf_op jit(solution)/shard_map/ppermute | solution.py:341
  22.3 4.3 %collective-permute-start.7 = (bf16[2,128,128]{2,1,0:T(8,128)(2,1)S(1)}, bf16[2,128,128]{2,1,0:T(8,128)(2,1)S(1)}, u32[]{:S(2)}, u32[]{:S(2)}) collective-permute-start(bf16[2,128,128]{2,1,0:T(8,128)(2,1)S(1)} %get-tuple-element.61), channel_id=1, source_target_pairs={{0,16},{8,24},{16,0},{24,8},{1,17},{9,25},{17,1},{25,9},{2,18},{10... | collective-permute-start | bytes 196616 | tf_op jit(solution)/shard_map/ppermute | solution.py:341
  22.9 5.2 %collective-permute-start.8 = (bf16[2,128,128]{2,1,0:T(8,128)(2,1)S(1)}, bf16[2,128,128]{2,1,0:T(8,128)(2,1)S(1)}, u32[]{:S(2)}, u32[]{:S(2)}) collective-permute-start(bf16[2,128,128]{2,1,0:T(8,128)(2,1)S(1)} %get-tuple-element.62), channel_id=1, source_target_pairs={{0,24},{8,16},{16,8},{24,0},{1,25},{9,17},{17,9},{25,1},{2,26},{10... | collective-permute-start | bytes 196616 | tf_op jit(solution)/shard_map/ppermute | solution.py:341
  29.1 23.8 %all-to-all-start.2 = ((bf16[4,2,128,128]{3,2,1,0:T(8,128)(2,1)}), bf16[4,2,128,128]{3,2,1,0:T(8,128)(2,1)S(1)}, u32[]{:S(2)}, u32[]{:S(2)}) async-start(bf16[4,2,128,128]{3,2,1,0:T(8,128)(2,1)} %join_groups.1), calls=%async_computation.2 | async-start | bytes 524288 | tf_op jit(solution)/shard_map/all_to_all | solution.py:362
  33.8 13.3 %collective-permute-start.3 = (bf16[4,2,128,128]{3,2,1,0:T(8,128)(2,1)S(1)}, bf16[4,2,128,128]{3,2,1,0:T(8,128)(2,1)S(1)}, u32[]{:S(2)}, u32[]{:S(2)}) collective-permute-start(bf16[4,2,128,128]{3,2,1,0:T(8,128)(2,1)S(1)} %all-to-all-done.1.refs_0_), channel_id=1, source_target_pairs={{0,8},{8,0},{16,24},{24,16},{1,9},{9,1},{17,25},{25,17},{2,10},{10... | collective-permute-start | bytes 786440 | tf_op jit(solution)/shard_map/ppermute | solution.py:341
  35.3 11.9 %collective-permute-start.4 = (bf16[4,2,128,128]{3,2,1,0:T(8,128)(2,1)S(1)}, bf16[4,2,128,128]{3,2,1,0:T(8,128)(2,1)S(1)}, u32[]{:S(2)}, u32[]{:S(2)}) collective-permute-start(bf16[4,2,128,128]{3,2,1,0:T(8,128)(2,1)S(1)} %all-to-all-done.1.refs_0_), channel_id=1, source_target_pairs={{0,16},{8,24},{16,0},{24,8},{1,17},{9,25},{17,1},{25,9},{2,18},{10... | collective-permute-start | bytes 786440 | tf_op jit(solution)/shard_map/ppermute | solution.py:341
  36.0 11.1 %collective-permute-start.5 = (bf16[4,2,128,128]{3,2,1,0:T(8,128)(2,1)S(1)}, bf16[4,2,128,128]{3,2,1,0:T(8,128)(2,1)S(1)}, u32[]{:S(2)}, u32[]{:S(2)}) collective-permute-start(bf16[4,2,128,128]{3,2,1,0:T(8,128)(2,1)S(1)} %all-to-all-done.1.refs_0_), channel_id=1, source_target_pairs={{0,24},{8,16},{16,8},{24,0},{1,25},{9,17},{17,9},{25,1},{2,26},{10... | collective-permute-start | bytes 786440 | tf_op jit(solution)/shard_map/ppermute | solution.py:341
  37.4 13.8 %collective-permute-start.9 = (bf16[9,128,128]{2,1,0:T(8,128)(2,1)S(1)}, bf16[9,128,128]{2,1,0:T(8,128)(2,1)S(1)}, u32[]{:S(2)}, u32[]{:S(2)}) collective-permute-start(bf16[9,128,128]{2,1,0:T(8,128)(2,1)S(1)} %broadcast_select_fusion), channel_id=1, source_target_pairs={{0,6},{2,4},{4,2},{6,0},{1,7},{3,5},{5,3},{7,1},{8,14},{10,12},{12... | collective-permute-start | bytes 884744 | tf_op jit(solution)/shard_map/ppermute | solution.py:341
  41.3 11.7 %collective-permute-start.10 = (bf16[9,128,128]{2,1,0:T(8,128)(2,1)S(1)}, bf16[9,128,128]{2,1,0:T(8,128)(2,1)S(1)}, u32[]{:S(2)}, u32[]{:S(2)}) collective-permute-start(bf16[9,128,128]{2,1,0:T(8,128)(2,1)S(1)} %collective-permute-done.2.refs_4_.refs_8_), channel_id=1, source_target_pairs={{2,0},{4,6},{3,1},{5,7},{10,8},{12,14},{11,9},{13,15},{18,16},{20,... | collective-permute-start | bytes 884744 | tf_op jit(solution)/shard_map/ppermute | solution.py:398
  53.0 29.9 %all-to-all-start.3 = ((bf16[4,8,128,128]{3,2,1,0:T(8,128)(2,1)}), bf16[4,8,128,128]{3,2,1,0:T(8,128)(2,1)S(1)}, u32[]{:S(2)}, u32[]{:S(2)}) async-start(bf16[4,8,128,128]{3,2,1,0:T(8,128)(2,1)} %level_one.1.ours), calls=%async_computation.3 | async-start | bytes 2097152 | tf_op jit(solution)/shard_map/all_to_all | solution.py:362
  56.6 9.5 %collective-permute-start.12 = (bf16[4,2,128,128]{3,2,1,0:T(8,128)(2,1)S(1)}, bf16[4,2,128,128]{3,2,1,0:T(8,128)(2,1)S(1)}, u32[]{:S(2)}, u32[]{:S(2)}) collective-permute-start(bf16[4,2,128,128]{3,2,1,0:T(8,128)(2,1)S(1)} %all-to-all-done.2.refs_0_), channel_id=1, source_target_pairs={{0,8},{8,0},{16,24},{24,16},{1,9},{9,1},{17,25},{25,17},{2,10},{10... | collective-permute-start | bytes 786440 | tf_op jit(solution)/shard_map/ppermute | solution.py:341
  57.8 12.5 %collective-permute-start.13 = (bf16[4,2,128,128]{3,2,1,0:T(8,128)(2,1)S(1)}, bf16[4,2,128,128]{3,2,1,0:T(8,128)(2,1)S(1)}, u32[]{:S(2)}, u32[]{:S(2)}) collective-permute-start(bf16[4,2,128,128]{3,2,1,0:T(8,128)(2,1)S(1)} %all-to-all-done.2.refs_0_), channel_id=1, source_target_pairs={{0,16},{8,24},{16,0},{24,8},{1,17},{9,25},{17,1},{25,9},{2,18},{10... | collective-permute-start | bytes 786440 | tf_op jit(solution)/shard_map/ppermute | solution.py:341
  58.5 13.6 %collective-permute-start.14 = (bf16[4,2,128,128]{3,2,1,0:T(8,128)(2,1)S(1)}, bf16[4,2,128,128]{3,2,1,0:T(8,128)(2,1)S(1)}, u32[]{:S(2)}, u32[]{:S(2)}) collective-permute-start(bf16[4,2,128,128]{3,2,1,0:T(8,128)(2,1)S(1)} %all-to-all-done.2.refs_0_), channel_id=1, source_target_pairs={{0,24},{8,16},{16,8},{24,0},{1,25},{9,17},{17,9},{25,1},{2,26},{10... | collective-permute-start | bytes 786440 | tf_op jit(solution)/shard_map/ppermute | solution.py:341
  78.5 7.6 %collective-permute-start.15 = (bf16[2,128,128]{2,1,0:T(8,128)(2,1)}, bf16[2,128,128]{2,1,0:T(8,128)(2,1)S(1)}, u32[]{:S(2)}, u32[]{:S(2)}) collective-permute-start(bf16[2,128,128]{2,1,0:T(8,128)(2,1)} %get-tuple-element.82), channel_id=1, source_target_pairs={{0,2},{2,0},{4,6},{6,4},{1,3},{3,1},{5,7},{7,5},{8,10},{10,8},{12,... | collective-permute-start | bytes 196616 | tf_op jit(solution)/shard_map/ppermute | solution.py:341
  80.5 7.4 %collective-permute-start.16 = (bf16[2,128,128]{2,1,0:T(8,128)(2,1)}, bf16[2,128,128]{2,1,0:T(8,128)(2,1)S(1)}, u32[]{:S(2)}, u32[]{:S(2)}) collective-permute-start(bf16[2,128,128]{2,1,0:T(8,128)(2,1)} %get-tuple-element.83), channel_id=1, source_target_pairs={{0,4},{2,6},{4,0},{6,2},{1,5},{3,7},{5,1},{7,3},{8,12},{10,14},{12... | collective-permute-start | bytes 196616 | tf_op jit(solution)/shard_map/ppermute | solution.py:341
  82.8 6.5 %collective-permute-start.17 = (bf16[2,128,128]{2,1,0:T(8,128)(2,1)S(1)}, bf16[2,128,128]{2,1,0:T(8,128)(2,1)S(1)}, u32[]{:S(2)}, u32[]{:S(2)}) collective-permute-start(bf16[2,128,128]{2,1,0:T(8,128)(2,1)S(1)} %get-tuple-element.84), channel_id=1, source_target_pairs={{0,6},{2,4},{4,2},{6,0},{1,7},{3,5},{5,3},{7,1},{8,14},{10,12},{12... | collective-permute-start | bytes 196616 | tf_op jit(solution)/shard_map/ppermute | solution.py:341
  83.8 5.5 %collective-permute-start.18 = (bf16[128,128]{1,0:T(8,128)(2,1)S(1)}, bf16[128,128]{1,0:T(8,128)(2,1)S(1)}, u32[]{:S(2)}, u32[]{:S(2)}) collective-permute-start(bf16[128,128]{1,0:T(8,128)(2,1)S(1)} %get-tuple-element.86), channel_id=1, source_target_pairs={{0,8},{8,0},{16,24},{24,16},{1,9},{9,1},{17,25},{25,17},{2,10},{10... | collective-permute-start | bytes 98312 | tf_op jit(solution)/shard_map/ppermute | solution.py:341
  84.4 4.9 %collective-permute-start.19 = (bf16[128,128]{1,0:T(8,128)(2,1)S(1)}, bf16[128,128]{1,0:T(8,128)(2,1)S(1)}, u32[]{:S(2)}, u32[]{:S(2)}) collective-permute-start(bf16[128,128]{1,0:T(8,128)(2,1)S(1)} %get-tuple-element.86), channel_id=1, source_target_pairs={{0,16},{8,24},{16,0},{24,8},{1,17},{9,25},{17,1},{25,9},{2,18},{10... | collective-permute-start | bytes 98312 | tf_op jit(solution)/shard_map/ppermute | solution.py:341
  86.1 4.8 %collective-permute-start.20 = (bf16[128,128]{1,0:T(8,128)(2,1)S(1)}, bf16[128,128]{1,0:T(8,128)(2,1)S(1)}, u32[]{:S(2)}, u32[]{:S(2)}) collective-permute-start(bf16[128,128]{1,0:T(8,128)(2,1)S(1)} %get-tuple-element.86), channel_id=1, source_target_pairs={{0,24},{8,16},{16,8},{24,0},{1,25},{9,17},{17,9},{25,1},{2,26},{10... | collective-permute-start | bytes 98312 | tf_op jit(solution)/shard_map/ppermute | solution.py:341
  87.8 27.9 %collective-permute-start.23 = (bf16[8,128,128]{2,1,0:T(8,128)(2,1)}, bf16[8,128,128]{2,1,0:T(8,128)(2,1)S(1)}, u32[]{:S(2)}, u32[]{:S(2)}) collective-permute-start(bf16[8,128,128]{2,1,0:T(8,128)(2,1)} %copy-done.12), channel_id=1, source_target_pairs={{0,4},{2,6},{4,0},{6,2},{1,5},{3,7},{5,1},{7,3},{8,12},{10,14},{12... | collective-permute-start | bytes 786440 | tf_op jit(solution)/shard_map/ppermute | solution.py:341
  91.0 8.1 %collective-permute-start.28 = (bf16[2,128,128]{2,1,0:T(8,128)(2,1)S(1)}, bf16[2,128,128]{2,1,0:T(8,128)(2,1)S(1)}, u32[]{:S(2)}, u32[]{:S(2)}) collective-permute-start(bf16[2,128,128]{2,1,0:T(8,128)(2,1)S(1)} %add_convert_fusion.refs_4_), channel_id=1, source_target_pairs={{0,8},{8,0},{16,24},{24,16},{1,9},{9,1},{17,25},{25,17},{2,10},{10... | collective-permute-start | bytes 196616 | tf_op jit(solution)/shard_map/ppermute | solution.py:341
  91.5 24.2 %collective-permute-start.21 = (bf16[8,128,128]{2,1,0:T(8,128)(2,1)}, bf16[8,128,128]{2,1,0:T(8,128)(2,1)S(1)}, u32[]{:S(2)}, u32[]{:S(2)}) collective-permute-start(bf16[8,128,128]{2,1,0:T(8,128)(2,1)} %copy-done.11), channel_id=1, source_target_pairs={{0,2},{2,0},{4,6},{6,4},{1,3},{3,1},{5,7},{7,5},{8,10},{10,8},{12,... | collective-permute-start | bytes 786440 | tf_op jit(solution)/shard_map/ppermute | solution.py:341
  92.4 23.3 %collective-permute-start.22 = (bf16[8,128,128]{2,1,0:T(8,128)(2,1)}, bf16[8,128,128]{2,1,0:T(8,128)(2,1)S(1)}, u32[]{:S(2)}, u32[]{:S(2)}) collective-permute-start(bf16[8,128,128]{2,1,0:T(8,128)(2,1)} %copy-done.10), channel_id=1, source_target_pairs={{0,6},{2,4},{4,2},{6,0},{1,7},{3,5},{5,3},{7,1},{8,14},{10,12},{12... | collective-permute-start | bytes 786440 | tf_op jit(solution)/shard_map/ppermute | solution.py:341
  99.0 5.2 %collective-permute-start.30 = (bf16[2,128,128]{2,1,0:T(8,128)(2,1)S(1)}, bf16[2,128,128]{2,1,0:T(8,128)(2,1)S(1)}, u32[]{:S(2)}, u32[]{:S(2)}) collective-permute-start(bf16[2,128,128]{2,1,0:T(8,128)(2,1)S(1)} %add_convert_fusion.refs_4_), channel_id=1, source_target_pairs={{0,24},{8,16},{16,8},{24,0},{1,25},{9,17},{17,9},{25,1},{2,26},{10... | collective-permute-start | bytes 196616 | tf_op jit(solution)/shard_map/ppermute | solution.py:341
  101.8 6.4 %collective-permute-start.25 = (bf16[128,128]{1,0:T(8,128)(2,1)S(1)}, bf16[128,128]{1,0:T(8,128)(2,1)S(1)}, u32[]{:S(2)}, u32[]{:S(2)}) collective-permute-start(bf16[128,128]{1,0:T(8,128)(2,1)S(1)} %get-tuple-element.94), channel_id=1, source_target_pairs={{0,2},{2,0},{4,6},{6,4},{1,3},{3,1},{5,7},{7,5},{8,10},{10,8},{12,... | collective-permute-start | bytes 98312 | tf_op jit(solution)/shard_map/ppermute | solution.py:341
  104.2 10.1 %collective-permute-start.26 = (bf16[128,128]{1,0:T(8,128)(2,1)S(1)}, bf16[128,128]{1,0:T(8,128)(2,1)S(1)}, u32[]{:S(2)}, u32[]{:S(2)}) collective-permute-start(bf16[128,128]{1,0:T(8,128)(2,1)S(1)} %get-tuple-element.95), channel_id=1, source_target_pairs={{0,4},{2,6},{4,0},{6,2},{1,5},{3,7},{5,1},{7,3},{8,12},{10,14},{12... | collective-permute-start | bytes 98312 | tf_op jit(solution)/shard_map/ppermute | solution.py:341
  108.1 6.1 %collective-permute-start.27 = (bf16[128,128]{1,0:T(8,128)(2,1)S(1)}, bf16[128,128]{1,0:T(8,128)(2,1)S(1)}, u32[]{:S(2)}, u32[]{:S(2)}) collective-permute-start(bf16[128,128]{1,0:T(8,128)(2,1)S(1)} %get-tuple-element.96), channel_id=1, source_target_pairs={{0,6},{2,4},{4,2},{6,0},{1,7},{3,5},{5,3},{7,1},{8,14},{10,12},{12... | collective-permute-start | bytes 98312 | tf_op jit(solution)/shard_map/ppermute | solution.py:341
  (16 other events, 185.9 us)
